TPU v7x, 128 devices: a whole 4x4x4 slice. The times are simulated.
128 devices in a mesh: bx: 16 (over x, z), by: 8 (over y, core).
Axes of the slice: x: 4, y: 4, z: 4, core: 2. Of those that a mesh axis runs over, the one named last changes fastest.
Arguments:
- tokens: bfloat16 [16, 8, 1024, 512], P('bx', 'by'), may hold values from -6 to 6
- norm_gain: float32 [512], replicated, may hold values from 0.1 to 1.9
- w_query_key: bfloat16 [512, 1024], replicated
- w_value: bfloat16 [512, 512], replicated, may hold values from -1 to 1
- w_out: bfloat16 [512, 512], replicated, may hold values from -0.25 to 0.25
- cotangent: bfloat16 [16, 8, 1024, 512], P('bx', 'by'), may hold values from -6 to 6
- block_order: int32 [16, 8, 1024], P('bx', 'by'), may hold values from 0 to 1023, each once within a row
- neighbour_ids: int32 [16, 8, 4, 4], replicated, may hold values from 0 to 511, as said below
- neighbour_count: int32 [16, 8, 4], replicated, may hold values from 1 to 4
Outputs:
- branch_out: bfloat16 [16, 8, 1024, 512], P('bx', 'by')
- grad_tokens: float32 [16, 8, 1024, 512], P('bx', 'by')
- grad_w_query_key: float32 [512, 1024], replicated
- grad_w_value: float32 [512, 512], replicated
- grad_w_out: float32 [512, 512], replicated
- grad_norm_gain: float32 [512], replicated
Inputs may be any that keep to these rules, and one draw needn't show every extreme that they name: `neighbour_ids`: block ids are (x * 8 + y) * 4 + b. Entry j < neighbour_count of query block b on brick (x, y) names a block other than b itself, either another block of brick (x, y) or a block of a brick one step away along exactly one axis (x - 1, x + 1, y - 1 or y + 1); the live entries of one list differ. Entries from neighbour_count on hold the query block's own id. Over all query blocks of one brick, at most 2 distinct blocks of any one other brick are named, and every brick names exactly 2 blocks of some other brick. `block_order`: on every brick, a permutation of the arrival rows.
All inputs are finite; a program needn't handle non-finite values.
Results may differ from a plain program's by a relative error of at most 0.006.
The roundings to bfloat16 on the way count: a program that leaves them out, or rounds other values in their place, can miss the bound.
Values may be sent and summed in bfloat16 or wider, within the bound.
No kernel may reach another device: no remote copies, remote signals or barrier semaphores. Data moves between devices by JAX's collectives and lax.ppermute only.
A program may use at most 256 MiB of HBM per device.

v0:
```python
import math

import jax
import jax.numpy as jnp
from jax import lax
from jax.sharding import PartitionSpec as P

HEADS = 8
BLK = 256


EPSILON = 1e-06


def from_behind(block, axis, distance):
    devices = range(lax.axis_size(axis))
    route = [(i - distance, i) for i in devices if i - distance in devices]
    return lax.ppermute(block, axis, route)


def rms_rows(token_rows, gain_row):
    values = token_rows.astype(jnp.float32)
    inv_rms = lax.rsqrt(jnp.mean(values * values, axis=-1, keepdims=True) + EPSILON)
    return (values, inv_rms, (values * inv_rms * gain_row).astype(jnp.bfloat16))


def attend_block(query_rows, key_value_rows, live_cols, grad_context):
    features = query_rows.shape[-1]
    head_size = features // HEADS
    row_count = query_rows.shape[0]
    factor = 1.0 / math.sqrt(head_size)
    queries = query_rows.reshape(row_count, HEADS, head_size)
    kv_rows = key_value_rows.reshape(-1, 2 * features)
    key_rows = kv_rows[:, :features].reshape(-1, HEADS, head_size)
    value_rows = kv_rows[:, features:].reshape(-1, HEADS, head_size)
    grad_rows = grad_context.reshape(row_count, HEADS, head_size)
    scores = (
        jnp.einsum("ihd,jhd->hij", queries, key_rows, preferred_element_type=jnp.float32) * factor
    )
    scores = jnp.where(live_cols[None, None, :], scores, -1e30)
    row_max = jnp.max(scores, axis=-1, keepdims=True)
    powers = jnp.exp(scores - row_max)
    attn_probs = powers / jnp.sum(powers, axis=-1, keepdims=True)
    probs_low = attn_probs.astype(jnp.bfloat16)
    context = jnp.einsum(
        "hij,jhd->ihd", probs_low, value_rows, preferred_element_type=jnp.float32
    ).astype(jnp.bfloat16)
    grad_probs = jnp.einsum(
        "ihd,jhd->hij", grad_rows, value_rows, preferred_element_type=jnp.float32
    )
    centre = jnp.sum(attn_probs * grad_probs, axis=-1, keepdims=True)
    grad_scores = (attn_probs * (grad_probs - centre) * factor).astype(jnp.bfloat16)
    grad_query = jnp.einsum(
        "hij,jhd->ihd", grad_scores, key_rows, preferred_element_type=jnp.float32
    ).astype(jnp.bfloat16)
    grad_keys = jnp.einsum("hij,ihd->jhd", grad_scores, queries, preferred_element_type=jnp.float32)
    grad_values = jnp.einsum(
        "hij,ihd->jhd", probs_low, grad_rows, preferred_element_type=jnp.float32
    )
    slots = key_value_rows.shape[0]
    return (
        context.reshape(row_count, features),
        grad_query.reshape(row_count, features),
        grad_keys.reshape(slots, row_count, features),
        grad_values.reshape(slots, row_count, features),
    )


def shards(
    tokens,
    norm_gain,
    w_query_key,
    w_value,
    w_out,
    cotangent,
    block_order,
    neighbour_ids,
    neighbour_count,
):
    row_count = tokens.shape[2]
    features = tokens.shape[3]
    blocks = row_count // BLK
    slot_count = neighbour_ids.shape[3]
    extent_y = lax.axis_size("by")
    brick_x = lax.axis_index("bx")
    brick_y = lax.axis_index("by")
    row_order = block_order[0, 0]
    sorted_rows = tokens[0, 0][row_order]
    sorted_grad = cotangent[0, 0][row_order]
    values, inv_rms, normed = rms_rows(sorted_rows, norm_gain)
    query_rows = jnp.dot(
        normed, w_query_key[:, :features], preferred_element_type=jnp.float32
    ).astype(jnp.bfloat16)
    w_pair = jnp.concatenate([w_query_key[:, features:], w_value], axis=1)
    key_value = jnp.dot(normed, w_pair, preferred_element_type=jnp.float32).astype(jnp.bfloat16)
    key_value = key_value.reshape(blocks, BLK, 2 * features)
    d_context = lax.dot_general(
        sorted_grad, w_out, (((1,), (1,)), ((), ())), preferred_element_type=jnp.float32
    ).astype(jnp.bfloat16)
    slot_range = jnp.arange(slot_count, dtype=jnp.int32)
    block_range = jnp.arange(blocks, dtype=jnp.int32)
    my_ids = neighbour_ids[brick_x, brick_y]
    my_count = neighbour_count[brick_x, brick_y]
    live_slots = slot_range[None, :] < my_count[:, None]
    owner_brick = my_ids // blocks
    offset = my_ids % blocks
    delta_x = owner_brick // extent_y - brick_x
    delta_y = owner_brick % extent_y - brick_y
    segment = jnp.where(
        delta_x == -1,
        1,
        jnp.where(delta_x == 1, 2, jnp.where(delta_y == -1, 3, jnp.where(delta_y == 1, 4, 0))),
    )
    entry_index = segment * blocks + offset

    def incoming(returned):
        return returned.astype(jnp.float32)

    fetched = {}
    for shift_step in (1, -1):
        fetched["bx", shift_step] = from_behind(key_value, "bx", shift_step)
    for shift_step in (1, -1):
        fetched["by", shift_step] = from_behind(key_value, "by", shift_step)
    key_pool = jnp.concatenate(
        [key_value, fetched["bx", 1], fetched["bx", -1], fetched["by", 1], fetched["by", -1]],
        axis=0,
    )
    key_index = jnp.concatenate([block_range[:, None], entry_index], axis=1)
    live_keys = jnp.concatenate([jnp.ones((blocks, 1), dtype=jnp.bool_), live_slots], axis=1)
    pool_rows = key_pool.shape[0]

    def per_block(totals, block_item):
        block_query, block_grad, key_ids, live_here = block_item
        live_cols = jnp.repeat(live_here, BLK)
        context, grad_query, key_terms, value_terms = attend_block(
            block_query, key_pool[key_ids], live_cols, block_grad
        )
        key_total = totals[0].at[key_ids].add(key_terms)
        value_total = totals[1].at[key_ids].add(value_terms)
        return ((key_total, value_total), (context, grad_query))

    empty_total = jnp.zeros((pool_rows, BLK, features), jnp.float32)
    (key_total, value_total), (context, grad_query) = lax.scan(
        per_block,
        (empty_total, empty_total),
        (
            query_rows.reshape(blocks, BLK, features),
            d_context.reshape(blocks, BLK, features),
            key_index,
            live_keys,
        ),
    )
    seg_rows = (pool_rows - blocks) // 4

    def segment_rows(index):
        lower = blocks + index * seg_rows
        upper = lower + seg_rows
        return jnp.concatenate([key_total[lower:upper], value_total[lower:upper]], axis=-1).astype(
            jnp.bfloat16
        )

    own_grad = jnp.concatenate([key_total[:blocks], value_total[:blocks]], axis=-1)
    for shift_step, index in ((1, 0), (-1, 1)):
        returned = from_behind(segment_rows(index), "bx", -shift_step)
        own_grad = own_grad + incoming(returned)
    for shift_step, index in ((1, 2), (-1, 3)):
        returned = from_behind(segment_rows(index), "by", -shift_step)
        own_grad = own_grad + incoming(returned)
    grad_kv = own_grad.astype(jnp.bfloat16).reshape(row_count, 2 * features)
    context = context.reshape(row_count, features)
    grad_query = grad_query.reshape(row_count, features)
    out_rows = jnp.dot(context, w_out, preferred_element_type=jnp.float32).astype(jnp.bfloat16)
    grad_out_part = lax.dot_general(
        context, sorted_grad, (((0,), (0,)), ((), ())), preferred_element_type=jnp.float32
    )
    grad_proj = jnp.concatenate([grad_query, grad_kv], axis=1)
    w_all = jnp.concatenate([w_query_key, w_value], axis=1)
    grad_normed = lax.dot_general(
        grad_proj, w_all, (((1,), (1,)), ((), ())), preferred_element_type=jnp.float32
    )
    grad_all_part = lax.dot_general(
        normed, grad_proj, (((0,), (0,)), ((), ())), preferred_element_type=jnp.float32
    )
    gain_part = jnp.sum(grad_normed * (values * inv_rms), axis=0)
    scaled_grad = grad_normed * norm_gain
    grad_rows = inv_rms * scaled_grad - values * (inv_rms * inv_rms * inv_rms) * jnp.mean(
        values * scaled_grad, axis=-1, keepdims=True
    )
    grad_qk, grad_val, grad_output, grad_gain = lax.psum(
        (
            grad_all_part[:, : 2 * features],
            grad_all_part[:, 2 * features :],
            grad_out_part,
            gain_part,
        ),
        ("bx", "by"),
    )
    inverse = (
        jnp.zeros((row_count,), jnp.int32).at[row_order].set(jnp.arange(row_count, dtype=jnp.int32))
    )
    branch_out = out_rows[inverse][None, None]
    grad_tokens = grad_rows[inverse][None, None]
    return (branch_out, grad_tokens, grad_qk, grad_val, grad_output, grad_gain)


def solution(mesh):
    placed = (
        P("bx", "by", None, None),
        P(),
        P(),
        P(),
        P(),
        P("bx", "by", None, None),
        P("bx", "by", None),
        P(),
        P(),
    )
    return jax.shard_map(
        shards,
        mesh=mesh,
        in_specs=placed,
        out_specs=(P("bx", "by", None, None), P("bx", "by", None, None), P(), P(), P(), P()),
        check_vma=False,
    )
```

profile of v0, /device:TPU:1, one launch (start us, length us, event | category | flops | bytes accessed | tf_op | source)
XLA Modules:
  0.0 827.2 jit_solution(16518932368567936794)
XLA Ops:
  43.2 22.0 %collective-permute-done = bf16[4,256,1024]{2,1,0:T(8,128)(2,1)} collective-permute-done((bf16[4,256,1024]{2,1,0:T(8,128)(2,1)}, bf16[4,256,1024]{2,1,0:T(8,128)(2,1)}, u32[]{:S(2)}, u32[]{:S(2)}) %collective-permute-start) | collective-permute-done | bytes 2097184 | tf_op jit(solution)/shard_map/ppermute | solution.py:18
  90.0 485.8 %while.16 = (s32[]{:T(128)}, f32[20,256,512]{2,1,0:T(8,128)}, f32[20,256,512]{2,1,0:T(8,128)}, bf16[4,256,512]{2,1,0:T(8,128)(2,1)}, bf16[4,256,512]{2,1,0:T(8,1...) while((s32[]{:T(128)}, f32[20,256,512]{2,1,0:T(8,128)}, ...), condition=%wide.region_7.8_spmd, body=%wide.region_1.7_spmd.sunk | while | flops 2759343360 | bytes 153670032 | solution.py:143
  103.8 8.4 %fusion.138 = (f32[8,256]{1,0:T(8,128)S(1)}, f32[8,256,1280]{2,1,0:T(8,128)}) fusion(pred[1280]{0:T(1024)(128)(4,1)S(1)} %broadcast_in_dim.109, bf16[256,8,64]{0,2,1:T(8,128)(2,1)S(1)} %bitcast.119, bf16[1280,8,64]{0,2,1:T(8,128)(2,1)} %bitcast.113), kind=kOutput, calls=%fused_computation.120.clone.1 | convolution fusion | flops 346031360 | bytes 12068096 | tf_op jit(solution)/shard_map/while/body/eval_jaxpr/sub | solution.py:42
  120.7 19.1 %fusion.140 = bf16[8,64,256]{2,1,0:T(8,128)(2,1)S(1)} fusion(bf16[1280,8,64]{0,2,1:T(8,128)(2,1)} %bitcast.114, f32[8,256,1280]{2,1,0:T(8,128)} %fusion.137, f32[8,256,1280]{2,1,0:T(8,128)} %get-tuple-element.200, f32[8,256]{1,0:T(8,128)S(1)} %get-tuple-element.201), kind=kOutput, calls=%fused_computation.29.clone.1 | convolution fusion | flops 354028800 | bytes 22552576 | tf_op jit(solution)/shard_map/while/body/eval_jaxpr/hij,jhd->ihd/dot_general | solution.py:53
  145.7 25.9 %fusion.139 = f32[1280,8,64]{0,2,1:T(8,128)} fusion(bf16[256,8,64]{0,2,1:T(8,128)(2,1)S(1)} %bitcast.121, f32[8,256,1280]{2,1,0:T(8,128)} %fusion.137, f32[8,256,1280]{2,1,0:T(8,128)} %get-tuple-element.200, f32[8,256]{1,0:T(8,128)S(1)} %get-tuple-element.201), kind=kOutput, calls=%fused_computation.23.clone.1 | convolution fusion | flops 353897728 | bytes 23863296 | tf_op jit(solution)/shard_map/while/body/eval_jaxpr/hij,ihd->jhd/dot_general | solution.py:56
  180.9 8.3 %scatter_fusion = f32[20,256,512]{2,1,0:T(8,128)} fusion(f32[20,256,512]{2,1,0:T(8,128)} %get-tuple-element.216, s32[5]{0:T(128)S(1)} %fusion.135, f32[5,256,512]{2,1,0:T(8,128)} %copy.49), kind=kCustom, calls=%fused_computation.5.clone.1 | custom fusion | flops 655360 | bytes 7864340 | tf_op jit(solution)/shard_map/while/body/eval_jaxpr/scatter-add | solution.py:138
  203.5 8.4 %scatter_fusion.1 = f32[20,256,512]{2,1,0:T(8,128)} fusion(f32[20,256,512]{2,1,0:T(8,128)} %get-tuple-element.217, s32[5]{0:T(128)S(1)} %fusion.135, f32[5,256,512]{2,1,0:T(8,128)} %copy.50), kind=kCustom, calls=%fused_computation.6.clone.1 | custom fusion | flops 655360 | bytes 7864340 | tf_op jit(solution)/shard_map/while/body/eval_jaxpr/scatter-add | solution.py:139
  225.2 8.4 %fusion.138 = (f32[8,256]{1,0:T(8,128)S(1)}, f32[8,256,1280]{2,1,0:T(8,128)}) fusion(pred[1280]{0:T(1024)(128)(4,1)S(1)} %broadcast_in_dim.109, bf16[256,8,64]{0,2,1:T(8,128)(2,1)S(1)} %bitcast.119, bf16[1280,8,64]{0,2,1:T(8,128)(2,1)} %bitcast.113), kind=kOutput, calls=%fused_computation.120.clone.1 | convolution fusion | flops 346031360 | bytes 12068096 | tf_op jit(solution)/shard_map/while/body/eval_jaxpr/sub | solution.py:42
  242.1 19.1 %fusion.140 = bf16[8,64,256]{2,1,0:T(8,128)(2,1)S(1)} fusion(bf16[1280,8,64]{0,2,1:T(8,128)(2,1)} %bitcast.114, f32[8,256,1280]{2,1,0:T(8,128)} %fusion.137, f32[8,256,1280]{2,1,0:T(8,128)} %get-tuple-element.200, f32[8,256]{1,0:T(8,128)S(1)} %get-tuple-element.201), kind=kOutput, calls=%fused_computation.29.clone.1 | convolution fusion | flops 354028800 | bytes 22552576 | tf_op jit(solution)/shard_map/while/body/eval_jaxpr/hij,jhd->ihd/dot_general | solution.py:53
  267.2 25.9 %fusion.139 = f32[1280,8,64]{0,2,1:T(8,128)} fusion(bf16[256,8,64]{0,2,1:T(8,128)(2,1)S(1)} %bitcast.121, f32[8,256,1280]{2,1,0:T(8,128)} %fusion.137, f32[8,256,1280]{2,1,0:T(8,128)} %get-tuple-element.200, f32[8,256]{1,0:T(8,128)S(1)} %get-tuple-element.201), kind=kOutput, calls=%fused_computation.23.clone.1 | convolution fusion | flops 353897728 | bytes 23863296 | tf_op jit(solution)/shard_map/while/body/eval_jaxpr/hij,ihd->jhd/dot_general | solution.py:56
  302.3 8.3 %scatter_fusion = f32[20,256,512]{2,1,0:T(8,128)} fusion(f32[20,256,512]{2,1,0:T(8,128)} %get-tuple-element.216, s32[5]{0:T(128)S(1)} %fusion.135, f32[5,256,512]{2,1,0:T(8,128)} %copy.49), kind=kCustom, calls=%fused_computation.5.clone.1 | custom fusion | flops 655360 | bytes 7864340 | tf_op jit(solution)/shard_map/while/body/eval_jaxpr/scatter-add | solution.py:138
  324.9 8.5 %scatter_fusion.1 = f32[20,256,512]{2,1,0:T(8,128)} fusion(f32[20,256,512]{2,1,0:T(8,128)} %get-tuple-element.217, s32[5]{0:T(128)S(1)} %fusion.135, f32[5,256,512]{2,1,0:T(8,128)} %copy.50), kind=kCustom, calls=%fused_computation.6.clone.1 | custom fusion | flops 655360 | bytes 7864340 | tf_op jit(solution)/shard_map/while/body/eval_jaxpr/scatter-add | solution.py:139
  346.8 8.4 %fusion.138 = (f32[8,256]{1,0:T(8,128)S(1)}, f32[8,256,1280]{2,1,0:T(8,128)}) fusion(pred[1280]{0:T(1024)(128)(4,1)S(1)} %broadcast_in_dim.109, bf16[256,8,64]{0,2,1:T(8,128)(2,1)S(1)} %bitcast.119, bf16[1280,8,64]{0,2,1:T(8,128)(2,1)} %bitcast.113), kind=kOutput, calls=%fused_computation.120.clone.1 | convolution fusion | flops 346031360 | bytes 12068096 | tf_op jit(solution)/shard_map/while/body/eval_jaxpr/sub | solution.py:42
  363.6 19.1 %fusion.140 = bf16[8,64,256]{2,1,0:T(8,128)(2,1)S(1)} fusion(bf16[1280,8,64]{0,2,1:T(8,128)(2,1)} %bitcast.114, f32[8,256,1280]{2,1,0:T(8,128)} %fusion.137, f32[8,256,1280]{2,1,0:T(8,128)} %get-tuple-element.200, f32[8,256]{1,0:T(8,128)S(1)} %get-tuple-element.201), kind=kOutput, calls=%fused_computation.29.clone.1 | convolution fusion | flops 354028800 | bytes 22552576 | tf_op jit(solution)/shard_map/while/body/eval_jaxpr/hij,jhd->ihd/dot_general | solution.py:53
  388.7 25.9 %fusion.139 = f32[1280,8,64]{0,2,1:T(8,128)} fusion(bf16[256,8,64]{0,2,1:T(8,128)(2,1)S(1)} %bitcast.121, f32[8,256,1280]{2,1,0:T(8,128)} %fusion.137, f32[8,256,1280]{2,1,0:T(8,128)} %get-tuple-element.200, f32[8,256]{1,0:T(8,128)S(1)} %get-tuple-element.201), kind=kOutput, calls=%fused_computation.23.clone.1 | convolution fusion | flops 353897728 | bytes 23863296 | tf_op jit(solution)/shard_map/while/body/eval_jaxpr/hij,ihd->jhd/dot_general | solution.py:56
  423.8 8.4 %scatter_fusion = f32[20,256,512]{2,1,0:T(8,128)} fusion(f32[20,256,512]{2,1,0:T(8,128)} %get-tuple-element.216, s32[5]{0:T(128)S(1)} %fusion.135, f32[5,256,512]{2,1,0:T(8,128)} %copy.49), kind=kCustom, calls=%fused_computation.5.clone.1 | custom fusion | flops 655360 | bytes 7864340 | tf_op jit(solution)/shard_map/while/body/eval_jaxpr/scatter-add | solution.py:138
  446.5 8.4 %scatter_fusion.1 = f32[20,256,512]{2,1,0:T(8,128)} fusion(f32[20,256,512]{2,1,0:T(8,128)} %get-tuple-element.217, s32[5]{0:T(128)S(1)} %fusion.135, f32[5,256,512]{2,1,0:T(8,128)} %copy.50), kind=kCustom, calls=%fused_computation.6.clone.1 | custom fusion | flops 655360 | bytes 7864340 | tf_op jit(solution)/shard_map/while/body/eval_jaxpr/scatter-add | solution.py:139
  468.2 8.4 %fusion.138 = (f32[8,256]{1,0:T(8,128)S(1)}, f32[8,256,1280]{2,1,0:T(8,128)}) fusion(pred[1280]{0:T(1024)(128)(4,1)S(1)} %broadcast_in_dim.109, bf16[256,8,64]{0,2,1:T(8,128)(2,1)S(1)} %bitcast.119, bf16[1280,8,64]{0,2,1:T(8,128)(2,1)} %bitcast.113), kind=kOutput, calls=%fused_computation.120.clone.1 | convolution fusion | flops 346031360 | bytes 12068096 | tf_op jit(solution)/shard_map/while/body/eval_jaxpr/sub | solution.py:42
  485.1 19.1 %fusion.140 = bf16[8,64,256]{2,1,0:T(8,128)(2,1)S(1)} fusion(bf16[1280,8,64]{0,2,1:T(8,128)(2,1)} %bitcast.114, f32[8,256,1280]{2,1,0:T(8,128)} %fusion.137, f32[8,256,1280]{2,1,0:T(8,128)} %get-tuple-element.200, f32[8,256]{1,0:T(8,128)S(1)} %get-tuple-element.201), kind=kOutput, calls=%fused_computation.29.clone.1 | convolution fusion | flops 354028800 | bytes 22552576 | tf_op jit(solution)/shard_map/while/body/eval_jaxpr/hij,jhd->ihd/dot_general | solution.py:53
  510.1 25.9 %fusion.139 = f32[1280,8,64]{0,2,1:T(8,128)} fusion(bf16[256,8,64]{0,2,1:T(8,128)(2,1)S(1)} %bitcast.121, f32[8,256,1280]{2,1,0:T(8,128)} %fusion.137, f32[8,256,1280]{2,1,0:T(8,128)} %get-tuple-element.200, f32[8,256]{1,0:T(8,128)S(1)} %get-tuple-element.201), kind=kOutput, calls=%fused_computation.23.clone.1 | convolution fusion | flops 353897728 | bytes 23863296 | tf_op jit(solution)/shard_map/while/body/eval_jaxpr/hij,ihd->jhd/dot_general | solution.py:56
  567.6 8.1 scatter_fusion.1
  612.5 27.0 %collective-permute-done.4 = bf16[4,256,1024]{2,1,0:T(8,128)(2,1)} collective-permute-done((bf16[4,256,1024]{2,1,0:T(8,128)(2,1)S(1)}, bf16[4,256,1024]{2,1,0:T(8,128)(2,1)}, u32[]{:S(2)}, u32[]{:S(2)}) %collective-permute-start.4) | collective-permute-done | bytes 2097184 | tf_op jit(solution)/shard_map/ppermute | solution.py:18
  673.4 73.5 %psum.31 = f32[512]{0:T(512)} all-reduce(f32[512]{0:T(512)S(1)} %get-tuple-element.85), channel_id=1, replica_groups=mesh['bx'=16,'by'=8] {'bx','by'}, use_global_device_ids=true, to_apply=%region_14.15 | all-reduce | flops 512 | bytes 4096 | tf_op jit(solution)/shard_map/psum | solution.py:189
  746.9 68.0 %all-reduce.4.cloned.1.call-done = (f32[512,1024]{1,0:T(8,128)}, f32[512,512]{1,0:T(8,128)}, f32[512,512]{1,0:T(8,128)}) async-done(((f32[512,1024]{1,0:T(8,128)}, f32[512,512]{1,0:T(8,128)}, f32[512,512]{1,0:T(8,128)}), (f32[512,1024]{1,0:T(8,128)}, f32[512,512]{1,0:T(8,128)}, f32[512,512]{1,0:T(8,128)})) %all-reduce.4.cloned.1.call-update) | async-done | bytes 4194320 | tf_op jit(solution)/shard_map/psum | solution.py:189
  (242 shorter events, 349.2 us)
Async XLA Ops:
  7.2 807.7 %all-reduce.4.cloned.1.call-start = ((), (), s32[]{:S(2)}) async-start(), calls=%async_computation | async-start | bytes 8388608 | tf_op jit(solution)/shard_map/psum | solution.py:189
  12.6 28.8 %copy-start.6 = (bf16[1024,512]{1,0:T(8,128)(2,1)}, bf16[1024,512]{1,0:T(8,128)(2,1)S(1)}, u32[]{:S(2)}) copy-start(bf16[1024,512]{1,0:T(8,128)(2,1)S(1)} %gather_fusion.1) | copy-start | bytes 3145732
  13.5 27.9 %copy-start.21 = (f32[1024]{0:T(1024)}, f32[1024]{0:T(1024)S(1)}, u32[]{:S(2)}) copy-start(f32[1024]{0:T(1024)S(1)} %get-tuple-element.125) | copy-start | bytes 12292
  13.5 15.7 %copy-start.4 = (bf16[1,1,1024,512]{3,2,1,0:T(8,128)(2,1)S(1)}, bf16[1,1,1024,512]{3,2,1,0:T(8,128)(2,1)}, u32[]{:S(2)}) copy-start(bf16[1,1,1024,512]{3,2,1,0:T(8,128)(2,1)} %param.16) | copy-start | bytes 3145732
  16.2 49.0 %collective-permute-start = (bf16[4,256,1024]{2,1,0:T(8,128)(2,1)}, bf16[4,256,1024]{2,1,0:T(8,128)(2,1)}, u32[]{:S(2)}, u32[]{:S(2)}) collective-permute-start(bf16[4,256,1024]{2,1,0:T(8,128)(2,1)} %bitcast.18), channel_id=1, source_target_pairs={{0,8},{8,16},{16,24},{24,32},{32,40},{40,48},{48,56},{56,64},{64,7... | collective-permute-start | bytes 6291464 | tf_op jit(solution)/shard_map/ppermute | solution.py:18
  21.9 48.4 %collective-permute-start.1 = (bf16[4,256,1024]{2,1,0:T(8,128)(2,1)}, bf16[4,256,1024]{2,1,0:T(8,128)(2,1)}, u32[]{:S(2)}, u32[]{:S(2)}) collective-permute-start(bf16[4,256,1024]{2,1,0:T(8,128)(2,1)} %bitcast.18), channel_id=1, source_target_pairs={{8,0},{16,8},{24,16},{32,24},{40,32},{48,40},{56,48},{64,56},{72,6... | collective-permute-start | bytes 6291464 | tf_op jit(solution)/shard_map/ppermute | solution.py:18
  23.2 50.2 %collective-permute-start.2 = (bf16[4,256,1024]{2,1,0:T(8,128)(2,1)}, bf16[4,256,1024]{2,1,0:T(8,128)(2,1)}, u32[]{:S(2)}, u32[]{:S(2)}) collective-permute-start(bf16[4,256,1024]{2,1,0:T(8,128)(2,1)} %bitcast.18), channel_id=1, source_target_pairs={{0,1},{1,2},{2,3},{3,4},{4,5},{5,6},{6,7},{8,9},{9,10},{10,11},{11... | collective-permute-start | bytes 6291464 | tf_op jit(solution)/shard_map/ppermute | solution.py:18
  27.2 49.2 %collective-permute-start.3 = (bf16[4,256,1024]{2,1,0:T(8,128)(2,1)}, bf16[4,256,1024]{2,1,0:T(8,128)(2,1)}, u32[]{:S(2)}, u32[]{:S(2)}) collective-permute-start(bf16[4,256,1024]{2,1,0:T(8,128)(2,1)} %bitcast.18), channel_id=1, source_target_pairs={{1,0},{2,1},{3,2},{4,3},{5,4},{6,5},{7,6},{9,8},{10,9},{11,10},{12... | collective-permute-start | bytes 6291464 | tf_op jit(solution)/shard_map/ppermute | solution.py:18
  90.5 23.2 %copy-start.11 = (bf16[4,256,512]{2,1,0:T(8,128)(2,1)}, bf16[4,256,512]{2,1,0:T(8,128)(2,1)S(1)}, u32[]{:S(2)}) copy-start(bf16[4,256,512]{2,1,0:T(8,128)(2,1)S(1)} %get-tuple-element.235) | copy-start | bytes 3145732 | tf_op jit(solution)/shard_map/while
  120.7 19.2 %copy-start.2 = (bf16[1280,512]{0,1:T(8,128)(2,1)S(1)}, bf16[1280,512]{0,1:T(8,128)(2,1)}, u32[]{:S(2)}) copy-start(bf16[1280,512]{0,1:T(8,128)(2,1)} %copy.47) | copy-start | bytes 3932164 | tf_op jit(solution)/shard_map/while
  211.9 23.2 %copy-start.11 = (bf16[4,256,512]{2,1,0:T(8,128)(2,1)}, bf16[4,256,512]{2,1,0:T(8,128)(2,1)S(1)}, u32[]{:S(2)}) copy-start(bf16[4,256,512]{2,1,0:T(8,128)(2,1)S(1)} %get-tuple-element.235) | copy-start | bytes 3145732 | tf_op jit(solution)/shard_map/while
  242.1 19.2 %copy-start.2 = (bf16[1280,512]{0,1:T(8,128)(2,1)S(1)}, bf16[1280,512]{0,1:T(8,128)(2,1)}, u32[]{:S(2)}) copy-start(bf16[1280,512]{0,1:T(8,128)(2,1)} %copy.47) | copy-start | bytes 3932164 | tf_op jit(solution)/shard_map/while
  333.4 23.2 %copy-start.11 = (bf16[4,256,512]{2,1,0:T(8,128)(2,1)}, bf16[4,256,512]{2,1,0:T(8,128)(2,1)S(1)}, u32[]{:S(2)}) copy-start(bf16[4,256,512]{2,1,0:T(8,128)(2,1)S(1)} %get-tuple-element.235) | copy-start | bytes 3145732 | tf_op jit(solution)/shard_map/while
  363.6 19.2 %copy-start.2 = (bf16[1280,512]{0,1:T(8,128)(2,1)S(1)}, bf16[1280,512]{0,1:T(8,128)(2,1)}, u32[]{:S(2)}) copy-start(bf16[1280,512]{0,1:T(8,128)(2,1)} %copy.47) | copy-start | bytes 3932164 | tf_op jit(solution)/shard_map/while
  454.9 23.2 %copy-start.11 = (bf16[4,256,512]{2,1,0:T(8,128)(2,1)}, bf16[4,256,512]{2,1,0:T(8,128)(2,1)S(1)}, u32[]{:S(2)}) copy-start(bf16[4,256,512]{2,1,0:T(8,128)(2,1)S(1)} %get-tuple-element.235) | copy-start | bytes 3145732 | tf_op jit(solution)/shard_map/while
  485.1 19.2 %copy-start.2 = (bf16[1280,512]{0,1:T(8,128)(2,1)S(1)}, bf16[1280,512]{0,1:T(8,128)(2,1)}, u32[]{:S(2)}) copy-start(bf16[1280,512]{0,1:T(8,128)(2,1)} %copy.47) | copy-start | bytes 3932164 | tf_op jit(solution)/shard_map/while
  592.0 47.5 %collective-permute-start.4 = (bf16[4,256,1024]{2,1,0:T(8,128)(2,1)S(1)}, bf16[4,256,1024]{2,1,0:T(8,128)(2,1)}, u32[]{:S(2)}, u32[]{:S(2)}) collective-permute-start(bf16[4,256,1024]{2,1,0:T(8,128)(2,1)S(1)} %pad_maximum_fusion.1), channel_id=1, source_target_pairs={{8,0},{16,8},{24,16},{32,24},{40,32},{48,40},{56,48},{64,56},{72,6... | collective-permute-start | bytes 6291464 | tf_op jit(solution)/shard_map/ppermute | solution.py:18
  593.6 47.0 %collective-permute-start.5 = (bf16[4,256,1024]{2,1,0:T(8,128)(2,1)S(1)}, bf16[4,256,1024]{2,1,0:T(8,128)(2,1)}, u32[]{:S(2)}, u32[]{:S(2)}) collective-permute-start(bf16[4,256,1024]{2,1,0:T(8,128)(2,1)S(1)} %pad_maximum_fusion.2), channel_id=1, source_target_pairs={{0,8},{8,16},{16,24},{24,32},{32,40},{40,48},{48,56},{56,64},{64,7... | collective-permute-start | bytes 6291464 | tf_op jit(solution)/shard_map/ppermute | solution.py:18
  599.2 41.4 %collective-permute-start.6 = (bf16[4,256,1024]{2,1,0:T(8,128)(2,1)S(1)}, bf16[4,256,1024]{2,1,0:T(8,128)(2,1)S(1)}, u32[]{:S(2)}, u32[]{:S(2)}) collective-permute-start(bf16[4,256,1024]{2,1,0:T(8,128)(2,1)S(1)} %pad_maximum_fusion.3), channel_id=1, source_target_pairs={{1,0},{2,1},{3,2},{4,3},{5,4},{6,5},{7,6},{9,8},{10,9},{11,10},{12... | collective-permute-start | bytes 6291464 | tf_op jit(solution)/shard_map/ppermute | solution.py:18
  603.6 38.3 %collective-permute-start.7 = (bf16[4,256,1024]{2,1,0:T(8,128)(2,1)S(1)}, bf16[4,256,1024]{2,1,0:T(8,128)(2,1)}, u32[]{:S(2)}, u32[]{:S(2)}) collective-permute-start(bf16[4,256,1024]{2,1,0:T(8,128)(2,1)S(1)} %pad_maximum_fusion.4), channel_id=1, source_target_pairs={{0,1},{1,2},{2,3},{3,4},{4,5},{5,6},{6,7},{8,9},{9,10},{10,11},{11... | collective-permute-start | bytes 6291464 | tf_op jit(solution)/shard_map/ppermute | solution.py:18
  612.5 35.2 %copy-start.7 = (bf16[1024,512]{1,0:T(8,128)(2,1)S(1)}, bf16[1024,512]{1,0:T(8,128)(2,1)}, u32[]{:S(2)}) copy-start(bf16[1024,512]{1,0:T(8,128)(2,1)} %copy-done.6) | copy-start | bytes 3145732
  612.5 35.2 %copy-start.22 = (f32[1024]{0:T(1024)S(1)}, f32[1024]{0:T(1024)}, u32[]{:S(2)}) copy-start(f32[1024]{0:T(1024)} %copy-done.21) | copy-start | bytes 12292
  612.5 35.3 %copy-start.24 = (f32[512]{0:T(512)S(1)}, f32[512]{0:T(512)}, u32[]{:S(2)}) copy-start(f32[512]{0:T(512)} %param.12) | copy-start | bytes 6148
  612.5 35.3 %copy-start.26 = (bf16[4,256,512]{2,1,0:T(8,128)(2,1)S(1)}, bf16[4,256,512]{2,1,0:T(8,128)(2,1)}, u32[]{:S(2)}) copy-start(bf16[4,256,512]{2,1,0:T(8,128)(2,1)} %get-tuple-element.62) | copy-start | bytes 3145732
  (26 other events, 135.3 us)
Sparse Core Ops, SparseCore 0:
  652.4 162.4 all-reduce.3
where the time goes:
time: 836 us; the launch traced here: 827 us
  matrix products  296 us (35%)
  local copies, waits for them, and re-layouts  208 us (25%)
  waiting for transfers between devices  120 us (14%)
  other arithmetic  86.6 us (10%)
  blocking collectives  73.5 us (9%)
  starting transfers between devices  27.5 us (3%)
  between operations  14.7 us (2%)
    dot_general x4, matrix products, attend_block(): jnp.einsum('hij,ihd->jhd', grad_scores, queries, preferred_element_type=j...  104 us
    dot_general x4, matrix products, attend_block(): jnp.einsum('hij,jhd->ihd', grad_scores, key_rows, preferred_element_type=...  76.2 us
    psum x1, blocking collectives, shards(): lax.psum((grad_all_part[:, :2 * features], grad_all_part[:, 2 * features:...  73.5 us
    psum x1, waiting for transfers between devices, shards(): lax.psum((grad_all_part[:, :2 * features], grad_all_part[:, 2 * features:...  68 us
    ppermute x8, waiting for transfers between devices, from_behind(): return lax.ppermute(block, axis, route)  52.1 us
    reshape x8, local copies, waits for them, and re-layouts, attend_block(): grad_keys.reshape(slots, row_count, features)  37.1 us
    reshape x8, local copies, waits for them, and re-layouts, attend_block(): grad_values.reshape(slots, row_count, features)  37.1 us
    sub x4, matrix products, attend_block(): powers = jnp.exp(scores - row_max)  33.7 us
  transfers between devices with their start and end apart: 9, of which 5 were waited for; matrix products, arithmetic and copies ran while one was open for 6% of the time, Pallas kernels for 0%

commit v1 on v0

v1 whole, which is shorter than its diff:
```python
import functools

import jax
import jax.numpy as jnp
from jax import lax
from jax.experimental import pallas as pl
from jax.experimental.pallas import tpu as pltpu
from jax.sharding import PartitionSpec as P

BLK = 256
PAIR = 128
EPSILON = 1e-06
BF = jnp.bfloat16
F32 = jnp.float32
MIB = 1 << 20
VM = pl.BlockSpec(memory_space=pltpu.VMEM)
SM = pl.BlockSpec(memory_space=pltpu.SMEM)
NT = (((1,), (1,)), ((), ()))


def mm(a, b):
    return jnp.dot(a, b, preferred_element_type=F32)


def mm_nt(a, b):
    return lax.dot_general(a, b, NT, preferred_element_type=F32)


def rms(rows):
    values = rows.astype(F32)
    inv = lax.rsqrt(jnp.mean(values * values, axis=-1, keepdims=True) + EPSILON)
    return values, inv


def named_mask(ids, cnt, reader, owner, blocks, slots):
    mask = jnp.int32(0)
    for b in range(blocks):
        count = cnt[reader * blocks + b]
        for j in range(slots):
            entry = ids[(reader * blocks + b) * slots + j]
            hit = jnp.logical_and(j < count, lax.div(entry, blocks) == owner)
            mask = mask | jnp.where(hit, jnp.left_shift(1, lax.rem(entry, blocks)), 0)
    return mask


def first_two(mask, blocks):
    def lowest(m):
        at = jnp.int32(blocks - 1)
        for b in range(blocks - 2, -1, -1):
            at = jnp.where((m & (1 << b)) != 0, b, at)
        return at

    first = lowest(mask)
    return first, lowest(mask & ~jnp.left_shift(1, first))


def send_table(ids, cnt, pos, extent_x, extent_y, blocks, slots):
    x, y = pos[0], pos[1]
    me = x * extent_y + y
    readers = (
        jnp.minimum(x + 1, extent_x - 1) * extent_y + y,
        jnp.maximum(x - 1, 0) * extent_y + y,
        x * extent_y + jnp.minimum(y + 1, extent_y - 1),
        x * extent_y + jnp.maximum(y - 1, 0),
    )
    return [first_two(named_mask(ids, cnt, r, me, blocks, slots), blocks) for r in readers]


def pool_table(ids, cnt, pos, extent_y, blocks, slots):
    me = pos[0] * extent_y + pos[1]
    owners = (me - extent_y, me + extent_y, me - 1, me + 1)
    masks = [named_mask(ids, cnt, me, o, blocks, slots) for o in owners]
    table = []
    for b in range(blocks):
        row = []
        for j in range(slots):
            entry = ids[(me * blocks + b) * slots + j]
            owner, off = lax.div(entry, blocks), lax.rem(entry, blocks)
            at = off
            for seg, (o, mask) in enumerate(zip(owners, masks)):
                below = mask & (jnp.left_shift(1, off) - 1)
                at = jnp.where(owner == o, blocks + 2 * seg + jnp.where(below != 0, 1, 0), at)
            live = j < cnt[me * blocks + b]
            row.append((jnp.where(live, at, b), live))
        table.append(row)
    return table


def order_columns(order_ref):
    n = order_ref.shape[1]
    return jnp.broadcast_to(order_ref[...], (128, n)).T


def one_hot_rows(cols, n):
    lane = lax.broadcasted_iota(jnp.int32, cols.shape, 1)
    return jnp.concatenate(
        [(cols == lane + c).astype(F32).astype(BF) for c in range(0, n, 128)], axis=1
    )


def one_hot_back(order_ref, start, rows):
    n = order_ref.shape[1]
    row = lax.broadcasted_iota(jnp.int32, (rows, n), 0) + start
    return (row == order_ref[...]).astype(F32).astype(BF)


def sort_kernel(dims, pos, ids, cnt, order, tok, out, s0, s1, s2, s3, cols):
    extent_x, extent_y, blocks, slots = dims
    n = tok.shape[0]
    cols[...] = order_columns(order)

    def body(b, _):
        rows = pl.ds(pl.multiple_of(b * BLK, BLK), BLK)
        out[rows, :] = mm(one_hot_rows(cols[rows, :], n), tok[...]).astype(BF)
        return 0

    lax.fori_loop(0, n // BLK, body, 0)
    table = send_table(ids, cnt, pos, extent_x, extent_y, blocks, slots)
    for ref, pair in zip((s0, s1, s2, s3), table):
        for k, b in enumerate(pair):
            ref[k * BLK : (k + 1) * BLK, :] = out[pl.ds(pl.multiple_of(b * BLK, BLK), BLK), :]


def project_kernel(groups, np_, order, tok, cot, gain, w_qk, w_v, w_out, *rest):
    sc, n_t = rest[:2]
    outs = rest[2:-1]
    cols = rest[-1]
    d = tok.shape[1]
    n = tok.shape[0]
    cols[...] = order_columns(order)
    per = 8

    def body(b, _):
        rows = pl.ds(pl.multiple_of(b * BLK, BLK), BLK)
        grad = mm(one_hot_rows(cols[rows, :], n), cot[...]).astype(BF)
        sc[b] = grad
        values, inv = rms(tok[rows, :])
        normed = (values * inv * gain[...]).astype(BF)
        n_t[b] = normed.T
        query = (mm(normed, w_qk[:, :d]).astype(BF)) * BF(0.125)
        key = mm(normed, w_qk[:, d:]).astype(BF)
        value = mm(normed, w_v[...]).astype(BF)
        dctx = mm_nt(grad, w_out[...]).astype(BF)
        for at, mat in enumerate((query, key, value, dctx)):
            mat_t = mat.T
            for g in range(groups):
                for p in range(np_):
                    lo = (g * np_ + p) * PAIR
                    outs[g * per + 2 * at][b, p] = mat[:, lo : lo + PAIR]
                    outs[g * per + 2 * at + 1][b, p] = mat_t[lo : lo + PAIR, :]
        return 0

    lax.fori_loop(0, n // BLK, body, 0)


def attend_kernel(dims, np_, pos, ids, cnt, r0, r1, r2, r3, gain, w_k, w_v,
                  qn, qt, kn, kt, vn, vt, gn, gt,
                  ctx_t, dq_t, own, h0, h1, h2, h3, n_t,
                  pkn, pkt, pvn, pvt, acc, s_scr, dp_scr, p_scr, ds_scr, where_ref):
    extent_x, extent_y, blocks, slots = dims
    table = pool_table(ids, cnt, pos, extent_y, blocks, slots)
    for b in range(blocks):
        for j in range(slots):
            where_ref[b * slots + j] = table[b][j][0]
            where_ref[blocks * slots + b * slots + j] = table[b][j][1].astype(jnp.int32)
    for own_ref, pool in ((kn, pkn), (kt, pkt), (vn, pvn), (vt, pvt)):
        pool[:blocks] = own_ref[...]
    for seg, ref in enumerate((r0, r1, r2, r3)):
        for k in range(2):
            at = blocks + 2 * seg + k
            values, inv = rms(ref[k * BLK : (k + 1) * BLK, :])
            normed = (values * inv * gain[...]).astype(BF)
            n_t[2 * seg + k] = normed.T
            for w, nat, tra in ((w_k, pkn, pkt), (w_v, pvn, pvt)):
                made = mm(normed, w[...]).astype(BF)
                made_t = made.T
                for p in range(np_):
                    nat[at, p] = made[:, p * PAIR : (p + 1) * PAIR]
                    tra[at, p] = made_t[p * PAIR : (p + 1) * PAIR, :]
    acc[...] = jnp.zeros_like(acc)
    lane = lax.broadcasted_iota(jnp.int32, (1, PAIR), 1)
    low_lanes = (lane < PAIR // 2).astype(F32).astype(BF)
    high_lanes = (lane >= PAIR // 2).astype(F32).astype(BF)
    half = PAIR // 2

    def diagonal(mat):
        zero = jnp.zeros((half, BLK), BF)
        return jnp.concatenate(
            [jnp.concatenate([mat[:half], zero], axis=1), jnp.concatenate([zero, mat[half:]], axis=1)],
            axis=0,
        )

    def body(step, _):
        b, p = lax.div(step, np_), lax.rem(step, np_)
        q_diag, g_diag = diagonal(qt[b, p]), diagonal(gt[b, p])
        at = [b] + [where_ref[b * slots + j] for j in range(slots)]
        live = [None] + [where_ref[blocks * slots + b * slots + j] for j in range(slots)]
        top = None
        for j in range(slots + 1):
            s = mm(pkn[at[j], p], q_diag)
            if j:
                s = jnp.where(live[j] != 0, s, -1e30)
            s_scr[j] = s
            m = jnp.max(s, axis=0, keepdims=True)
            top = m if top is None else jnp.maximum(top, m)
        total = jnp.zeros((1, 2 * BLK), F32)
        centre = jnp.zeros((1, 2 * BLK), F32)
        for j in range(slots + 1):
            e = jnp.exp(s_scr[j] - top)
            s_scr[j] = e
            total += jnp.sum(e, axis=0, keepdims=True)
            dp = mm(pvn[at[j], p], g_diag)
            dp_scr[j] = dp
            centre += jnp.sum(e * dp, axis=0, keepdims=True)
        scale = 1.0 / total
        centre = centre * scale
        for j in range(slots + 1):
            prob = s_scr[j] * scale
            p_scr[j] = prob.astype(BF)
            ds_scr[j] = (prob * (dp_scr[j] - centre)).astype(BF)
        q_rows = qn[b, p]
        g_rows = gn[b, p]
        q_mask = jnp.concatenate([q_rows * low_lanes, q_rows * high_lanes], axis=0)
        g_mask = jnp.concatenate([g_rows * low_lanes, g_rows * high_lanes], axis=0)
        for h in range(2):
            feats, lanes = slice(h * half, (h + 1) * half), slice(h * BLK, (h + 1) * BLK)
            ctx = dq = None
            for j in range(slots + 1):
                c = mm(pvt[at[j], p, feats, :], p_scr[j, :, lanes])
                k = mm(pkt[at[j], p, feats, :], ds_scr[j, :, lanes])
                ctx = c if ctx is None else ctx + c
                dq = k if dq is None else dq + k
            rows = pl.ds(pl.multiple_of(p * PAIR + h * half, half), half)
            ctx_t[b, rows, :] = ctx.astype(BF)
            dq_t[b, rows, :] = (dq * 0.125).astype(BF)
        for j in range(slots + 1):
            acc[at[j], 0, p] += mm(ds_scr[j], q_mask)
            acc[at[j], 1, p] += mm(p_scr[j], g_mask)
        return 0

    lax.fori_loop(0, blocks * np_, body, 0)
    own[...] = acc[:blocks]
    for seg, ref in enumerate((h0, h1, h2, h3)):
        ref[...] = acc[blocks + 2 * seg : blocks + 2 * seg + 2].astype(BF)


def weights_kernel(np_, gain, w_qk, w_v, sc, n_t, far_t, ctx_t, dq_t, own, h0, h1, h2, h3,
                   out, gain_out, rows_scr, nt_scr):
    blocks = n_t.shape[0]
    d = w_v.shape[0]
    for b in range(blocks):
        nt_scr[:, b * BLK : (b + 1) * BLK] = n_t[b]
    for b in range(far_t.shape[0]):
        at = blocks + b
        nt_scr[:, at * BLK : (at + 1) * BLK] = far_t[b]
    for part in range(2):
        for p in range(np_):
            lanes = slice(p * PAIR, (p + 1) * PAIR)
            for b in range(blocks):
                rows_scr[part, b * BLK : (b + 1) * BLK, lanes] = own[b, part, p].astype(BF)
            for seg, ref in enumerate((h0, h1, h2, h3)):
                for k in range(2):
                    at = blocks + 2 * seg + k
                    rows_scr[part, at * BLK : (at + 1) * BLK, lanes] = ref[k, part, p]
    g_q = None
    g_o = None
    for b in range(blocks):
        a = mm_nt(n_t[b], dq_t[b])
        c = mm(ctx_t[b], sc[b])
        g_q = a if g_q is None else g_q + a
        g_o = c if g_o is None else g_o + c
    out[0] = g_q.astype(BF)
    out[3] = g_o.astype(BF)
    g_k = mm(nt_scr[...], rows_scr[0])
    out[1] = g_k.astype(BF)
    g_v = mm(nt_scr[...], rows_scr[1])
    out[2] = g_v.astype(BF)
    total = (
        jnp.sum(g_q * w_qk[:, :d].astype(F32), axis=1, keepdims=True)
        + jnp.sum(g_k * w_qk[:, d:].astype(F32), axis=1, keepdims=True)
        + jnp.sum(g_v * w_v[...].astype(F32), axis=1, keepdims=True)
    )
    gain_out[...] = jnp.broadcast_to(total, (d, 128)).T[:8] / gain[...]


def output_kernel(order, w_qk, w_out, ctx_t, dq_t, out, part):
    blocks, d = ctx_t.shape[:2]

    def body(a, _):
        rows = pl.ds(pl.multiple_of(a * BLK, BLK), BLK)
        back = one_hot_back(order, a * BLK, BLK)
        ctx = dq = None
        for b in range(blocks):
            pick = back[:, b * BLK : (b + 1) * BLK]
            c, k = mm_nt(pick, ctx_t[b]), mm_nt(pick, dq_t[b])
            ctx = c if ctx is None else ctx + c
            dq = k if dq is None else dq + k
        out[rows, :] = mm(ctx.astype(BF), w_out[...]).astype(BF)
        part[rows, :] = mm_nt(dq.astype(BF), w_qk[:, :d])
        return 0

    lax.fori_loop(0, out.shape[0] // BLK, body, 0)


def rows_kernel(dims, np_, pos, ids, cnt, order, tok, gain, w_qk, w_v, part, own, b0, b1, b2, b3,
                out, acc, rows_scr):
    extent_x, extent_y, blocks, slots = dims
    d = w_v.shape[0]
    acc[...] = own[...]
    table = send_table(ids, cnt, pos, extent_x, extent_y, blocks, slots)
    for ref, pair in zip((b0, b1, b2, b3), table):
        for k, b in enumerate(pair):
            acc[b] += ref[k].astype(F32)
    for half in range(2):
        for p in range(np_):
            lo = half * d + p * PAIR
            for b in range(blocks):
                rows_scr[b * BLK : (b + 1) * BLK, lo : lo + PAIR] = acc[b, half, p].astype(BF)

    def body(a, _):
        rows = pl.ds(pl.multiple_of(a * BLK, BLK), BLK)
        back = one_hot_back(order, a * BLK, BLK)
        mine = mm(back, rows_scr[...]).astype(BF)
        grad = part[rows, :] + mm_nt(mine[:, :d], w_qk[:, d:]) + mm_nt(mine[:, d:], w_v[...])
        values, inv = rms(tok[rows, :])
        u = grad * gain[...]
        mean = jnp.mean(values * u, axis=-1, keepdims=True)
        out[rows, :] = inv * u - values * (inv * inv * inv * mean)
        return 0

    lax.fori_loop(0, out.shape[0] // BLK, body, 0)


def step_to(block, axis, distance):
    n = lax.axis_size(axis)
    route = [(i, i + distance) for i in range(n) if 0 <= i + distance < n]
    return lax.ppermute(block, axis, route)


def stage_of(axis, stride, count):
    n = lax.axis_size(axis)
    me = lax.rem(lax.div(lax.axis_index(axis), stride), count)

    def route(s):
        pairs = []
        for i in range(n):
            k = (i // stride) % count
            pairs.append((i, i + (((k + s) % count) - k) * stride))
        return pairs

    return me, route


def scatter_sum(rows, gain, stage, axis, kind):
    me, route = stage
    count = stage_count(stage)
    size = rows.shape[0] // count
    pad = 16
    sent = []
    tail = jnp.broadcast_to(gain, (pad, gain.shape[1])).astype(kind)
    for s in range(1, count):
        to = lax.rem(me + s, count)
        part = lax.dynamic_slice_in_dim(rows, to * size, size).astype(kind)
        sent.append(lax.ppermute(jnp.concatenate([part, tail], axis=0), axis, route(s)))
    total = lax.dynamic_slice_in_dim(rows, me * size, size).astype(F32)
    for r in sent:
        total = total + r[:size].astype(F32)
        gain = gain + r[size : size + 1].astype(F32)
    return total, gain


def gather_all(rows, stage, axis):
    me, route = stage
    count = stage_count(stage)
    size = rows.shape[0]
    out = jnp.zeros((count * size, rows.shape[1]), rows.dtype)
    out = lax.dynamic_update_slice_in_dim(out, rows, me * size, 0)
    for s in range(1, count):
        got = lax.ppermute(rows, axis, route(s))
        out = lax.dynamic_update_slice_in_dim(out, got, lax.rem(me - s + count, count) * size, 0)
    return out


def stage_count(stage):
    return stage[1].count


def make_stage(axis, stride, count):
    me, route = stage_of(axis, stride, count)
    route.count = count
    return me, route


def call(kernel, name, outs, ins, specs, scratch, limit, flops, moved, exps=0):
    return pl.pallas_call(
        kernel,
        out_shape=outs,
        in_specs=specs,
        out_specs=jax.tree.map(lambda _: VM, outs),
        scratch_shapes=scratch,
        compiler_params=pltpu.CompilerParams(vmem_limit_bytes=limit * MIB),
        cost_estimate=pl.CostEstimate(flops=flops, bytes_accessed=moved, transcendentals=exps),
        name=name,
    )(*ins)


def shards(tokens, norm_gain, w_query_key, w_value, w_out, cotangent, block_order,
           neighbour_ids, neighbour_count):
    n, d = tokens.shape[2:]
    extent_x, extent_y, blocks, slots = neighbour_ids.shape
    dims = (extent_x, extent_y, blocks, slots)
    groups = 1
    np_ = d // PAIR // groups
    tok, cot = tokens[0, 0], cotangent[0, 0]
    order = block_order[0]
    gain = norm_gain[None, :]
    ids = neighbour_ids.reshape(-1)
    cnt = neighbour_count.reshape(-1)
    pos = jnp.stack([lax.axis_index("bx"), lax.axis_index("by")]).astype(jnp.int32)
    shape = jax.ShapeDtypeStruct

    sends = [shape((2 * BLK, d), BF)] * 4
    sorted_rows, *sent = call(
        functools.partial(sort_kernel, dims), "sort_rows",
        [shape((n, d), BF)] + sends, (pos, ids, cnt, order, tok), [SM, SM, SM, VM, VM],
        [pltpu.VMEM((n, 128), jnp.int32)], 32, 2 * n * n * d, 4 << 20,
    )
    arrived = [
        step_to(sent[0], "bx", 1), step_to(sent[1], "bx", -1),
        step_to(sent[2], "by", 1), step_to(sent[3], "by", -1),
    ]
    nat, tra = shape((blocks, np_, BLK, PAIR), BF), shape((blocks, np_, PAIR, BLK), BF)
    sc, n_t, *made = call(
        functools.partial(project_kernel, groups, np_), "project",
        [shape((blocks, BLK, d), BF), shape((blocks, d, BLK), BF)] + [nat, tra] * (4 * groups),
        (order, sorted_rows, cot, gain, w_query_key, w_value, w_out), [VM] * 7,
        [pltpu.VMEM((n, 128), jnp.int32)], 40, 2 * n * n * d + 8 * n * d * d, 14 << 20,
    )
    pool = blocks + 8
    back = [shape((2, 2, np_, BLK, PAIR), BF)] * 4
    tile = (slots + 1, BLK, 2 * BLK)
    ctx_t, dq_t, own, h0, h1, h2, h3, far_t = call(
        functools.partial(attend_kernel, dims, np_), "attend",
        [shape((blocks, d, BLK), BF)] * 2 + [shape((blocks, 2, np_, BLK, PAIR), F32)] + back
        + [shape((8, d, BLK), BF)],
        (pos, ids, cnt, *arrived, gain, w_query_key[:, d:], w_value, *made),
        [SM] * 3 + [VM] * 15,
        [pltpu.VMEM((pool, np_, BLK, PAIR), BF), pltpu.VMEM((pool, np_, PAIR, BLK), BF)] * 2
        + [pltpu.VMEM((pool, 2, np_, BLK, PAIR), F32), pltpu.VMEM(tile, F32), pltpu.VMEM(tile, F32),
           pltpu.VMEM(tile, BF), pltpu.VMEM(tile, BF), pltpu.SMEM((2 * blocks * slots,), jnp.int32)],
        60, 12 * blocks * 5 * BLK * BLK * d, 24 << 20, blocks * 5 * BLK * BLK * 8,
    )
    returned = [
        step_to(h0, "bx", -1), step_to(h1, "bx", 1), step_to(h2, "by", -1), step_to(h3, "by", 1),
    ]
    terms, gain_term = call(
        functools.partial(weights_kernel, np_), "weight_terms",
        [shape((4, d, d), BF), shape((8, d), F32)],
        (gain, w_query_key, w_value, sc, n_t, far_t, ctx_t, dq_t, own, h0, h1, h2, h3), [VM] * 13,
        [pltpu.VMEM((2, pool * BLK, d), BF), pltpu.VMEM((d, pool * BLK), BF)],
        56, 4 * n * d * d + 4 * pool * BLK * d * d, 20 << 20,
    )
    branch_out, part = call(
        output_kernel, "branch_rows", [shape((n, d), BF), shape((n, d), F32)],
        (order, w_query_key, w_out, ctx_t, dq_t), [VM] * 5, [], 40,
        4 * n * n * d + 4 * n * d * d, 7 << 20,
    )

    stages = [("by", 1, 2), ("by", 2, 4), ("bx", 1, 4), ("bx", 4, 4)]
    made_stages = [make_stage(*s) for s in stages]
    rows, gain_sum = terms.reshape(4 * d, d), gain_term[:1]
    for (axis, _, _), stage, kind in zip(stages, made_stages, (BF, BF, F32, F32)):
        rows, gain_sum = scatter_sum(rows, gain_sum, stage, axis, kind)
    rows = rows.astype(BF)
    for (axis, _, _), stage in reversed(list(zip(stages, made_stages))):
        rows = gather_all(rows, stage, axis)
    grads = rows.reshape(4, d, d).astype(F32)

    b_x1, b_xm, b_y1, b_ym = returned
    grad_rows = call(
        functools.partial(rows_kernel, dims, np_), "token_rows", shape((n, d), F32),
        (pos, ids, cnt, order, tok, gain, w_query_key, w_value, part, own, b_x1, b_xm, b_y1, b_ym),
        [SM] * 3 + [VM] * 11,
        [pltpu.VMEM((blocks, 2, np_, BLK, PAIR), F32), pltpu.VMEM((n, 2 * d), BF)],
        56, 4 * n * n * d + 4 * n * d * d, 16 << 20,
    )
    return (
        branch_out[None, None],
        grad_rows[None, None],
        jnp.concatenate([grads[0], grads[1]], axis=1),
        grads[2],
        grads[3],
        gain_sum[0],
    )


def solution(mesh):
    local = P("bx", "by", None, None)
    placed = (local, P(), P(), P(), P(), local, P("bx", "by", None), P(), P())
    return jax.shard_map(
        shards,
        mesh=mesh,
        in_specs=placed,
        out_specs=(local, local, P(), P(), P(), P()),
        check_vma=False,
    )
```

time: 836 us -> 234 us (0.28)
  matrix products: 296 us -> 0 us
  local copies, waits for them, and re-layouts: 208 us -> 25.7 us
  Pallas kernels: 0 us -> 95.2 us
  waiting for transfers between devices: 120 us -> 36.5 us
  other arithmetic: 86.6 us -> 9.56 us
  blocking collectives: 73.5 us -> 0 us
  starting transfers between devices: 27.5 us -> 64.6 us
  between operations: 14.7 us -> 1.19 us
    dot_general x27 -> x0, matrix products: 262 us -> none  [the longest x4 104 us: attend_block(): jnp.einsum('hij,ihd->jhd', grad_scores, queries, preferred_element_type=j...]
    pallas_call x0 -> x6, Pallas kernels: none -> 95.2 us  [call(): pl.pallas_call(kernel, out_shape=outs, in_specs=specs, out_specs=jax.tree...]
    reshape x16 -> x2, local copies, waits for them, and re-layouts: 74.2 us -> 0.36 us  [the longest x1 0.26 us: shards(): ids = neighbour_ids.reshape(-1)]
    psum x1 -> x0, blocking collectives: 73.5 us -> none  [shards(): lax.psum((grad_all_part[:, :2 * features], grad_all_part[:, 2 * features:...]
    psum x1 -> x0, waiting for transfers between devices: 68 us -> none  [shards(): lax.psum((grad_all_part[:, :2 * features], grad_all_part[:, 2 * features:...]
    scatter-add x8 -> x0, other arithmetic: 66.5 us -> none  [the longest x4 33.5 us: per_block(): value_total = totals[1].at[key_ids].add(value_terms)]
    gather x8 -> x0, local copies, waits for them, and re-layouts: 46.2 us -> none  [the longest x4 27 us: per_block(): key_pool[key_ids]]
    ppermute x8 -> x28, starting transfers between devices: 27.5 us -> 64.6 us  [the longest x8 28 us: step_to(): return lax.ppermute(block, axis, route)]
  transfers between devices with their start and end apart: 9 -> 28, of which waited for: 5 -> 16; matrix products, arithmetic and copies ran while one was open for 6% -> 1% of each run, Pallas kernels for 0% -> 10%
where the time goes in v1:
time: 234 us; the launch traced here: 233 us
  Pallas kernels  95.2 us (41%)
  starting transfers between devices  64.6 us (28%)
  waiting for transfers between devices  36.5 us (16%)
  local copies, waits for them, and re-layouts  25.7 us (11%)
  other arithmetic  9.56 us (4%)
    pallas_call x6, Pallas kernels, call(): pl.pallas_call(kernel, out_shape=outs, in_specs=specs, out_specs=jax.tree...  95.2 us
    ppermute x8, starting transfers between devices, step_to(): return lax.ppermute(block, axis, route)  28 us
    ppermute x10, waiting for transfers between devices, scatter_sum(): lax.ppermute(jnp.concatenate([part, tail], axis=0), axis, route(s))  24 us
    ppermute x10, starting transfers between devices, gather_all(): got = lax.ppermute(rows, axis, route(s))  21.2 us
    unnamed x68, local copies, waits for them, and re-layouts  20 us
    ppermute x10, starting transfers between devices, scatter_sum(): lax.ppermute(jnp.concatenate([part, tail], axis=0), axis, route(s))  15.4 us
    ppermute x10, waiting for transfers between devices, gather_all(): got = lax.ppermute(rows, axis, route(s))  12.5 us
  transfers between devices with their start and end apart: 28, of which 16 were waited for; matrix products, arithmetic and copies ran while one was open for 1% of the time, Pallas kernels for 10%

profile of v1, /device:TPU:1, one launch (start us, length us, event | category | flops | bytes accessed | tf_op | source)
XLA Modules:
  0.0 232.7 jit_solution(16331945730865761599)
XLA Ops:
  5.2 4.3 %sort_rows.1 = (bf16[1024,512]{1,0:T(8,128)(2,1)S(1)}, bf16[512,512]{1,0:T(8,128)(2,1)}, bf16[512,512]{1,0:T(8,128)(2,1)}, bf16[512,512]{1,0:T(8,128)(2,1)}, bf16[512,512]{1,0:T(8,128)(2,1)}) custom-call(s32[2]{0:T(128)S(1)} %pad_add_fusion.pos, s32[2048]{0:T(1024)S(1)} %reshape.33.ids, s32[512]{0:T(512)S(1)} %reshape.34.cnt, s32[1,1024]{1,0:T(1,128)S(1)} %bitcast.19, ...), custom_call_target="tpu_custom_call" | custom-call | flops 1073741824 | bytes 4194304 | tf_op jit(solution)/shard_map/sort_rows/pallas_call | solution.py:395
  10.5 5.2 %collective-permute-start = (bf16[512,512]{1,0:T(8,128)(2,1)}, bf16[512,512]{1,0:T(8,128)(2,1)}, u32[]{:S(2)}, u32[]{:S(2)}) collective-permute-start(bf16[512,512]{1,0:T(8,128)(2,1)} %get-tuple-element.33), channel_id=1, source_target_pairs={{0,8},{8,16},{16,24},{24,32},{32,40},{40,48},{48,56},{56,64},{64,7... | collective-permute-start | bytes 1572872 | tf_op jit(solution)/shard_map/ppermute | solution.py:337
  16.9 4.0 %collective-permute-start.2 = (bf16[512,512]{1,0:T(8,128)(2,1)}, bf16[512,512]{1,0:T(8,128)(2,1)}, u32[]{:S(2)}, u32[]{:S(2)}) collective-permute-start(bf16[512,512]{1,0:T(8,128)(2,1)} %get-tuple-element.35), channel_id=1, source_target_pairs={{0,1},{1,2},{2,3},{3,4},{4,5},{5,6},{6,7},{8,9},{9,10},{10,11},{11... | collective-permute-start | bytes 1572872 | tf_op jit(solution)/shard_map/ppermute | solution.py:337
  25.0 5.7 %project.1 = (bf16[4,256,512]{2,1,0:T(8,128)(2,1)S(1)}, bf16[4,512,256]{2,1,0:T(8,128)(2,1)S(1)}, bf16[4,4,256,128]{3,2,1,0:T(8,128)(2,1)S(1)}, bf16[4,4,128,256...) custom-call(s32[1,1024]{1,0:T(1,128)S(1)} %bitcast.20, ...), custom_call_target="tpu_custom_call" | custom-call | flops 3221225472 | bytes 14680064 | tf_op jit(solution)/shard_map/project/pallas_call | solution.py:395
  40.6 55.9 %attend.1 = (bf16[4,512,256]{2,1,0:T(8,128)(2,1)}, bf16[4,512,256]{2,1,0:T(8,128)(2,1)}, f32[4,2,4,256,128]{4,3,2,1,0:T(8,128)}, bf16[2,2,4,256,128]{4,3,2,1,0:T...) custom-call(s32[2]{0:T(128)} %copy-done.14, ...), custom_call_target="tpu_custom_call" | custom-call | flops 8053063680 | bytes 25165824 | tf_op jit(solution)/shard_map/attend/pallas_call | solution.py:395
  96.5 11.9 %weight_terms.1 = (bf16[4,512,512]{2,1,0:T(8,128)(2,1)}, f32[8,512]{1,0:T(8,128)}) custom-call(f32[1,512]{1,0:T(1,128)} %bitcast.15, bf16[512,1024]{1,0:T(8,128)(2,1)} %w_qk.7, bf16[512,512]{1,0:T(8,128)(2,1)} %w_v.7, bf16[4,256,512]{2,1,0:T(8,128)(2,1)} %copy-done.6, bf16[4,512,256]{2,1,0:T(8,128)(2,1)} %copy-done.7, ...), custom_call_target="tpu_custom_call" | custom-call | flops 4294967296 | bytes 20971520 | tf_op jit(solution)/shard_map/weight_terms/pallas_call | solution.py:395
  110.8 2.8 %collective-permute-done.8 = bf16[1040,512]{1,0:T(8,128)(2,1)} collective-permute-done((bf16[1040,512]{1,0:T(8,128)(2,1)S(1)}, bf16[1040,512]{1,0:T(8,128)(2,1)}, u32[]{:S(2)}, u32[]{:S(2)}) %collective-permute-start.8) | collective-permute-done | bytes 1064992 | tf_op jit(solution)/shard_map/ppermute | solution.py:364
  116.4 3.2 %collective-permute-start.10 = (bf16[272,512]{1,0:T(8,128)(2,1)S(1)}, bf16[272,512]{1,0:T(8,128)(2,1)}, u32[]{:S(2)}, u32[]{:S(2)}) collective-permute-start(bf16[272,512]{1,0:T(8,128)(2,1)S(1)} %get-tuple-element.84), channel_id=1, source_target_pairs={{0,4},{1,5},{2,6},{3,7},{4,0},{5,1},{6,2},{7,3},{8,12},{9,13},{10,... | collective-permute-start | bytes 835592 | tf_op jit(solution)/shard_map/ppermute | solution.py:364
  121.0 5.4 %collective-permute-done.10 = bf16[272,512]{1,0:T(8,128)(2,1)} collective-permute-done((bf16[272,512]{1,0:T(8,128)(2,1)S(1)}, bf16[272,512]{1,0:T(8,128)(2,1)}, u32[]{:S(2)}, u32[]{:S(2)}) %collective-permute-start.10) | collective-permute-done | bytes 278560 | tf_op jit(solution)/shard_map/ppermute | solution.py:364
  126.4 6.0 %collective-permute-done.11 = bf16[272,512]{1,0:T(8,128)(2,1)} collective-permute-done((bf16[272,512]{1,0:T(8,128)(2,1)S(1)}, bf16[272,512]{1,0:T(8,128)(2,1)}, u32[]{:S(2)}, u32[]{:S(2)}) %collective-permute-start.11) | collective-permute-done | bytes 278560 | tf_op jit(solution)/shard_map/ppermute | solution.py:364
  135.6 2.4 %collective-permute-start.12 = (f32[80,512]{1,0:T(8,128)}, f32[80,512]{1,0:T(8,128)}, u32[]{:S(2)}, u32[]{:S(2)}) collective-permute-start(f32[80,512]{1,0:T(8,128)} %get-tuple-element.80), channel_id=1, source_target_pairs={{0,8},{8,16},{16,24},{24,0},{32,40},{40,48},{48,56},{56,32},{64,72... | collective-permute-start | bytes 491528 | tf_op jit(solution)/shard_map/ppermute | solution.py:364
  138.0 2.5 %collective-permute-start.13 = (f32[80,512]{1,0:T(8,128)S(1)}, f32[80,512]{1,0:T(8,128)}, u32[]{:S(2)}, u32[]{:S(2)}) collective-permute-start(f32[80,512]{1,0:T(8,128)S(1)} %get-tuple-element.81), channel_id=1, source_target_pairs={{0,16},{8,24},{16,0},{24,8},{32,48},{40,56},{48,32},{56,40},{64,80... | collective-permute-start | bytes 491528 | tf_op jit(solution)/shard_map/ppermute | solution.py:364
  143.3 4.4 %collective-permute-done.13 = f32[80,512]{1,0:T(8,128)} collective-permute-done((f32[80,512]{1,0:T(8,128)S(1)}, f32[80,512]{1,0:T(8,128)}, u32[]{:S(2)}, u32[]{:S(2)}) %collective-permute-start.13) | collective-permute-done | bytes 163872 | tf_op jit(solution)/shard_map/ppermute | solution.py:364
  150.8 3.2 %collective-permute-start.16 = (f32[32,512]{1,0:T(8,128)S(1)}, f32[32,512]{1,0:T(8,128)S(1)}, u32[]{:S(2)}, u32[]{:S(2)}) collective-permute-start(f32[32,512]{1,0:T(8,128)S(1)} %get-tuple-element.78), channel_id=1, source_target_pairs={{0,64},{8,72},{16,80},{24,88},{32,96},{40,104},{48,112},{56,120},{... | collective-permute-start | bytes 196616 | tf_op jit(solution)/shard_map/ppermute | solution.py:364
  157.7 2.4 %collective-permute-start.19 = (bf16[16,512]{1,0:T(8,128)(2,1)S(1)}, bf16[16,512]{1,0:T(8,128)(2,1)S(1)}, u32[]{:S(2)}, u32[]{:S(2)}) collective-permute-start(bf16[16,512]{1,0:T(8,128)(2,1)S(1)} %get-tuple-element.61), channel_id=1, source_target_pairs={{0,64},{8,72},{16,80},{24,88},{32,96},{40,104},{48,112},{56,120},{... | collective-permute-start | bytes 49160 | tf_op jit(solution)/shard_map/ppermute | solution.py:379
  162.7 2.5 %collective-permute-start.21 = (bf16[64,512]{1,0:T(8,128)(2,1)S(1)}, bf16[64,512]{1,0:T(8,128)(2,1)S(1)}, u32[]{:S(2)}, u32[]{:S(2)}) collective-permute-start(bf16[64,512]{1,0:T(8,128)(2,1)S(1)} %constant_dynamic-update-slice_fusion.10), channel_id=1, source_target_pairs={{0,8},{8,16},{16,24},{24,0},{32,40},{40,48},{48,56},{56,32},{64,72... | collective-permute-start | bytes 196616 | tf_op jit(solution)/shard_map/ppermute | solution.py:379
  165.2 2.5 %collective-permute-start.22 = (bf16[64,512]{1,0:T(8,128)(2,1)S(1)}, bf16[64,512]{1,0:T(8,128)(2,1)S(1)}, u32[]{:S(2)}, u32[]{:S(2)}) collective-permute-start(bf16[64,512]{1,0:T(8,128)(2,1)S(1)} %constant_dynamic-update-slice_fusion.10), channel_id=1, source_target_pairs={{0,16},{8,24},{16,0},{24,8},{32,48},{40,56},{48,32},{56,40},{64,80... | collective-permute-start | bytes 196616 | tf_op jit(solution)/shard_map/ppermute | solution.py:379
  172.6 2.6 %collective-permute-start.25 = (bf16[256,512]{1,0:T(8,128)(2,1)S(1)}, bf16[256,512]{1,0:T(8,128)(2,1)S(1)}, u32[]{:S(2)}, u32[]{:S(2)}) collective-permute-start(bf16[256,512]{1,0:T(8,128)(2,1)S(1)} %constant_dynamic-update-slice_fusion.6), channel_id=1, source_target_pairs={{0,4},{1,5},{2,6},{3,7},{4,0},{5,1},{6,2},{7,3},{8,12},{9,13},{10,... | collective-permute-start | bytes 786440 | tf_op jit(solution)/shard_map/ppermute | solution.py:379
  176.6 4.1 %collective-permute-start.5 = (bf16[2,2,4,256,128]{4,3,2,1,0:T(8,128)(2,1)}, bf16[2,2,4,256,128]{4,3,2,1,0:T(8,128)(2,1)S(1)}, u32[]{:S(2)}, u32[]{:S(2)}) collective-permute-start(bf16[2,2,4,256,128]{4,3,2,1,0:T(8,128)(2,1)} %get-tuple-element.52.h1), channel_id=1, source_target_pairs={{0,8},{8,16},{16,24},{24,32},{32,40},{40,48},{48,56},{56,64},{64,7... | collective-permute-start | bytes 3145736 | tf_op jit(solution)/shard_map/ppermute | solution.py:337
  180.6 8.4 %collective-permute-start.6 = (bf16[2,2,4,256,128]{4,3,2,1,0:T(8,128)(2,1)S(1)}, bf16[2,2,4,256,128]{4,3,2,1,0:T(8,128)(2,1)S(1)}, u32[]{:S(2)}, u32[]{:S(2)}) collective-permute-start(bf16[2,2,4,256,128]{4,3,2,1,0:T(8,128)(2,1)S(1)} %copy-done.28), channel_id=1, source_target_pairs={{1,0},{2,1},{3,2},{4,3},{5,4},{6,5},{7,6},{9,8},{10,9},{11,10},{12... | collective-permute-start | bytes 3145736 | tf_op jit(solution)/shard_map/ppermute | solution.py:337
  191.7 7.7 %collective-permute-done.26 = bf16[256,512]{1,0:T(8,128)(2,1)S(1)} collective-permute-done((bf16[256,512]{1,0:T(8,128)(2,1)S(1)}, bf16[256,512]{1,0:T(8,128)(2,1)S(1)}, u32[]{:S(2)}, u32[]{:S(2)}) %collective-permute-start.26) | collective-permute-done | bytes 262176 | tf_op jit(solution)/shard_map/ppermute | solution.py:379
  199.4 7.8 %collective-permute-start.27 = (bf16[1024,512]{1,0:T(8,128)(2,1)S(1)}, bf16[1024,512]{1,0:T(8,128)(2,1)S(1)}, u32[]{:S(2)}, u32[]{:S(2)}) collective-permute-start(bf16[1024,512]{1,0:T(8,128)(2,1)S(1)} %constant_dynamic-update-slice_fusion.2), channel_id=1, source_target_pairs={{0,1},{1,0},{2,3},{3,2},{4,5},{5,4},{6,7},{7,6},{8,9},{9,8},{10,11... | collective-permute-start | bytes 3145736 | tf_op jit(solution)/shard_map/ppermute | solution.py:379
  207.3 4.9 %branch_rows.1 = (bf16[1024,512]{1,0:T(8,128)(2,1)}, f32[1024,512]{1,0:T(8,128)S(1)}) custom-call(s32[1,1024]{1,0:T(1,128)S(1)} %bitcast.21, bf16[512,1024]{1,0:T(8,128)(2,1)S(1)} %copy-done.1, bf16[512,512]{1,0:T(8,128)(2,1)S(1)} %copy-done.16, bf16[4,512,256]{2,1,0:T(8,128)(2,1)S(1)} %copy-done.4, bf16[4,512,256]{2,1,0:T(8,128)(2,1)S(1)} %copy-done.5), custom_call_target="tpu_custom_call" | custom-call | flops 3221225472 | bytes 7340032 | tf_op jit(solution)/shard_map/branch_rows/pallas_call | solution.py:395
  216.2 12.4 %token_rows.1 = f32[1024,512]{1,0:T(8,128)} custom-call(s32[2]{0:T(128)} %copy-done.14, s32[2048]{0:T(1024)} %copy-done.9, s32[512]{0:T(512)} %copy-done.11, s32[1,1024]{1,0:T(1,128)} %bitcast.18, bf16[1024,512]{1,0:T(8,128)(2,1)} %bitcast.12, f32[1,512]{1,0:T(1,128)} %bitcast.16, bf16[512,1024]{1,0:T(8,128)(2,1)} %w_qk.7, bf16[512,512]{1,0:T(8,128)(2,1)} %w_v.7, ...), custom_call_target="tpu_custom_call" | custom-call | flops 3221225472 | bytes 16777216 | tf_op jit(solution)/shard_map/token_rows/pallas_call | solution.py:395
  (150 shorter events, 59.3 us)
Async XLA Ops:
  10.5 30.1 %collective-permute-start = (bf16[512,512]{1,0:T(8,128)(2,1)}, bf16[512,512]{1,0:T(8,128)(2,1)}, u32[]{:S(2)}, u32[]{:S(2)}) collective-permute-start(bf16[512,512]{1,0:T(8,128)(2,1)} %get-tuple-element.33), channel_id=1, source_target_pairs={{0,8},{8,16},{16,24},{24,32},{32,40},{40,48},{48,56},{56,64},{64,7... | collective-permute-start | bytes 1572872 | tf_op jit(solution)/shard_map/ppermute | solution.py:337
  15.6 24.9 %collective-permute-start.1 = (bf16[512,512]{1,0:T(8,128)(2,1)}, bf16[512,512]{1,0:T(8,128)(2,1)}, u32[]{:S(2)}, u32[]{:S(2)}) collective-permute-start(bf16[512,512]{1,0:T(8,128)(2,1)} %get-tuple-element.34), channel_id=1, source_target_pairs={{8,0},{16,8},{24,16},{32,24},{40,32},{48,40},{56,48},{64,56},{72,6... | collective-permute-start | bytes 1572872 | tf_op jit(solution)/shard_map/ppermute | solution.py:337
  16.9 23.7 %collective-permute-start.2 = (bf16[512,512]{1,0:T(8,128)(2,1)}, bf16[512,512]{1,0:T(8,128)(2,1)}, u32[]{:S(2)}, u32[]{:S(2)}) collective-permute-start(bf16[512,512]{1,0:T(8,128)(2,1)} %get-tuple-element.35), channel_id=1, source_target_pairs={{0,1},{1,2},{2,3},{3,4},{4,5},{5,6},{6,7},{8,9},{9,10},{10,11},{11... | collective-permute-start | bytes 1572872 | tf_op jit(solution)/shard_map/ppermute | solution.py:337
  21.0 19.6 %collective-permute-start.3 = (bf16[512,512]{1,0:T(8,128)(2,1)}, bf16[512,512]{1,0:T(8,128)(2,1)}, u32[]{:S(2)}, u32[]{:S(2)}) collective-permute-start(bf16[512,512]{1,0:T(8,128)(2,1)} %get-tuple-element.36), channel_id=1, source_target_pairs={{1,0},{2,1},{3,2},{4,3},{5,4},{6,5},{7,6},{9,8},{10,9},{11,10},{12... | collective-permute-start | bytes 1572872 | tf_op jit(solution)/shard_map/ppermute | solution.py:337
  116.4 10.0 %collective-permute-start.10 = (bf16[272,512]{1,0:T(8,128)(2,1)S(1)}, bf16[272,512]{1,0:T(8,128)(2,1)}, u32[]{:S(2)}, u32[]{:S(2)}) collective-permute-start(bf16[272,512]{1,0:T(8,128)(2,1)S(1)} %get-tuple-element.84), channel_id=1, source_target_pairs={{0,4},{1,5},{2,6},{3,7},{4,0},{5,1},{6,2},{7,3},{8,12},{9,13},{10,... | collective-permute-start | bytes 835592 | tf_op jit(solution)/shard_map/ppermute | solution.py:364
  119.5 12.9 %collective-permute-start.11 = (bf16[272,512]{1,0:T(8,128)(2,1)S(1)}, bf16[272,512]{1,0:T(8,128)(2,1)}, u32[]{:S(2)}, u32[]{:S(2)}) collective-permute-start(bf16[272,512]{1,0:T(8,128)(2,1)S(1)} %get-tuple-element.85), channel_id=1, source_target_pairs={{0,6},{1,7},{2,0},{3,1},{4,2},{5,3},{6,4},{7,5},{8,14},{9,15},{10,... | collective-permute-start | bytes 835592 | tf_op jit(solution)/shard_map/ppermute | solution.py:364
  120.3 12.4 %collective-permute-start.9 = (bf16[272,512]{1,0:T(8,128)(2,1)S(1)}, bf16[272,512]{1,0:T(8,128)(2,1)}, u32[]{:S(2)}, u32[]{:S(2)}) collective-permute-start(bf16[272,512]{1,0:T(8,128)(2,1)S(1)} %get-tuple-element.83), channel_id=1, source_target_pairs={{0,2},{1,3},{2,4},{3,5},{4,6},{5,7},{6,0},{7,1},{8,10},{9,11},{10,... | collective-permute-start | bytes 835592 | tf_op jit(solution)/shard_map/ppermute | solution.py:364
  135.6 7.7 %collective-permute-start.12 = (f32[80,512]{1,0:T(8,128)}, f32[80,512]{1,0:T(8,128)}, u32[]{:S(2)}, u32[]{:S(2)}) collective-permute-start(f32[80,512]{1,0:T(8,128)} %get-tuple-element.80), channel_id=1, source_target_pairs={{0,8},{8,16},{16,24},{24,0},{32,40},{40,48},{48,56},{56,32},{64,72... | collective-permute-start | bytes 491528 | tf_op jit(solution)/shard_map/ppermute | solution.py:364
  138.0 9.7 %collective-permute-start.13 = (f32[80,512]{1,0:T(8,128)S(1)}, f32[80,512]{1,0:T(8,128)}, u32[]{:S(2)}, u32[]{:S(2)}) collective-permute-start(f32[80,512]{1,0:T(8,128)S(1)} %get-tuple-element.81), channel_id=1, source_target_pairs={{0,16},{8,24},{16,0},{24,8},{32,48},{40,56},{48,32},{56,40},{64,80... | collective-permute-start | bytes 491528 | tf_op jit(solution)/shard_map/ppermute | solution.py:364
  140.5 7.1 %collective-permute-start.14 = (f32[80,512]{1,0:T(8,128)S(1)}, f32[80,512]{1,0:T(8,128)}, u32[]{:S(2)}, u32[]{:S(2)}) collective-permute-start(f32[80,512]{1,0:T(8,128)S(1)} %get-tuple-element.82), channel_id=1, source_target_pairs={{0,24},{8,0},{16,8},{24,16},{32,56},{40,32},{48,40},{56,48},{64,88... | collective-permute-start | bytes 491528 | tf_op jit(solution)/shard_map/ppermute | solution.py:364
  149.6 5.0 %collective-permute-start.15 = (f32[32,512]{1,0:T(8,128)S(1)}, f32[32,512]{1,0:T(8,128)S(1)}, u32[]{:S(2)}, u32[]{:S(2)}) collective-permute-start(f32[32,512]{1,0:T(8,128)S(1)} %get-tuple-element.77), channel_id=1, source_target_pairs={{0,32},{8,40},{16,48},{24,56},{32,64},{40,72},{48,80},{56,88},{64,... | collective-permute-start | bytes 196616 | tf_op jit(solution)/shard_map/ppermute | solution.py:364
  150.8 5.6 %collective-permute-start.16 = (f32[32,512]{1,0:T(8,128)S(1)}, f32[32,512]{1,0:T(8,128)S(1)}, u32[]{:S(2)}, u32[]{:S(2)}) collective-permute-start(f32[32,512]{1,0:T(8,128)S(1)} %get-tuple-element.78), channel_id=1, source_target_pairs={{0,64},{8,72},{16,80},{24,88},{32,96},{40,104},{48,112},{56,120},{... | collective-permute-start | bytes 196616 | tf_op jit(solution)/shard_map/ppermute | solution.py:364
  157.6 3.9 %collective-permute-start.18 = (bf16[16,512]{1,0:T(8,128)(2,1)S(1)}, bf16[16,512]{1,0:T(8,128)(2,1)S(1)}, u32[]{:S(2)}, u32[]{:S(2)}) collective-permute-start(bf16[16,512]{1,0:T(8,128)(2,1)S(1)} %get-tuple-element.61), channel_id=1, source_target_pairs={{0,32},{8,40},{16,48},{24,56},{32,64},{40,72},{48,80},{56,88},{64,... | collective-permute-start | bytes 49160 | tf_op jit(solution)/shard_map/ppermute | solution.py:379
  157.7 4.2 %collective-permute-start.19 = (bf16[16,512]{1,0:T(8,128)(2,1)S(1)}, bf16[16,512]{1,0:T(8,128)(2,1)S(1)}, u32[]{:S(2)}, u32[]{:S(2)}) collective-permute-start(bf16[16,512]{1,0:T(8,128)(2,1)S(1)} %get-tuple-element.61), channel_id=1, source_target_pairs={{0,64},{8,72},{16,80},{24,88},{32,96},{40,104},{48,112},{56,120},{... | collective-permute-start | bytes 49160 | tf_op jit(solution)/shard_map/ppermute | solution.py:379
  162.7 5.5 %collective-permute-start.21 = (bf16[64,512]{1,0:T(8,128)(2,1)S(1)}, bf16[64,512]{1,0:T(8,128)(2,1)S(1)}, u32[]{:S(2)}, u32[]{:S(2)}) collective-permute-start(bf16[64,512]{1,0:T(8,128)(2,1)S(1)} %constant_dynamic-update-slice_fusion.10), channel_id=1, source_target_pairs={{0,8},{8,16},{16,24},{24,0},{32,40},{40,48},{48,56},{56,32},{64,72... | collective-permute-start | bytes 196616 | tf_op jit(solution)/shard_map/ppermute | solution.py:379
  165.2 4.9 %collective-permute-start.22 = (bf16[64,512]{1,0:T(8,128)(2,1)S(1)}, bf16[64,512]{1,0:T(8,128)(2,1)S(1)}, u32[]{:S(2)}, u32[]{:S(2)}) collective-permute-start(bf16[64,512]{1,0:T(8,128)(2,1)S(1)} %constant_dynamic-update-slice_fusion.10), channel_id=1, source_target_pairs={{0,16},{8,24},{16,0},{24,8},{32,48},{40,56},{48,32},{56,40},{64,80... | collective-permute-start | bytes 196616 | tf_op jit(solution)/shard_map/ppermute | solution.py:379
  170.8 18.2 %collective-permute-start.24 = (bf16[256,512]{1,0:T(8,128)(2,1)S(1)}, bf16[256,512]{1,0:T(8,128)(2,1)S(1)}, u32[]{:S(2)}, u32[]{:S(2)}) collective-permute-start(bf16[256,512]{1,0:T(8,128)(2,1)S(1)} %constant_dynamic-update-slice_fusion.6), channel_id=1, source_target_pairs={{0,2},{1,3},{2,4},{3,5},{4,6},{5,7},{6,0},{7,1},{8,10},{9,11},{10,... | collective-permute-start | bytes 786440 | tf_op jit(solution)/shard_map/ppermute | solution.py:379
  172.6 18.3 %collective-permute-start.25 = (bf16[256,512]{1,0:T(8,128)(2,1)S(1)}, bf16[256,512]{1,0:T(8,128)(2,1)S(1)}, u32[]{:S(2)}, u32[]{:S(2)}) collective-permute-start(bf16[256,512]{1,0:T(8,128)(2,1)S(1)} %constant_dynamic-update-slice_fusion.6), channel_id=1, source_target_pairs={{0,4},{1,5},{2,6},{3,7},{4,0},{5,1},{6,2},{7,3},{8,12},{9,13},{10,... | collective-permute-start | bytes 786440 | tf_op jit(solution)/shard_map/ppermute | solution.py:379
  175.3 38.2 %collective-permute-start.4 = (bf16[2,2,4,256,128]{4,3,2,1,0:T(8,128)(2,1)}, bf16[2,2,4,256,128]{4,3,2,1,0:T(8,128)(2,1)S(1)}, u32[]{:S(2)}, u32[]{:S(2)}) collective-permute-start(bf16[2,2,4,256,128]{4,3,2,1,0:T(8,128)(2,1)} %get-tuple-element.51.h0), channel_id=1, source_target_pairs={{8,0},{16,8},{24,16},{32,24},{40,32},{48,40},{56,48},{64,56},{72,6... | collective-permute-start | bytes 3145736 | tf_op jit(solution)/shard_map/ppermute | solution.py:337
  176.6 36.9 %collective-permute-start.5 = (bf16[2,2,4,256,128]{4,3,2,1,0:T(8,128)(2,1)}, bf16[2,2,4,256,128]{4,3,2,1,0:T(8,128)(2,1)S(1)}, u32[]{:S(2)}, u32[]{:S(2)}) collective-permute-start(bf16[2,2,4,256,128]{4,3,2,1,0:T(8,128)(2,1)} %get-tuple-element.52.h1), channel_id=1, source_target_pairs={{0,8},{8,16},{16,24},{24,32},{32,40},{40,48},{48,56},{56,64},{64,7... | collective-permute-start | bytes 3145736 | tf_op jit(solution)/shard_map/ppermute | solution.py:337
  180.6 32.9 %collective-permute-start.6 = (bf16[2,2,4,256,128]{4,3,2,1,0:T(8,128)(2,1)S(1)}, bf16[2,2,4,256,128]{4,3,2,1,0:T(8,128)(2,1)S(1)}, u32[]{:S(2)}, u32[]{:S(2)}) collective-permute-start(bf16[2,2,4,256,128]{4,3,2,1,0:T(8,128)(2,1)S(1)} %copy-done.28), channel_id=1, source_target_pairs={{1,0},{2,1},{3,2},{4,3},{5,4},{6,5},{7,6},{9,8},{10,9},{11,10},{12... | collective-permute-start | bytes 3145736 | tf_op jit(solution)/shard_map/ppermute | solution.py:337
  189.0 24.5 %collective-permute-start.7 = (bf16[2,2,4,256,128]{4,3,2,1,0:T(8,128)(2,1)S(1)}, bf16[2,2,4,256,128]{4,3,2,1,0:T(8,128)(2,1)S(1)}, u32[]{:S(2)}, u32[]{:S(2)}) collective-permute-start(bf16[2,2,4,256,128]{4,3,2,1,0:T(8,128)(2,1)S(1)} %copy-done.27), channel_id=1, source_target_pairs={{0,1},{1,2},{2,3},{3,4},{4,5},{5,6},{6,7},{8,9},{9,10},{10,11},{11... | collective-permute-start | bytes 3145736 | tf_op jit(solution)/shard_map/ppermute | solution.py:337
  190.9 8.5 %collective-permute-start.26 = (bf16[256,512]{1,0:T(8,128)(2,1)S(1)}, bf16[256,512]{1,0:T(8,128)(2,1)S(1)}, u32[]{:S(2)}, u32[]{:S(2)}) collective-permute-start(bf16[256,512]{1,0:T(8,128)(2,1)S(1)} %constant_dynamic-update-slice_fusion.6), channel_id=1, source_target_pairs={{0,6},{1,7},{2,0},{3,1},{4,2},{5,3},{6,4},{7,5},{8,14},{9,15},{10,... | collective-permute-start | bytes 786440 | tf_op jit(solution)/shard_map/ppermute | solution.py:379
  199.4 30.0 %collective-permute-start.27 = (bf16[1024,512]{1,0:T(8,128)(2,1)S(1)}, bf16[1024,512]{1,0:T(8,128)(2,1)S(1)}, u32[]{:S(2)}, u32[]{:S(2)}) collective-permute-start(bf16[1024,512]{1,0:T(8,128)(2,1)S(1)} %constant_dynamic-update-slice_fusion.2), channel_id=1, source_target_pairs={{0,1},{1,0},{2,3},{3,2},{4,5},{5,4},{6,7},{7,6},{8,9},{9,8},{10,11... | collective-permute-start | bytes 3145736 | tf_op jit(solution)/shard_map/ppermute | solution.py:379
  (37 other events, 459.9 us)

commit v2 on v1

v2 whole, which is shorter than its diff:
```python
import functools

import jax
import jax.numpy as jnp
from jax import lax
from jax.experimental import pallas as pl
from jax.experimental.pallas import tpu as pltpu
from jax.sharding import PartitionSpec as P

BLK = 256
PAIR = 128
EPSILON = 1e-06
BF = jnp.bfloat16
F32 = jnp.float32
MIB = 1 << 20
LIMIT = 58
VM = pl.BlockSpec(memory_space=pltpu.VMEM)
SM = pl.BlockSpec(memory_space=pltpu.SMEM)
AN = pl.BlockSpec(memory_space=pl.ANY)
NT = (((1,), (1,)), ((), ()))


def mm(a, b):
    return jnp.dot(a, b, preferred_element_type=F32)


def mm_nt(a, b):
    return lax.dot_general(a, b, NT, preferred_element_type=F32)


def rms(rows):
    values = rows.astype(F32)
    inv = lax.rsqrt(jnp.mean(values * values, axis=-1, keepdims=True) + EPSILON)
    return values, inv


def named_mask(ids, cnt, reader, owner, blocks, slots):
    mask = jnp.int32(0)
    for b in range(blocks):
        count = cnt[reader * blocks + b]
        for j in range(slots):
            entry = ids[(reader * blocks + b) * slots + j]
            hit = jnp.logical_and(j < count, lax.div(entry, blocks) == owner)
            mask = mask | jnp.where(hit, jnp.left_shift(1, lax.rem(entry, blocks)), 0)
    return mask


def first_two(mask, blocks):
    def lowest(m):
        at = jnp.int32(blocks - 1)
        for b in range(blocks - 2, -1, -1):
            at = jnp.where((m & (1 << b)) != 0, b, at)
        return at

    first = lowest(mask)
    return first, lowest(mask & ~jnp.left_shift(1, first))


def send_table(ids, cnt, pos, extent_x, extent_y, blocks, slots):
    x, y = pos[0], pos[1]
    me = x * extent_y + y
    readers = (
        jnp.minimum(x + 1, extent_x - 1) * extent_y + y,
        jnp.maximum(x - 1, 0) * extent_y + y,
        x * extent_y + jnp.minimum(y + 1, extent_y - 1),
        x * extent_y + jnp.maximum(y - 1, 0),
    )
    return [first_two(named_mask(ids, cnt, r, me, blocks, slots), blocks) for r in readers]


def pool_table(ids, cnt, pos, extent_y, blocks, slots):
    me = pos[0] * extent_y + pos[1]
    owners = (me - extent_y, me + extent_y, me - 1, me + 1)
    masks = [named_mask(ids, cnt, me, o, blocks, slots) for o in owners]
    table = []
    for b in range(blocks):
        row = []
        for j in range(slots):
            entry = ids[(me * blocks + b) * slots + j]
            owner, off = lax.div(entry, blocks), lax.rem(entry, blocks)
            at = off
            for seg, (o, mask) in enumerate(zip(owners, masks)):
                below = mask & (jnp.left_shift(1, off) - 1)
                at = jnp.where(owner == o, blocks + 2 * seg + jnp.where(below != 0, 1, 0), at)
            live = j < cnt[me * blocks + b]
            row.append((jnp.where(live, at, b), live))
        table.append(row)
    return table


def order_columns(order_ref):
    n = order_ref.shape[1]
    return jnp.broadcast_to(order_ref[...], (128, n)).T


def one_hot_rows(cols, n):
    lane = lax.broadcasted_iota(jnp.int32, cols.shape, 1)
    return jnp.concatenate(
        [(cols == lane + c).astype(F32).astype(BF) for c in range(0, n, 128)], axis=1
    )


def one_hot_back(order_ref, start, rows):
    n = order_ref.shape[1]
    row = lax.broadcasted_iota(jnp.int32, (rows, n), 0) + start
    return (row == order_ref[...]).astype(F32).astype(BF)


def sort_kernel(dims, pos, ids, cnt, order, tok, out, s0, s1, s2, s3, cols):
    extent_x, extent_y, blocks, slots = dims
    n = tok.shape[0]
    cols[...] = order_columns(order)

    def body(b, _):
        rows = pl.ds(pl.multiple_of(b * BLK, BLK), BLK)
        out[rows, :] = mm(one_hot_rows(cols[rows, :], n), tok[...]).astype(BF)
        return 0

    lax.fori_loop(0, n // BLK, body, 0)
    table = send_table(ids, cnt, pos, extent_x, extent_y, blocks, slots)
    for ref, pair in zip((s0, s1, s2, s3), table):
        for k, b in enumerate(pair):
            ref[k * BLK : (k + 1) * BLK, :] = out[pl.ds(pl.multiple_of(b * BLK, BLK), BLK), :]


def project_kernel(np_, order, tok, cot, gain, w_qk, w_v, w_out, sc, n_t, *rest):
    *outs, cols = rest
    n, d = cot.shape
    b = pl.program_id(0)

    @pl.when(b == 0)
    def _():
        cols[...] = order_columns(order)

    rows = pl.ds(pl.multiple_of(b * BLK, BLK), BLK)
    grad = mm(one_hot_rows(cols[rows, :], n), cot[...]).astype(BF)
    sc[0] = grad
    values, inv = rms(tok[...])
    normed = (values * inv * gain[...]).astype(BF)
    n_t[0] = normed.T
    query = (mm(normed, w_qk[:, :d]).astype(BF)) * BF(0.125)
    key = mm(normed, w_qk[:, d:]).astype(BF)
    value = mm(normed, w_v[...]).astype(BF)
    dctx = mm_nt(grad, w_out[...]).astype(BF)
    for at, mat in enumerate((query, key, value, dctx)):
        mat_t = mat.T
        for p in range(np_):
            outs[2 * at][0, p] = mat[:, p * PAIR : (p + 1) * PAIR]
            outs[2 * at + 1][0, p] = mat_t[p * PAIR : (p + 1) * PAIR, :]


def attend_kernel(dims, np_, pos, ids, cnt, gain, r0, r1, r2, r3, w_qk_in, w_v_in,
                  qn_in, qt_in, kn_in, kt_in, vn_in, vt_in, gn_in, gt_in, sc_in, nt_in,
                  ctx_out, dq_out, own, h0, h1, h2, h3, keep, send, gain_out,
                  far, w_qk, w_v, qn, qt, gn, gt, pkn, pkt, pvn, pvt, sc, n_t, ctx_t, dq_t, acc,
                  s_scr, dp_scr, p_scr, ds_scr, terms, where_ref, sem_in, sem_out):
    extent_x, extent_y, blocks, slots = dims
    d = w_v.shape[0]
    mine = pl.ds(0, blocks)
    first, later = [], []

    def fetch(src, dst, into):
        copy = pltpu.make_async_copy(src, dst, sem_in.at[len(first) + len(later)])
        copy.start()
        into.append(copy)

    fetch(w_qk_in, w_qk, first)
    fetch(w_v_in, w_v, first)
    for seg, ref in enumerate((r0, r1, r2, r3)):
        fetch(ref, far.at[seg], first)
    for src, dst in ((kn_in, pkn.at[mine]), (kt_in, pkt.at[mine]), (vn_in, pvn.at[mine]),
                     (vt_in, pvt.at[mine]), (qt_in, qt), (gt_in, gt), (qn_in, qn), (gn_in, gn),
                     (nt_in, n_t.at[mine]), (sc_in, sc)):
        fetch(src, dst, later)
    table = pool_table(ids, cnt, pos, extent_y, blocks, slots)
    for b in range(blocks):
        for j in range(slots):
            where_ref[b * slots + j] = table[b][j][0]
    acc[...] = jnp.zeros_like(acc)
    for copy in first:
        copy.wait()

    def remote(i, _):
        rows = pl.ds(pl.multiple_of(lax.rem(i, 2) * BLK, BLK), BLK)
        values, inv = rms(far[lax.div(i, 2), rows, :])
        normed = (values * inv * gain[...]).astype(BF)
        n_t[blocks + i] = normed.T
        made = mm(normed, w_qk[:, d:]).astype(BF)
        made_v = mm(normed, w_v[...]).astype(BF)
        for mat, nat, tra in ((made, pkn, pkt), (made_v, pvn, pvt)):
            mat_t = mat.T
            for p in range(np_):
                nat[blocks + i, p] = mat[:, p * PAIR : (p + 1) * PAIR]
                tra[blocks + i, p] = mat_t[p * PAIR : (p + 1) * PAIR, :]
        return 0

    lax.fori_loop(0, 8, remote, 0)
    for copy in later:
        copy.wait()
    lane = lax.broadcasted_iota(jnp.int32, (1, PAIR), 1)
    low_lanes = (lane < PAIR // 2).astype(F32).astype(BF)
    high_lanes = (lane >= PAIR // 2).astype(F32).astype(BF)
    half = PAIR // 2

    def diagonal(mat):
        zero = jnp.zeros((half, BLK), BF)
        return jnp.concatenate(
            [jnp.concatenate([mat[:half], zero], axis=1), jnp.concatenate([zero, mat[half:]], axis=1)],
            axis=0,
        )

    def pair(b, p, at):
        q_diag, g_diag = diagonal(qt[b, p]), diagonal(gt[b, p])
        top = None
        for j, k in enumerate(at):
            s = mm(pkn[k, p], q_diag)
            s_scr[j] = s
            m = jnp.max(s, axis=0, keepdims=True)
            top = m if top is None else jnp.maximum(top, m)
        total = jnp.zeros((1, 2 * BLK), F32)
        centre = jnp.zeros((1, 2 * BLK), F32)
        for j, k in enumerate(at):
            e = jnp.exp(s_scr[j] - top)
            s_scr[j] = e
            total += jnp.sum(e, axis=0, keepdims=True)
            dp = mm(pvn[k, p], g_diag)
            dp_scr[j] = dp
            centre += jnp.sum(e * dp, axis=0, keepdims=True)
        scale = 1.0 / total
        centre = centre * scale
        for j in range(len(at)):
            prob = s_scr[j] * scale
            p_scr[j] = prob.astype(BF)
            ds_scr[j] = (prob * (dp_scr[j] - centre)).astype(BF)
        q_rows = qn[b, p]
        g_rows = gn[b, p]
        q_mask = jnp.concatenate([q_rows * low_lanes, q_rows * high_lanes], axis=0)
        g_mask = jnp.concatenate([g_rows * low_lanes, g_rows * high_lanes], axis=0)
        for h in range(2):
            feats, lanes = slice(h * half, (h + 1) * half), slice(h * BLK, (h + 1) * BLK)
            ctx = dq = None
            for j, k in enumerate(at):
                c = mm(pvt[k, p, feats, :], p_scr[j, :, lanes])
                t = mm(pkt[k, p, feats, :], ds_scr[j, :, lanes])
                ctx = c if ctx is None else ctx + c
                dq = t if dq is None else dq + t
            rows = pl.ds(pl.multiple_of(p * PAIR + h * half, half), half)
            ctx_t[b, rows, :] = ctx.astype(BF)
            dq_t[b, rows, :] = (dq * 0.125).astype(BF)
        for j, k in enumerate(at):
            acc[k, 0, p] += mm(ds_scr[j], q_mask)
            acc[k, 1, p] += mm(p_scr[j], g_mask)

    me = pos[0] * extent_y + pos[1]

    def block(b, _):
        count = cnt[me * blocks + b]
        for live in range(1, slots + 1):

            @pl.when(count == live)
            def _():
                at = [b] + [where_ref[b * slots + j] for j in range(live)]
                lax.fori_loop(0, np_, lambda p, c: (pair(b, p, at), c)[1], 0)

        return 0

    lax.fori_loop(0, blocks, block, 0)
    out = []

    def ship(src, dst):
        copy = pltpu.make_async_copy(src, dst, sem_out.at[len(out)])
        copy.start()
        out.append(copy)

    ship(ctx_t, ctx_out)
    ship(dq_t, dq_out)
    ship(acc.at[mine], own)

    def lower(b, _):
        for p in range(np_):
            pkn[b, p] = acc[b, 0, p].astype(BF)
            pvn[b, p] = acc[b, 1, p].astype(BF)
        return 0

    lax.fori_loop(0, blocks + 8, lower, 0)
    for seg, ref in enumerate((h0, h1, h2, h3)):
        part = pl.ds(blocks + 2 * seg, 2)
        ship(pkn.at[part], ref.at[0])
        ship(pvn.at[part], ref.at[1])
    core = lax.rem(pos[1], 2)
    total = jnp.zeros((d, 1), F32)

    def place(i, value):
        terms[lax.rem(i + core, 2), (i // 2) * BLK : (i // 2 + 1) * BLK, :] = value.astype(BF)

    g_q = g_o = None
    for b in range(blocks):
        a, c = mm_nt(n_t[b], dq_t[b]), mm(ctx_t[b], sc[b])
        g_q = a if g_q is None else g_q + a
        g_o = c if g_o is None else g_o + c
    for i, g in ((0, g_q), (6, g_o)):
        place(i, g[:BLK])
        place(i + 1, g[BLK:])
    total += jnp.sum(g_q * w_qk[:, :d].astype(F32), axis=1, keepdims=True)
    for i, pool, w, lo in ((2, pkn, w_qk, d), (4, pvn, w_v, 0)):
        made = []
        for p in range(0, np_, 2):
            g = None
            for b in range(blocks + 8):
                t = mm(n_t[b], jnp.concatenate([pool[b, p], pool[b, p + 1]], axis=1))
                g = t if g is None else g + t
            at = lo + p * PAIR
            total += jnp.sum(g * w[:, at : at + 2 * PAIR].astype(F32), axis=1, keepdims=True)
            made.append(g)
        g = jnp.concatenate(made, axis=1)
        place(i, g[:BLK])
        place(i + 1, g[BLK:])
    gain_term = jnp.broadcast_to(total, (d, 128)).T[:8] / gain[...]
    gain_out[...] = gain_term
    terms[:, blocks * BLK :, :] = jnp.broadcast_to(gain_term[:1].astype(BF)[None], (2, 16, d))
    ship(terms.at[0, pl.ds(0, blocks * BLK)], keep)
    ship(terms.at[1], send)
    for copy in out:
        copy.wait()


def core_kernel(pos, keep, got, gain, own, s1, s2, s3, gain_out):
    size, d = own.shape
    rows = 4 * size
    total = gain[:1] + got[rows : rows + 1, :].astype(F32)
    gain_out[...] = jnp.broadcast_to(total, gain_out.shape)
    y = lax.div(pos[1], 2)
    for s, ref in enumerate((own, s1, s2, s3)):
        at = pl.ds(pl.multiple_of(lax.rem(y + s, 4) * size, size), size)
        value = keep[at, :].astype(F32) + got[at, :].astype(F32)
        if s:
            ref[:size, :] = value.astype(BF)
            ref[size:, :] = jnp.broadcast_to(total, (ref.shape[0] - size, d)).astype(BF)
        else:
            ref[...] = value


def output_kernel(order, w_qk, w_out, ctx_t, dq_t, out, part):
    blocks, d = ctx_t.shape[0], w_out.shape[0]

    def body(a, _):
        rows = pl.ds(pl.multiple_of(a * BLK, BLK), BLK)
        back = one_hot_back(order, a * BLK, BLK)
        made = []
        for ref in (ctx_t, dq_t):
            total = None
            for b in range(blocks):
                t = mm_nt(back[:, b * BLK : (b + 1) * BLK], ref[b])
                total = t if total is None else total + t
            made.append(total.astype(BF))
        out[rows, :] = mm(made[0], w_out[...]).astype(BF)
        part[rows, :] = mm_nt(made[1], w_qk[:, :d])
        return 0

    lax.fori_loop(0, out.shape[0] // BLK, body, 0)


def rows_kernel(dims, np_, pos, ids, cnt, order, tok, gain, w_qk, w_v, part, own, b0, b1, b2, b3,
                out, acc, rows_scr):
    extent_x, extent_y, blocks, slots = dims
    d = w_v.shape[0]
    acc[...] = own[...]
    table = send_table(ids, cnt, pos, extent_x, extent_y, blocks, slots)
    for ref, pair in zip((b0, b1, b2, b3), table):
        for k, b in enumerate(pair):
            acc[b, 0] += ref[0, k].astype(F32)
            acc[b, 1] += ref[1, k].astype(F32)
    for half in range(2):
        for p in range(np_):
            lo = half * d + p * PAIR
            for b in range(blocks):
                rows_scr[b * BLK : (b + 1) * BLK, lo : lo + PAIR] = acc[b, half, p].astype(BF)

    def body(a, _):
        rows = pl.ds(pl.multiple_of(a * BLK, BLK), BLK)
        back = one_hot_back(order, a * BLK, BLK)
        mine = mm(back, rows_scr[...]).astype(BF)
        grad = part[rows, :] + mm_nt(mine[:, :d], w_qk[:, d:]) + mm_nt(mine[:, d:], w_v[...])
        values, inv = rms(tok[rows, :])
        u = grad * gain[...]
        mean = jnp.mean(values * u, axis=-1, keepdims=True)
        out[rows, :] = inv * u - values * (inv * inv * inv * mean)
        return 0

    lax.fori_loop(0, out.shape[0] // BLK, body, 0)


def place_kernel(rows, qk, v, o):
    d = v.shape[0]
    qk[:, :d] = rows[:d, :].astype(F32)
    qk[:, d:] = rows[d : 2 * d, :].astype(F32)
    v[...] = rows[2 * d : 3 * d, :].astype(F32)
    o[...] = rows[3 * d :, :].astype(F32)


def step_to(block, axis, distance):
    n = lax.axis_size(axis)
    route = [(i, i + distance) for i in range(n) if 0 <= i + distance < n]
    return lax.ppermute(block, axis, route)


def across_x(rows, gain):
    count = lax.axis_size("bx")
    size = rows.shape[0] // count
    extra = jnp.zeros((size, 128), F32).at[: gain.shape[1] // 128].set(gain.reshape(-1, 128))
    extra = jnp.broadcast_to(extra[None], (count, size, 128))
    parts = jnp.concatenate([rows.reshape(count, size, -1), extra], axis=2).astype(BF)
    got = lax.all_to_all(parts, "bx", 0, 0, tiled=True)
    total = jnp.sum(got.astype(F32), axis=0)
    gain = total[: gain.shape[1] // 128, rows.shape[1] :].reshape(1, -1)
    mine = total[:, : rows.shape[1]].astype(BF)
    back = lax.all_to_all(jnp.broadcast_to(mine[None], (count,) + mine.shape), "bx", 0, 0, tiled=True)
    return back.reshape(rows.shape), gain


def call(kernel, name, outs, ins, specs, scratch, limit, flops, moved, exps=0, out_specs=None, grid=()):
    return pl.pallas_call(
        kernel,
        out_shape=outs,
        grid=grid,
        in_specs=specs,
        out_specs=jax.tree.map(lambda _: VM, outs) if out_specs is None else out_specs,
        scratch_shapes=scratch,
        compiler_params=pltpu.CompilerParams(vmem_limit_bytes=limit * MIB),
        cost_estimate=pl.CostEstimate(flops=flops, bytes_accessed=moved, transcendentals=exps),
        name=name,
    )(*ins)


def shards(tokens, norm_gain, w_query_key, w_value, w_out, cotangent, block_order,
           neighbour_ids, neighbour_count):
    n, d = tokens.shape[2:]
    extent_x, extent_y, blocks, slots = neighbour_ids.shape
    dims = (extent_x, extent_y, blocks, slots)
    np_ = d // PAIR
    tok, cot = tokens[0, 0], cotangent[0, 0]
    order = block_order[0]
    gain = norm_gain[None, :]
    ids = neighbour_ids.reshape(-1)
    cnt = neighbour_count.reshape(-1)
    pos = jnp.stack([lax.axis_index("bx"), lax.axis_index("by")]).astype(jnp.int32)
    shape = jax.ShapeDtypeStruct

    sends = [shape((2 * BLK, d), BF)] * 4
    sorted_rows, *sent = call(
        functools.partial(sort_kernel, dims), "sort_rows",
        [shape((n, d), BF)] + sends, (pos, ids, cnt, order, tok), [SM, SM, SM, VM, VM],
        [pltpu.VMEM((n, 128), jnp.int32)], 32, 2 * n * n * d, 4 << 20,
    )
    arrived = [
        step_to(sent[0], "bx", 1), step_to(sent[1], "bx", -1),
        step_to(sent[2], "by", 1), step_to(sent[3], "by", -1),
    ]
    nat, tra = (blocks, np_, BLK, PAIR), (blocks, np_, PAIR, BLK)

    def a_block(dims_):
        return pl.BlockSpec((1,) + dims_[1:], lambda b: (b,) + (0,) * (len(dims_) - 1))

    whole = pl.BlockSpec(memory_space=pltpu.VMEM)
    out_dims = [(blocks, BLK, d), (blocks, d, BLK)] + [nat, tra] * 4
    sc, n_t, *made = call(
        functools.partial(project_kernel, np_), "project", [shape(k, BF) for k in out_dims],
        (order, sorted_rows, cot, gain, w_query_key, w_value, w_out),
        [whole, pl.BlockSpec((BLK, d), lambda b: (b, 0))] + [whole] * 5,
        [pltpu.VMEM((n, 128), jnp.int32)], LIMIT, 2 * n * n * d + 8 * n * d * d, 14 << 20,
        out_specs=[a_block(k) for k in out_dims], grid=(blocks,),
    )
    pool = blocks + 8
    tile = (slots + 1, BLK, 2 * BLK)
    vmem = pltpu.VMEM
    ins = (pos, ids, cnt, gain, *arrived, w_query_key, w_value, *made, sc, n_t)
    ctx_t, dq_t, own, *back, keep, send, gain_term = call(
        functools.partial(attend_kernel, dims, np_), "attend",
        [shape((blocks, d, BLK), BF)] * 2 + [shape((blocks, 2, np_, BLK, PAIR), F32)]
        + [shape((2, 2, np_, BLK, PAIR), BF)] * 4
        + [shape((n, d), BF), shape((n + 16, d), BF), shape((8, d), F32)],
        ins, [SM] * 3 + [VM] + [AN] * (len(ins) - 4),
        [vmem((4, 2 * BLK, d), BF), vmem((d, 2 * d), BF), vmem((d, d), BF)]
        + [vmem(nat, BF), vmem(tra, BF)] * 2
        + [vmem((pool,) + nat[1:], BF), vmem((pool,) + tra[1:], BF)] * 2
        + [vmem((blocks, BLK, d), BF), vmem((pool, d, BLK), BF)] + [vmem((blocks, d, BLK), BF)] * 2
        + [vmem((pool, 2) + nat[1:], F32), vmem(tile, F32), vmem(tile, F32), vmem(tile, BF), vmem(tile, BF),
           vmem((2, n + 16, d), BF), pltpu.SMEM((blocks * slots,), jnp.int32),
           pltpu.SemaphoreType.DMA((16,)), pltpu.SemaphoreType.DMA((13,))],
        LIMIT, 12 * blocks * 5 * BLK * BLK * d, 24 << 20, blocks * 5 * BLK * BLK * 8,
        out_specs=[AN] * 9 + [VM],
    )
    h0, h1, h2, h3 = back
    cores = lax.ppermute(send, "by", [(i, i ^ 1) for i in range(extent_y)])
    returned = [
        step_to(h0, "bx", -1), step_to(h1, "bx", 1), step_to(h2, "by", -1), step_to(h3, "by", 1),
    ]
    mine, *cut, gain_sum = call(
        core_kernel, "add_cores",
        [shape((BLK, d), F32)] + [shape((BLK + 16, d), BF)] * 3 + [shape((8, d), F32)],
        (pos, keep, cores, gain_term), [SM, VM, VM, VM], [], 32, 0, 4 << 20,
    )
    count = extent_y // 2
    got = [
        lax.ppermute(cut[s - 1], "by", [(i, (i + 2 * s) % extent_y) for i in range(extent_y)])
        for s in range(1, count)
    ]
    branch_out, part = call(
        output_kernel, "branch_rows", [shape((n, d), BF), shape((n, d), F32)],
        (order, w_query_key, w_out, ctx_t, dq_t), [VM] * 5, [], 40,
        4 * n * n * d + 4 * n * d * d, 7 << 20,
    )
    rows, gain_sum = mine, gain_sum[:1]
    for g in got:
        rows = rows + g[:BLK].astype(F32)
        gain_sum = gain_sum + g[BLK : BLK + 1].astype(F32)
    rows, gain_sum, part, branch_out, *returned = lax.optimization_barrier(
        (rows, gain_sum, part, branch_out, *returned)
    )
    rows, gain_sum = across_x(rows, gain_sum)
    rows, part = lax.optimization_barrier((rows, part))
    rows = lax.all_gather(rows, "by", axis=0, tiled=True)

    b_x1, b_xm, b_y1, b_ym = returned
    grad_rows = call(
        functools.partial(rows_kernel, dims, np_), "token_rows", shape((n, d), F32),
        (pos, ids, cnt, order, tok, gain, w_query_key, w_value, part, own, b_x1, b_xm, b_y1, b_ym),
        [SM] * 3 + [VM] * 11,
        [pltpu.VMEM((blocks, 2, np_, BLK, PAIR), F32), pltpu.VMEM((n, 2 * d), BF)],
        56, 4 * n * n * d + 4 * n * d * d, 16 << 20,
    )
    grad_qk, grad_v, grad_o = call(
        place_kernel, "weight_grads", [shape((d, 2 * d), F32), shape((d, d), F32), shape((d, d), F32)],
        (rows,), [VM], [], 32, 0, 6 << 20,
    )
    return (branch_out[None, None], grad_rows[None, None], grad_qk, grad_v, grad_o, gain_sum[0])


def solution(mesh):
    local = P("bx", "by", None, None)
    placed = (local, P(), P(), P(), P(), local, P("bx", "by", None), P(), P())
    return jax.shard_map(
        shards,
        mesh=mesh,
        in_specs=placed,
        out_specs=(local, local, P(), P(), P(), P()),
        check_vma=False,
    )
```

time: 234 us -> 196 us (0.84)
  starting transfers between devices: 64.6 us -> 31.8 us
  blocking collectives: 0 us -> 30.8 us
  local copies, waits for them, and re-layouts: 25.7 us -> 11.6 us
  between operations: 1.19 us -> 14.4 us
  Pallas kernels: 95.2 us -> 82.6 us
  waiting for transfers between devices: 36.5 us -> 24.2 us
  other arithmetic: 9.56 us -> 0.3 us
    ppermute x20 -> x4, waiting for transfers between devices: 36.5 us -> 5.67 us  [the longest x3 3.15 us: shards(): lax.ppermute(cut[s - 1], 'by', [(i, (i + 2 * s) % extent_y) for i in rang...]
    all_to_all x0 -> x2, blocking collectives: none -> 30.8 us  [the longest x1 19.9 us: across_x(): got = lax.all_to_all(parts, 'bx', 0, 0, tiled=True)]
    ppermute x20 -> x4, starting transfers between devices: 36.6 us -> 5.87 us  [the longest x3 5.02 us: shards(): lax.ppermute(cut[s - 1], 'by', [(i, (i + 2 * s) % extent_y) for i in rang...]
    all_gather x0 -> x1, waiting for transfers between devices: none -> 13.9 us  [shards(): rows = lax.all_gather(rows, 'by', axis=0, tiled=True)]
    pallas_call x6 -> x7, Pallas kernels: 95.2 us -> 82.6 us  [call(): pl.pallas_call(kernel, out_shape=outs, grid=grid, in_specs=specs, out_spe...]
    unnamed x68 -> x50, local copies, waits for them, and re-layouts: 20 us -> 10.6 us
    add x6 -> x2, other arithmetic: 6.41 us -> 0.15 us  [the longest x1 0.14 us: shards(): rows = rows + g[:BLK].astype(F32)]
    ppermute x8, waiting for transfers between devices: 0.02 us -> 4.67 us  [step_to(): return lax.ppermute(block, axis, route)]
  transfers between devices with their start and end apart: 28 -> 13, of which waited for: 16 -> 6; matrix products, arithmetic and copies ran while one was open for 1% -> 0% of each run, Pallas kernels for 10% -> 13%
where the time goes in v2:
time: 196 us
  Pallas kernels  82.6 us (42%)
  starting transfers between devices  31.8 us (16%)
  blocking collectives  30.8 us (16%)
  waiting for transfers between devices  24.2 us (12%)
  between operations  14.4 us (7%)
  local copies, waits for them, and re-layouts  11.6 us (6%)
    pallas_call x7, Pallas kernels, call(): pl.pallas_call(kernel, out_shape=outs, grid=grid, in_specs=specs, out_spe...  82.6 us
    ppermute x8, starting transfers between devices, step_to(): return lax.ppermute(block, axis, route)  25.9 us
    all_to_all x1, blocking collectives, across_x(): got = lax.all_to_all(parts, 'bx', 0, 0, tiled=True)  19.9 us
    all_gather x1, waiting for transfers between devices, shards(): rows = lax.all_gather(rows, 'by', axis=0, tiled=True)  13.9 us
    all_to_all x1, blocking collectives, across_x(): lax.all_to_all(jnp.broadcast_to(mine[None], (count,) + mine.shape), 'bx',...  10.9 us
    unnamed x50, local copies, waits for them, and re-layouts  10.6 us
    ppermute x3, starting transfers between devices, shards(): lax.ppermute(cut[s - 1], 'by', [(i, (i + 2 * s) % extent_y) for i in rang...  5.02 us
    ppermute x8, waiting for transfers between devices, step_to(): return lax.ppermute(block, axis, route)  4.67 us
  transfers between devices with their start and end apart: 13, of which 6 were waited for; matrix products, arithmetic and copies ran while one was open for 0% of the time, Pallas kernels for 13%

profile of v2, /device:TPU:1, one launch (start us, length us, event | category | flops | bytes accessed | tf_op | source)
XLA Modules:
  0.0 195.6 jit_solution(4044921789167042221)
XLA Ops:
  11.6 3.0 %sort_rows.1 = (bf16[1024,512]{1,0:T(8,128)(2,1)S(1)}, bf16[512,512]{1,0:T(8,128)(2,1)S(1)}, bf16[512,512]{1,0:T(8,128)(2,1)S(1)}, bf16[512,512]{1,0:T(8,128)(2,1)S(1)}, bf16[512,512]{1,0:T(8,128)(2,1)S(1)}) custom-call(s32[2]{0:T(128)S(1)} %pad_add_fusion.pos, s32[2048]{0:T(1024)S(1)} %reshape.59.ids, s32[512]{0:T(512)S(1)} %reshape.60.cnt, ...), custom_call_target="tpu_custom_call" | custom-call | flops 1073741824 | bytes 4194304 | tf_op jit(solution)/shard_map/sort_rows/pallas_call | solution.py:422
  15.7 4.4 %collective-permute-start = (bf16[512,512]{1,0:T(8,128)(2,1)S(1)}, bf16[512,512]{1,0:T(8,128)(2,1)S(1)}, u32[]{:S(2)}, u32[]{:S(2)}) collective-permute-start(bf16[512,512]{1,0:T(8,128)(2,1)S(1)} %get-tuple-element.63), channel_id=1, source_target_pairs={{0,8},{8,16},{16,24},{24,32},{32,40},{40,48},{48,56},{56,64},{64,7... | collective-permute-start | bytes 1572872 | tf_op jit(solution)/shard_map/ppermute | solution.py:404
  20.1 1.3 collective-permute-start.1
  21.4 4.0 %collective-permute-start.2 = (bf16[512,512]{1,0:T(8,128)(2,1)S(1)}, bf16[512,512]{1,0:T(8,128)(2,1)S(1)}, u32[]{:S(2)}, u32[]{:S(2)}) collective-permute-start(bf16[512,512]{1,0:T(8,128)(2,1)S(1)} %get-tuple-element.65), channel_id=1, source_target_pairs={{0,1},{1,2},{2,3},{3,4},{4,5},{5,6},{6,7},{8,9},{9,10},{10,11},{11... | collective-permute-start | bytes 1572872 | tf_op jit(solution)/shard_map/ppermute | solution.py:404
  25.4 1.9 collective-permute-start.3
  27.4 7.7 %project.1 = (bf16[4,256,512]{2,1,0:T(8,128)(2,1)}, bf16[4,512,256]{2,1,0:T(8,128)(2,1)}, bf16[4,4,256,128]{3,2,1,0:T(8,128)(2,1)}, bf16[4,4,128,256]{3,2,1,0:T(...) custom-call(s32[1,1024]{1,0:T(1,128)} %bitcast.15, ...), custom_call_target="tpu_custom_call" | custom-call | flops 3221225472 | bytes 14680064 | tf_op jit(solution)/shard_map/project/pallas_call | solution.py:422
  36.9 51.7 %attend.1 = (bf16[4,512,256]{2,1,0:T(8,128)(2,1)}, bf16[4,512,256]{2,1,0:T(8,128)(2,1)}, f32[4,2,4,256,128]{4,3,2,1,0:T(8,128)}, bf16[2,2,4,256,128]{4,3,2,1,0:T...) custom-call(s32[2]{0:T(128)} %copy-done.10, ...), custom_call_target="tpu_custom_call" | custom-call | flops 8053063680 | bytes 25165824 | tf_op jit(solution)/shard_map/attend/pallas_call | solution.py:422
  89.4 2.5 %collective-permute-done.4.got = bf16[1040,512]{1,0:T(8,128)(2,1)S(1)} collective-permute-done((bf16[1040,512]{1,0:T(8,128)(2,1)}, bf16[1040,512]{1,0:T(8,128)(2,1)S(1)}, u32[]{:S(2)}, u32[]{:S(2)}) %collective-permute-start.4) | collective-permute-done | bytes 1064992 | tf_op jit(solution)/shard_map/ppermute | solution.py:494
  94.7 2.9 %collective-permute-start.5 = (bf16[272,512]{1,0:T(8,128)(2,1)S(1)}, bf16[272,512]{1,0:T(8,128)(2,1)S(1)}, u32[]{:S(2)}, u32[]{:S(2)}) collective-permute-start(bf16[272,512]{1,0:T(8,128)(2,1)S(1)} %get-tuple-element.82), channel_id=1, source_target_pairs={{0,2},{1,3},{2,4},{3,5},{4,6},{5,7},{6,0},{7,1},{8,10},{9,11},{10,... | collective-permute-start | bytes 835592 | tf_op jit(solution)/shard_map/ppermute | solution.py:505
  97.5 2.1 %collective-permute-start.6 = (bf16[272,512]{1,0:T(8,128)(2,1)S(1)}, bf16[272,512]{1,0:T(8,128)(2,1)S(1)}, u32[]{:S(2)}, u32[]{:S(2)}) collective-permute-start(bf16[272,512]{1,0:T(8,128)(2,1)S(1)} %get-tuple-element.83), channel_id=1, source_target_pairs={{0,4},{1,5},{2,6},{3,7},{4,0},{5,1},{6,2},{7,3},{8,12},{9,13},{10,... | collective-permute-start | bytes 835592 | tf_op jit(solution)/shard_map/ppermute | solution.py:505
  99.6 1.3 collective-permute-start.8
  100.9 4.3 %collective-permute-start.9 = (bf16[2,2,4,256,128]{4,3,2,1,0:T(8,128)(2,1)}, bf16[2,2,4,256,128]{4,3,2,1,0:T(8,128)(2,1)S(1)}, u32[]{:S(2)}, u32[]{:S(2)}) collective-permute-start(bf16[2,2,4,256,128]{4,3,2,1,0:T(8,128)(2,1)} %get-tuple-element.91), channel_id=1, source_target_pairs={{0,8},{8,16},{16,24},{24,32},{32,40},{40,48},{48,56},{56,64},{64,7... | collective-permute-start | bytes 3145736 | tf_op jit(solution)/shard_map/ppermute | solution.py:404
  105.2 2.9 %collective-permute-start.10 = (bf16[2,2,4,256,128]{4,3,2,1,0:T(8,128)(2,1)}, bf16[2,2,4,256,128]{4,3,2,1,0:T(8,128)(2,1)S(1)}, u32[]{:S(2)}, u32[]{:S(2)}) collective-permute-start(bf16[2,2,4,256,128]{4,3,2,1,0:T(8,128)(2,1)} %get-tuple-element.92), channel_id=1, source_target_pairs={{1,0},{2,1},{3,2},{4,3},{5,4},{6,5},{7,6},{9,8},{10,9},{11,10},{12... | collective-permute-start | bytes 3145736 | tf_op jit(solution)/shard_map/ppermute | solution.py:404
  108.1 5.8 %collective-permute-start.11 = (bf16[2,2,4,256,128]{4,3,2,1,0:T(8,128)(2,1)}, bf16[2,2,4,256,128]{4,3,2,1,0:T(8,128)(2,1)S(1)}, u32[]{:S(2)}, u32[]{:S(2)}) collective-permute-start(bf16[2,2,4,256,128]{4,3,2,1,0:T(8,128)(2,1)} %get-tuple-element.93), channel_id=1, source_target_pairs={{0,1},{1,2},{2,3},{3,4},{4,5},{5,6},{6,7},{8,9},{9,10},{10,11},{11... | collective-permute-start | bytes 3145736 | tf_op jit(solution)/shard_map/ppermute | solution.py:404
  114.0 4.9 %branch_rows.1 = (bf16[1024,512]{1,0:T(8,128)(2,1)}, f32[1024,512]{1,0:T(8,128)S(1)}) custom-call(s32[1,1024]{1,0:T(1,128)S(1)} %bitcast.18, bf16[512,1024]{1,0:T(8,128)(2,1)S(1)} %copy-done.3, bf16[512,512]{1,0:T(8,128)(2,1)S(1)} %copy-done.12, bf16[4,512,256]{2,1,0:T(8,128)(2,1)S(1)} %copy-done.14, bf16[4,512,256]{2,1,0:T(8,128)(2,1)S(1)} %copy-done.15), custom_call_target="tpu_custom_call" | custom-call | flops 3221225472 | bytes 7340032 | tf_op jit(solution)/shard_map/branch_rows/pallas_call | solution.py:422
  118.9 1.3 copy-done.1
  120.3 3.1 %collective-permute-done.7 = bf16[272,512]{1,0:T(8,128)(2,1)S(1)} collective-permute-done((bf16[272,512]{1,0:T(8,128)(2,1)S(1)}, bf16[272,512]{1,0:T(8,128)(2,1)S(1)}, u32[]{:S(2)}, u32[]{:S(2)}) %collective-permute-start.7) | collective-permute-done | bytes 278560 | tf_op jit(solution)/shard_map/ppermute | solution.py:505
  123.6 2.8 %collective-permute-done.8.b0 = bf16[2,2,4,256,128]{4,3,2,1,0:T(8,128)(2,1)S(1)} collective-permute-done((bf16[2,2,4,256,128]{4,3,2,1,0:T(8,128)(2,1)}, bf16[2,2,4,256,128]{4,3,2,1,0:T(8,128)(2,1)S(1)}, u32[]{:S(2)}, u32[]{:S(2)}) %collective-permute-start.8) | collective-permute-done | bytes 1048608 | tf_op jit(solution)/shard_map/ppermute | solution.py:404
  127.4 19.9 %all_to_all.10 = bf16[16,16,640]{2,1,0:T(8,128)(2,1)S(1)} all-to-all(bf16[16,16,640]{2,1,0:T(8,128)(2,1)S(1)} %pad_maximum_fusion), channel_id=1, replica_groups=mesh['bx'=16,'by'=8] {'bx'}, dimensions={0} | all-to-all | bytes 655360 | tf_op jit(solution)/shard_map/all_to_all | solution.py:413
  147.4 10.9 %all_to_all.11 = bf16[16,16,512]{2,1,0:T(8,128)(2,1)} all-to-all(bf16[16,16,512]{2,1,0:T(8,128)(2,1)S(1)} %broadcast_in_dim.28), channel_id=1, replica_groups=mesh['bx'=16,'by'=8] {'bx'}, dimensions={0} | all-to-all | bytes 524288 | tf_op jit(solution)/shard_map/all_to_all | solution.py:417
  158.9 12.2 %token_rows.1 = f32[1024,512]{1,0:T(8,128)} custom-call(s32[2]{0:T(128)} %copy-done.10, s32[2048]{0:T(1024)} %copy-done.5, s32[512]{0:T(512)} %copy-done.7, s32[1,1024]{1,0:T(1,128)} %bitcast.16, bf16[1024,512]{1,0:T(8,128)(2,1)} %bitcast.13, f32[1,512]{1,0:T(1,128)} %bitcast.25, bf16[512,1024]{1,0:T(8,128)(2,1)} %w_qk.5, bf16[512,512]{1,0:T(8,128)(2,1)} %w_v.3, ...), custom_call_target="tpu_custom_call" | custom-call | flops 3221225472 | bytes 16777216 | tf_op jit(solution)/shard_map/token_rows/pallas_call | solution.py:422
  171.1 13.9 %all-gather.2.cloned.1.call-done.rows = bf16[2048,512]{1,0:T(8,128)(2,1)} async-done(((bf16[256,512]{1,0:T(8,128)(2,1)}), bf16[2048,512]{1,0:T(8,128)(2,1)}) %all-gather.2.cloned.1.call-update) | async-done | bytes 2097168 | tf_op jit(solution)/shard_map/all_gather | solution.py:522
  185.0 1.6 copy-done
  186.6 2.2 %weight_grads.1 = (f32[512,1024]{1,0:T(8,128)}, f32[512,512]{1,0:T(8,128)}, f32[512,512]{1,0:T(8,128)}) custom-call(bf16[2048,512]{1,0:T(8,128)(2,1)S(1)} %copy-done), custom_call_target="tpu_custom_call" | custom-call | bytes 6291456 | tf_op jit(solution)/shard_map/weight_grads/pallas_call | solution.py:422
  (74 shorter events, 12.7 us)
Async XLA Ops:
  7.2 177.9 %all-gather.2.cloned.1.call-start = ((), (), s32[]{:S(2)}) async-start(), calls=%async_computation.2 | async-start | bytes 2359296 | tf_op jit(solution)/shard_map/all_gather | solution.py:522
  9.6 25.4 %copy-start.5 = (s32[2048]{0:T(1024)}, s32[2048]{0:T(1024)S(1)}, u32[]{:S(2)}) copy-start(s32[2048]{0:T(1024)S(1)} %reshape.59.ids) | copy-start | bytes 24580
  9.7 25.3 %copy-start.10 = (s32[2]{0:T(128)}, s32[2]{0:T(128)S(1)}, u32[]{:S(2)}) copy-start(s32[2]{0:T(128)S(1)} %pad_add_fusion.pos) | copy-start | bytes 28
  15.7 19.4 %collective-permute-start = (bf16[512,512]{1,0:T(8,128)(2,1)S(1)}, bf16[512,512]{1,0:T(8,128)(2,1)S(1)}, u32[]{:S(2)}, u32[]{:S(2)}) collective-permute-start(bf16[512,512]{1,0:T(8,128)(2,1)S(1)} %get-tuple-element.63), channel_id=1, source_target_pairs={{0,8},{8,16},{16,24},{24,32},{32,40},{40,48},{48,56},{56,64},{64,7... | collective-permute-start | bytes 1572872 | tf_op jit(solution)/shard_map/ppermute | solution.py:404
  20.1 15.0 %collective-permute-start.1 = (bf16[512,512]{1,0:T(8,128)(2,1)S(1)}, bf16[512,512]{1,0:T(8,128)(2,1)S(1)}, u32[]{:S(2)}, u32[]{:S(2)}) collective-permute-start(bf16[512,512]{1,0:T(8,128)(2,1)S(1)} %get-tuple-element.64), channel_id=1, source_target_pairs={{8,0},{16,8},{24,16},{32,24},{40,32},{48,40},{56,48},{64,56},{72,6... | collective-permute-start | bytes 1572872 | tf_op jit(solution)/shard_map/ppermute | solution.py:404
  21.4 13.7 %collective-permute-start.2 = (bf16[512,512]{1,0:T(8,128)(2,1)S(1)}, bf16[512,512]{1,0:T(8,128)(2,1)S(1)}, u32[]{:S(2)}, u32[]{:S(2)}) collective-permute-start(bf16[512,512]{1,0:T(8,128)(2,1)S(1)} %get-tuple-element.65), channel_id=1, source_target_pairs={{0,1},{1,2},{2,3},{3,4},{4,5},{5,6},{6,7},{8,9},{9,10},{10,11},{11... | collective-permute-start | bytes 1572872 | tf_op jit(solution)/shard_map/ppermute | solution.py:404
  25.4 10.6 %collective-permute-start.3 = (bf16[512,512]{1,0:T(8,128)(2,1)S(1)}, bf16[512,512]{1,0:T(8,128)(2,1)S(1)}, u32[]{:S(2)}, u32[]{:S(2)}) collective-permute-start(bf16[512,512]{1,0:T(8,128)(2,1)S(1)} %get-tuple-element.66), channel_id=1, source_target_pairs={{1,0},{2,1},{3,2},{4,3},{5,4},{6,5},{7,6},{9,8},{10,9},{11,10},{12... | collective-permute-start | bytes 1572872 | tf_op jit(solution)/shard_map/ppermute | solution.py:404
  36.9 55.1 %copy-start.11 = (s32[2]{0:T(128)S(1)}, s32[2]{0:T(128)}, u32[]{:S(2)}) copy-start(s32[2]{0:T(128)} %copy-done.10) | copy-start | bytes 28
  36.9 77.1 %copy-start.3 = (bf16[512,1024]{1,0:T(8,128)(2,1)S(1)}, bf16[512,1024]{1,0:T(8,128)(2,1)}, u32[]{:S(2)}) copy-start(bf16[512,1024]{1,0:T(8,128)(2,1)} %w_qk.5) | copy-start | bytes 3145732
  36.9 77.1 %copy-start.12 = (bf16[512,512]{1,0:T(8,128)(2,1)S(1)}, bf16[512,512]{1,0:T(8,128)(2,1)}, u32[]{:S(2)}) copy-start(bf16[512,512]{1,0:T(8,128)(2,1)} %w_out.3) | copy-start | bytes 1572868
  88.6 25.4 %copy-start.9 = (s32[1,1,1024]{2,1,0:T(1,128)S(1)}, s32[1,1,1024]{2,1,0:T(1,128)}, u32[]{:S(2)}) copy-start(s32[1,1,1024]{2,1,0:T(1,128)} %param.17) | copy-start | bytes 12292
  88.6 3.4 %collective-permute-start.4 = (bf16[1040,512]{1,0:T(8,128)(2,1)}, bf16[1040,512]{1,0:T(8,128)(2,1)S(1)}, u32[]{:S(2)}, u32[]{:S(2)}) collective-permute-start(bf16[1040,512]{1,0:T(8,128)(2,1)} %get-tuple-element.79), channel_id=1, source_target_pairs={{0,1},{1,0},{2,3},{3,2},{4,5},{5,4},{6,7},{7,6},{8,9},{9,8},{10,11... | collective-permute-start | bytes 3194888 | tf_op jit(solution)/shard_map/ppermute | solution.py:494
  93.9 20.1 %copy-start.15 = (bf16[4,512,256]{2,1,0:T(8,128)(2,1)S(1)}, bf16[4,512,256]{2,1,0:T(8,128)(2,1)}, u32[]{:S(2)}) copy-start(bf16[4,512,256]{2,1,0:T(8,128)(2,1)} %get-tuple-element.87.dq_t) | copy-start | bytes 3145732
  94.7 13.4 %collective-permute-start.5 = (bf16[272,512]{1,0:T(8,128)(2,1)S(1)}, bf16[272,512]{1,0:T(8,128)(2,1)S(1)}, u32[]{:S(2)}, u32[]{:S(2)}) collective-permute-start(bf16[272,512]{1,0:T(8,128)(2,1)S(1)} %get-tuple-element.82), channel_id=1, source_target_pairs={{0,2},{1,3},{2,4},{3,5},{4,6},{5,7},{6,0},{7,1},{8,10},{9,11},{10,... | collective-permute-start | bytes 835592 | tf_op jit(solution)/shard_map/ppermute | solution.py:505
  97.5 16.3 %collective-permute-start.6 = (bf16[272,512]{1,0:T(8,128)(2,1)S(1)}, bf16[272,512]{1,0:T(8,128)(2,1)S(1)}, u32[]{:S(2)}, u32[]{:S(2)}) collective-permute-start(bf16[272,512]{1,0:T(8,128)(2,1)S(1)} %get-tuple-element.83), channel_id=1, source_target_pairs={{0,4},{1,5},{2,6},{3,7},{4,0},{5,1},{6,2},{7,3},{8,12},{9,13},{10,... | collective-permute-start | bytes 835592 | tf_op jit(solution)/shard_map/ppermute | solution.py:505
  99.6 26.7 %collective-permute-start.8 = (bf16[2,2,4,256,128]{4,3,2,1,0:T(8,128)(2,1)}, bf16[2,2,4,256,128]{4,3,2,1,0:T(8,128)(2,1)S(1)}, u32[]{:S(2)}, u32[]{:S(2)}) collective-permute-start(bf16[2,2,4,256,128]{4,3,2,1,0:T(8,128)(2,1)} %get-tuple-element.90), channel_id=1, source_target_pairs={{8,0},{16,8},{24,16},{32,24},{40,32},{48,40},{56,48},{64,56},{72,6... | collective-permute-start | bytes 3145736 | tf_op jit(solution)/shard_map/ppermute | solution.py:404
  100.9 26.4 %collective-permute-start.9 = (bf16[2,2,4,256,128]{4,3,2,1,0:T(8,128)(2,1)}, bf16[2,2,4,256,128]{4,3,2,1,0:T(8,128)(2,1)S(1)}, u32[]{:S(2)}, u32[]{:S(2)}) collective-permute-start(bf16[2,2,4,256,128]{4,3,2,1,0:T(8,128)(2,1)} %get-tuple-element.91), channel_id=1, source_target_pairs={{0,8},{8,16},{16,24},{24,32},{32,40},{40,48},{48,56},{56,64},{64,7... | collective-permute-start | bytes 3145736 | tf_op jit(solution)/shard_map/ppermute | solution.py:404
  105.2 22.1 %collective-permute-start.10 = (bf16[2,2,4,256,128]{4,3,2,1,0:T(8,128)(2,1)}, bf16[2,2,4,256,128]{4,3,2,1,0:T(8,128)(2,1)S(1)}, u32[]{:S(2)}, u32[]{:S(2)}) collective-permute-start(bf16[2,2,4,256,128]{4,3,2,1,0:T(8,128)(2,1)} %get-tuple-element.92), channel_id=1, source_target_pairs={{1,0},{2,1},{3,2},{4,3},{5,4},{6,5},{7,6},{9,8},{10,9},{11,10},{12... | collective-permute-start | bytes 3145736 | tf_op jit(solution)/shard_map/ppermute | solution.py:404
  108.1 19.2 %collective-permute-start.11 = (bf16[2,2,4,256,128]{4,3,2,1,0:T(8,128)(2,1)}, bf16[2,2,4,256,128]{4,3,2,1,0:T(8,128)(2,1)S(1)}, u32[]{:S(2)}, u32[]{:S(2)}) collective-permute-start(bf16[2,2,4,256,128]{4,3,2,1,0:T(8,128)(2,1)} %get-tuple-element.93), channel_id=1, source_target_pairs={{0,1},{1,2},{2,3},{3,4},{4,5},{5,6},{6,7},{8,9},{9,10},{10,11},{11... | collective-permute-start | bytes 3145736 | tf_op jit(solution)/shard_map/ppermute | solution.py:404
  113.9 9.5 %collective-permute-start.7 = (bf16[272,512]{1,0:T(8,128)(2,1)S(1)}, bf16[272,512]{1,0:T(8,128)(2,1)S(1)}, u32[]{:S(2)}, u32[]{:S(2)}) collective-permute-start(bf16[272,512]{1,0:T(8,128)(2,1)S(1)} %get-tuple-element.84), channel_id=1, source_target_pairs={{0,6},{1,7},{2,0},{3,1},{4,2},{5,3},{6,4},{7,5},{8,14},{9,15},{10,... | collective-permute-start | bytes 835592 | tf_op jit(solution)/shard_map/ppermute | solution.py:505
  126.3 32.6 %copy-start.16 = (bf16[2,2,4,256,128]{4,3,2,1,0:T(8,128)(2,1)}, bf16[2,2,4,256,128]{4,3,2,1,0:T(8,128)(2,1)S(1)}, u32[]{:S(2)}) copy-start(bf16[2,2,4,256,128]{4,3,2,1,0:T(8,128)(2,1)S(1)} %collective-permute-done.8.b0) | copy-start | bytes 3145732
  127.3 31.6 %copy-start.17 = (bf16[2,2,4,256,128]{4,3,2,1,0:T(8,128)(2,1)}, bf16[2,2,4,256,128]{4,3,2,1,0:T(8,128)(2,1)S(1)}, u32[]{:S(2)}) copy-start(bf16[2,2,4,256,128]{4,3,2,1,0:T(8,128)(2,1)S(1)} %collective-permute-done.9.b1) | copy-start | bytes 3145732
  127.3 31.0 %copy-start.18 = (bf16[2,2,4,256,128]{4,3,2,1,0:T(8,128)(2,1)}, bf16[2,2,4,256,128]{4,3,2,1,0:T(8,128)(2,1)S(1)}, u32[]{:S(2)}) copy-start(bf16[2,2,4,256,128]{4,3,2,1,0:T(8,128)(2,1)S(1)} %collective-permute-done.10.b2) | copy-start | bytes 3145732
  127.3 31.0 %copy-start.19 = (bf16[2,2,4,256,128]{4,3,2,1,0:T(8,128)(2,1)}, bf16[2,2,4,256,128]{4,3,2,1,0:T(8,128)(2,1)S(1)}, u32[]{:S(2)}) copy-start(bf16[2,2,4,256,128]{4,3,2,1,0:T(8,128)(2,1)S(1)} %collective-permute-done.11.b3) | copy-start | bytes 3145732
  (13 other events, 38.3 us)
Sparse Core Ops, SparseCore 0:
  158.4 26.5 all-gather.1

commit v3 on v2

--- a/solution.py
+++ b/solution.py
@@ -106,10 +106,14 @@
     return (row == order_ref[...]).astype(F32).astype(BF)
 
 
-def sort_kernel(dims, pos, ids, cnt, order, tok, out, s0, s1, s2, s3, cols):
+def sort_kernel(dims, pos, ids, cnt, order, tok_in, out, s0, s1, s2, s3, cols, tok, sem):
     extent_x, extent_y, blocks, slots = dims
     n = tok.shape[0]
+    copy = pltpu.make_async_copy(tok_in, tok, sem.at[0])
+    copy.start()
     cols[...] = order_columns(order)
+    table = send_table(ids, cnt, pos, extent_x, extent_y, blocks, slots)
+    copy.wait()
 
     def body(b, _):
         rows = pl.ds(pl.multiple_of(b * BLK, BLK), BLK)
@@ -117,7 +121,6 @@
         return 0
 
     lax.fori_loop(0, n // BLK, body, 0)
-    table = send_table(ids, cnt, pos, extent_x, extent_y, blocks, slots)
     for ref, pair in zip((s0, s1, s2, s3), table):
         for k, b in enumerate(pair):
             ref[k * BLK : (k + 1) * BLK, :] = out[pl.ds(pl.multiple_of(b * BLK, BLK), BLK), :]
@@ -134,7 +137,7 @@
 
     rows = pl.ds(pl.multiple_of(b * BLK, BLK), BLK)
     grad = mm(one_hot_rows(cols[rows, :], n), cot[...]).astype(BF)
-    sc[0] = grad
+    sc[...] = grad
     values, inv = rms(tok[...])
     normed = (values * inv * gain[...]).astype(BF)
     n_t[0] = normed.T
@@ -170,8 +173,10 @@
         fetch(ref, far.at[seg], first)
     for src, dst in ((kn_in, pkn.at[mine]), (kt_in, pkt.at[mine]), (vn_in, pvn.at[mine]),
                      (vt_in, pvt.at[mine]), (qt_in, qt), (gt_in, gt), (qn_in, qn), (gn_in, gn),
-                     (nt_in, n_t.at[mine]), (sc_in, sc)):
+                     (sc_in, sc)):
         fetch(src, dst, later)
+    for b in range(blocks):
+        fetch(nt_in.at[b], n_t.at[:, pl.ds(b * BLK, BLK)], later)
     table = pool_table(ids, cnt, pos, extent_y, blocks, slots)
     for b in range(blocks):
         for j in range(slots):
@@ -184,7 +189,7 @@
         rows = pl.ds(pl.multiple_of(lax.rem(i, 2) * BLK, BLK), BLK)
         values, inv = rms(far[lax.div(i, 2), rows, :])
         normed = (values * inv * gain[...]).astype(BF)
-        n_t[blocks + i] = normed.T
+        n_t[:, pl.ds(pl.multiple_of((blocks + i) * BLK, BLK), BLK)] = normed.T
         made = mm(normed, w_qk[:, d:]).astype(BF)
         made_v = mm(normed, w_v[...]).astype(BF)
         for mat, nat, tra in ((made, pkn, pkt), (made_v, pvn, pvt)):
@@ -245,8 +250,9 @@
                 ctx = c if ctx is None else ctx + c
                 dq = t if dq is None else dq + t
             rows = pl.ds(pl.multiple_of(p * PAIR + h * half, half), half)
-            ctx_t[b, rows, :] = ctx.astype(BF)
-            dq_t[b, rows, :] = (dq * 0.125).astype(BF)
+            cols = pl.ds(pl.multiple_of(b * BLK, BLK), BLK)
+            ctx_t[rows, cols] = ctx.astype(BF)
+            dq_t[rows, cols] = (dq * 0.125).astype(BF)
         for j, k in enumerate(at):
             acc[k, 0, p] += mm(ds_scr[j], q_mask)
             acc[k, 1, p] += mm(p_scr[j], g_mask)
@@ -293,11 +299,8 @@
     def place(i, value):
         terms[lax.rem(i + core, 2), (i // 2) * BLK : (i // 2 + 1) * BLK, :] = value.astype(BF)
 
-    g_q = g_o = None
-    for b in range(blocks):
-        a, c = mm_nt(n_t[b], dq_t[b]), mm(ctx_t[b], sc[b])
-        g_q = a if g_q is None else g_q + a
-        g_o = c if g_o is None else g_o + c
+    g_q = mm_nt(n_t[:, : blocks * BLK], dq_t[...])
+    g_o = mm(ctx_t[...], sc[...])
     for i, g in ((0, g_q), (6, g_o)):
         place(i, g[:BLK])
         place(i + 1, g[BLK:])
@@ -305,10 +308,8 @@
     for i, pool, w, lo in ((2, pkn, w_qk, d), (4, pvn, w_v, 0)):
         made = []
         for p in range(0, np_, 2):
-            g = None
-            for b in range(blocks + 8):
-                t = mm(n_t[b], jnp.concatenate([pool[b, p], pool[b, p + 1]], axis=1))
-                g = t if g is None else g + t
+            cols = [jnp.concatenate([pool[b, p], pool[b, p + 1]], axis=1) for b in range(blocks + 8)]
+            g = mm(n_t[...], jnp.concatenate(cols, axis=0))
             at = lo + p * PAIR
             total += jnp.sum(g * w[:, at : at + 2 * PAIR].astype(F32), axis=1, keepdims=True)
             made.append(g)
@@ -341,20 +342,15 @@
 
 
 def output_kernel(order, w_qk, w_out, ctx_t, dq_t, out, part):
-    blocks, d = ctx_t.shape[0], w_out.shape[0]
+    d = w_out.shape[0]
 
     def body(a, _):
         rows = pl.ds(pl.multiple_of(a * BLK, BLK), BLK)
         back = one_hot_back(order, a * BLK, BLK)
-        made = []
-        for ref in (ctx_t, dq_t):
-            total = None
-            for b in range(blocks):
-                t = mm_nt(back[:, b * BLK : (b + 1) * BLK], ref[b])
-                total = t if total is None else total + t
-            made.append(total.astype(BF))
-        out[rows, :] = mm(made[0], w_out[...]).astype(BF)
-        part[rows, :] = mm_nt(made[1], w_qk[:, :d])
+        ctx = mm_nt(back, ctx_t[...]).astype(BF)
+        dq = mm_nt(back, dq_t[...]).astype(BF)
+        out[rows, :] = mm(ctx, w_out[...]).astype(BF)
+        part[rows, :] = mm_nt(dq, w_qk[:, :d])
         return 0
 
     lax.fori_loop(0, out.shape[0] // BLK, body, 0)
@@ -390,8 +386,16 @@
     lax.fori_loop(0, out.shape[0] // BLK, body, 0)
 
 
-def place_kernel(rows, qk, v, o):
+def place_kernel(pos, *refs):
+    *parts, qk, v, o, rows = refs
     d = v.shape[0]
+    count = len(parts) // 2
+    core, y = lax.rem(pos[1], 2), lax.div(pos[1], 2)
+    size = parts[0].shape[0]
+    for i, ref in enumerate(parts):
+        c = core if i < count else 1 - core
+        at = (lax.rem(y - i % count + count, count) * 2 + c) * size
+        rows[pl.ds(pl.multiple_of(at, size), size), :] = ref[...]
     qk[:, :d] = rows[:d, :].astype(F32)
     qk[:, d:] = rows[d : 2 * d, :].astype(F32)
     v[...] = rows[2 * d : 3 * d, :].astype(F32)
@@ -449,8 +453,8 @@
     sends = [shape((2 * BLK, d), BF)] * 4
     sorted_rows, *sent = call(
         functools.partial(sort_kernel, dims), "sort_rows",
-        [shape((n, d), BF)] + sends, (pos, ids, cnt, order, tok), [SM, SM, SM, VM, VM],
-        [pltpu.VMEM((n, 128), jnp.int32)], 32, 2 * n * n * d, 4 << 20,
+        [shape((n, d), BF)] + sends, (pos, ids, cnt, order, tok), [SM, SM, SM, VM, AN],
+        [pltpu.VMEM((n, 128), jnp.int32), pltpu.VMEM((n, d), BF), pltpu.SemaphoreType.DMA((1,))], 32, 2 * n * n * d, 4 << 20,
     )
     arrived = [
         step_to(sent[0], "bx", 1), step_to(sent[1], "bx", -1),
@@ -462,13 +466,13 @@
         return pl.BlockSpec((1,) + dims_[1:], lambda b: (b,) + (0,) * (len(dims_) - 1))
 
     whole = pl.BlockSpec(memory_space=pltpu.VMEM)
-    out_dims = [(blocks, BLK, d), (blocks, d, BLK)] + [nat, tra] * 4
+    out_dims = [(n, d), (blocks, d, BLK)] + [nat, tra] * 4
     sc, n_t, *made = call(
         functools.partial(project_kernel, np_), "project", [shape(k, BF) for k in out_dims],
         (order, sorted_rows, cot, gain, w_query_key, w_value, w_out),
         [whole, pl.BlockSpec((BLK, d), lambda b: (b, 0))] + [whole] * 5,
         [pltpu.VMEM((n, 128), jnp.int32)], LIMIT, 2 * n * n * d + 8 * n * d * d, 14 << 20,
-        out_specs=[a_block(k) for k in out_dims], grid=(blocks,),
+        out_specs=[pl.BlockSpec((BLK, d), lambda b: (b, 0))] + [a_block(k) for k in out_dims[1:]], grid=(blocks,),
     )
     pool = blocks + 8
     tile = (slots + 1, BLK, 2 * BLK)
@@ -476,62 +480,65 @@
     ins = (pos, ids, cnt, gain, *arrived, w_query_key, w_value, *made, sc, n_t)
     ctx_t, dq_t, own, *back, keep, send, gain_term = call(
         functools.partial(attend_kernel, dims, np_), "attend",
-        [shape((blocks, d, BLK), BF)] * 2 + [shape((blocks, 2, np_, BLK, PAIR), F32)]
+        [shape((d, n), BF)] * 2 + [shape((blocks, 2, np_, BLK, PAIR), F32)]
         + [shape((2, 2, np_, BLK, PAIR), BF)] * 4
         + [shape((n, d), BF), shape((n + 16, d), BF), shape((8, d), F32)],
         ins, [SM] * 3 + [VM] + [AN] * (len(ins) - 4),
         [vmem((4, 2 * BLK, d), BF), vmem((d, 2 * d), BF), vmem((d, d), BF)]
         + [vmem(nat, BF), vmem(tra, BF)] * 2
         + [vmem((pool,) + nat[1:], BF), vmem((pool,) + tra[1:], BF)] * 2
-        + [vmem((blocks, BLK, d), BF), vmem((pool, d, BLK), BF)] + [vmem((blocks, d, BLK), BF)] * 2
+        + [vmem((n, d), BF), vmem((d, pool * BLK), BF)] + [vmem((d, n), BF)] * 2
         + [vmem((pool, 2) + nat[1:], F32), vmem(tile, F32), vmem(tile, F32), vmem(tile, BF), vmem(tile, BF),
            vmem((2, n + 16, d), BF), pltpu.SMEM((blocks * slots,), jnp.int32),
-           pltpu.SemaphoreType.DMA((16,)), pltpu.SemaphoreType.DMA((13,))],
+           pltpu.SemaphoreType.DMA((20,)), pltpu.SemaphoreType.DMA((13,))],
         LIMIT, 12 * blocks * 5 * BLK * BLK * d, 24 << 20, blocks * 5 * BLK * BLK * 8,
         out_specs=[AN] * 9 + [VM],
     )
     h0, h1, h2, h3 = back
     cores = lax.ppermute(send, "by", [(i, i ^ 1) for i in range(extent_y)])
-    returned = [
-        step_to(h0, "bx", -1), step_to(h1, "bx", 1), step_to(h2, "by", -1), step_to(h3, "by", 1),
-    ]
+    b_x = [step_to(h0, "bx", -1), step_to(h1, "bx", 1)]
     mine, *cut, gain_sum = call(
         core_kernel, "add_cores",
         [shape((BLK, d), F32)] + [shape((BLK + 16, d), BF)] * 3 + [shape((8, d), F32)],
         (pos, keep, cores, gain_term), [SM, VM, VM, VM], [], 32, 0, 4 << 20,
     )
     count = extent_y // 2
-    got = [
-        lax.ppermute(cut[s - 1], "by", [(i, (i + 2 * s) % extent_y) for i in range(extent_y)])
-        for s in range(1, count)
-    ]
+
+    def along_y(rows, s):
+        return lax.ppermute(rows, "by", [(i, (i + 2 * s) % extent_y) for i in range(extent_y)])
+
+    def other_core(rows):
+        return lax.ppermute(rows, "by", [(i, i ^ 1) for i in range(extent_y)])
+
+    got = [along_y(cut[s - 1], s) for s in range(1, count)]
     branch_out, part = call(
         output_kernel, "branch_rows", [shape((n, d), BF), shape((n, d), F32)],
         (order, w_query_key, w_out, ctx_t, dq_t), [VM] * 5, [], 40,
         4 * n * n * d + 4 * n * d * d, 7 << 20,
     )
+    got, h2, h3 = lax.optimization_barrier((got, h2, h3))
+    b_y = [step_to(h2, "by", -1), step_to(h3, "by", 1)]
     rows, gain_sum = mine, gain_sum[:1]
     for g in got:
         rows = rows + g[:BLK].astype(F32)
         gain_sum = gain_sum + g[BLK : BLK + 1].astype(F32)
-    rows, gain_sum, part, branch_out, *returned = lax.optimization_barrier(
-        (rows, gain_sum, part, branch_out, *returned)
-    )
+    rows, gain_sum, part, branch_out, b_x = lax.optimization_barrier((rows, gain_sum, part, branch_out, b_x))
     rows, gain_sum = across_x(rows, gain_sum)
     rows, part = lax.optimization_barrier((rows, part))
-    rows = lax.all_gather(rows, "by", axis=0, tiled=True)
-
-    b_x1, b_xm, b_y1, b_ym = returned
+    chunks = [rows] + [along_y(rows, s) for s in range(1, count)]
+
     grad_rows = call(
         functools.partial(rows_kernel, dims, np_), "token_rows", shape((n, d), F32),
-        (pos, ids, cnt, order, tok, gain, w_query_key, w_value, part, own, b_x1, b_xm, b_y1, b_ym),
+        (pos, ids, cnt, order, tok, gain, w_query_key, w_value, part, own, *b_x, *b_y),
         [SM] * 3 + [VM] * 11,
         [pltpu.VMEM((blocks, 2, np_, BLK, PAIR), F32), pltpu.VMEM((n, 2 * d), BF)],
         56, 4 * n * n * d + 4 * n * d * d, 16 << 20,
     )
+    chunks, grad_rows = lax.optimization_barrier((chunks, grad_rows))
+    chunks = chunks + [other_core(c) for c in chunks]
     grad_qk, grad_v, grad_o = call(
         place_kernel, "weight_grads", [shape((d, 2 * d), F32), shape((d, d), F32), shape((d, d), F32)],
-        (rows,), [VM], [], 32, 0, 6 << 20,
+        (pos, *chunks), [SM] + [VM] * 8, [pltpu.VMEM((4 * d, d), BF)], 32, 0, 6 << 20,
     )
     return (branch_out[None, None], grad_rows[None, None], grad_qk, grad_v, grad_o, gain_sum[0])
 

time: 196 us -> 172 us (0.88)
  waiting for transfers between devices: 24.2 us -> 8.22 us
  between operations: 14.4 us -> 1.07 us
  Pallas kernels: 82.6 us -> 87.1 us
  blocking collectives: 30.8 us -> 26.6 us
  starting transfers between devices: 31.8 us -> 36 us
    all_gather x1 -> x0, waiting for transfers between devices: 13.9 us -> none  [shards(): rows = lax.all_gather(rows, 'by', axis=0, tiled=True)]
    ppermute x3 -> x10, starting transfers between devices: 5.02 us -> 13.3 us  [the longest x6 9.81 us: along_y(): lax.ppermute(rows, 'by', [(i, (i + 2 * s) % extent_y) for i in range(exte...]
    pallas_call x7, Pallas kernels: 82.6 us -> 87.1 us  [call(): pl.pallas_call(kernel, out_shape=outs, grid=grid, in_specs=specs, out_spe...]
    ppermute x3 -> x10, waiting for transfers between devices: 3.15 us -> 7.26 us  [the longest x6 6.15 us: along_y(): lax.ppermute(rows, 'by', [(i, (i + 2 * s) % extent_y) for i in range(exte...]
    all_to_all x1, blocking collectives: 19.9 us -> 15.8 us  [across_x(): got = lax.all_to_all(parts, 'bx', 0, 0, tiled=True)]
    ppermute x8, waiting for transfers between devices: 4.67 us -> 0.96 us  [step_to(): return lax.ppermute(block, axis, route)]
    ppermute x8, starting transfers between devices: 25.9 us -> 22.5 us  [step_to(): return lax.ppermute(block, axis, route)]
    ppermute x1, waiting for transfers between devices: 2.52 us -> 0.01 us  [shards(): cores = lax.ppermute(send, 'by', [(i, i ^ 1) for i in range(extent_y)])]
  transfers between devices with their start and end apart: 13 -> 19, of which waited for: 6 -> 5; matrix products, arithmetic and copies ran while one was open for 0% -> 0% of each run, Pallas kernels for 13% -> 15%
where the time goes in v3:
time: 172 us; the launch traced here: 171 us
  Pallas kernels  87.1 us (51%)
  starting transfers between devices  36 us (21%)
  blocking collectives  26.6 us (15%)
  local copies, waits for them, and re-layouts  11.3 us (7%)
  waiting for transfers between devices  8.22 us (5%)
    pallas_call x7, Pallas kernels, call(): pl.pallas_call(kernel, out_shape=outs, grid=grid, in_specs=specs, out_spe...  87.1 us
    ppermute x8, starting transfers between devices, step_to(): return lax.ppermute(block, axis, route)  22.5 us
    all_to_all x1, blocking collectives, across_x(): got = lax.all_to_all(parts, 'bx', 0, 0, tiled=True)  15.8 us
    all_to_all x1, blocking collectives, across_x(): lax.all_to_all(jnp.broadcast_to(mine[None], (count,) + mine.shape), 'bx',...  10.7 us
    unnamed x54, local copies, waits for them, and re-layouts  10.4 us
    ppermute x6, starting transfers between devices, along_y(): lax.ppermute(rows, 'by', [(i, (i + 2 * s) % extent_y) for i in range(exte...  9.81 us
    ppermute x6, waiting for transfers between devices, along_y(): lax.ppermute(rows, 'by', [(i, (i + 2 * s) % extent_y) for i in range(exte...  6.15 us
    ppermute x4, starting transfers between devices, other_core(): return lax.ppermute(rows, 'by', [(i, i ^ 1) for i in range(extent_y)])  3.52 us
  transfers between devices with their start and end apart: 19, of which 5 were waited for; matrix products, arithmetic and copies ran while one was open for 0% of the time, Pallas kernels for 15%

profile of v3, /device:TPU:1, one launch (start us, length us, event | category | flops | bytes accessed | tf_op | source)
XLA Modules:
  0.0 170.6 jit_solution(1271826455004462417)
XLA Ops:
  3.1 1.2 copy-done.3
  5.1 3.0 %sort_rows.1 = (bf16[1024,512]{1,0:T(8,128)(2,1)S(1)}, bf16[512,512]{1,0:T(8,128)(2,1)S(1)}, bf16[512,512]{1,0:T(8,128)(2,1)S(1)}, bf16[512,512]{1,0:T(8,128)(2,1)S(1)}, bf16[512,512]{1,0:T(8,128)(2,1)S(1)}) custom-call(s32[2]{0:T(128)S(1)} %pad_add_fusion.pos, s32[2048]{0:T(1024)S(1)} %reshape.59.ids, s32[512]{0:T(512)S(1)} %reshape.60.cnt, ...), custom_call_target="tpu_custom_call" | custom-call | flops 1073741824 | bytes 4194304 | tf_op jit(solution)/shard_map/sort_rows/pallas_call | solution.py:426
  9.1 4.4 %collective-permute-start = (bf16[512,512]{1,0:T(8,128)(2,1)S(1)}, bf16[512,512]{1,0:T(8,128)(2,1)S(1)}, u32[]{:S(2)}, u32[]{:S(2)}) collective-permute-start(bf16[512,512]{1,0:T(8,128)(2,1)S(1)} %get-tuple-element.71), channel_id=1, source_target_pairs={{0,8},{8,16},{16,24},{24,32},{32,40},{40,48},{48,56},{56,64},{64,7... | collective-permute-start | bytes 1572872 | tf_op jit(solution)/shard_map/ppermute | solution.py:408
  13.5 1.3 collective-permute-start.1
  14.8 4.0 %collective-permute-start.2 = (bf16[512,512]{1,0:T(8,128)(2,1)S(1)}, bf16[512,512]{1,0:T(8,128)(2,1)S(1)}, u32[]{:S(2)}, u32[]{:S(2)}) collective-permute-start(bf16[512,512]{1,0:T(8,128)(2,1)S(1)} %get-tuple-element.73), channel_id=1, source_target_pairs={{0,1},{1,2},{2,3},{3,4},{4,5},{5,6},{6,7},{8,9},{9,10},{10,11},{11... | collective-permute-start | bytes 1572872 | tf_op jit(solution)/shard_map/ppermute | solution.py:408
  18.8 1.9 %collective-permute-start.3 = (bf16[512,512]{1,0:T(8,128)(2,1)S(1)}, bf16[512,512]{1,0:T(8,128)(2,1)S(1)}, u32[]{:S(2)}, u32[]{:S(2)}) collective-permute-start(bf16[512,512]{1,0:T(8,128)(2,1)S(1)} %get-tuple-element.74), channel_id=1, source_target_pairs={{1,0},{2,1},{3,2},{4,3},{5,4},{6,5},{7,6},{9,8},{10,9},{11,10},{12... | collective-permute-start | bytes 1572872 | tf_op jit(solution)/shard_map/ppermute | solution.py:408
  20.7 7.7 %project.1 = (bf16[1024,512]{1,0:T(8,128)(2,1)}, bf16[4,512,256]{2,1,0:T(8,128)(2,1)}, bf16[4,4,256,128]{3,2,1,0:T(8,128)(2,1)}, bf16[4,4,128,256]{3,2,1,0:T(8,1...) custom-call(s32[1,1024]{1,0:T(1,128)} %bitcast.20, ...), custom_call_target="tpu_custom_call" | custom-call | flops 3221225472 | bytes 14680064 | tf_op jit(solution)/shard_map/project/pallas_call | solution.py:426
  30.3 55.7 %attend.1 = (bf16[512,1024]{1,0:T(8,128)(2,1)}, bf16[512,1024]{1,0:T(8,128)(2,1)}, f32[4,2,4,256,128]{4,3,2,1,0:T(8,128)}, bf16[2,2,4,256,128]{4,3,2,1,0:T(8,128...) custom-call(s32[2]{0:T(128)} %copy-done.7, ...), custom_call_target="tpu_custom_call" | custom-call | flops 8053063680 | bytes 25165824 | tf_op jit(solution)/shard_map/attend/pallas_call | solution.py:426
  86.1 1.3 collective-permute-start.8
  87.4 4.1 %collective-permute-start.9 = (bf16[2,2,4,256,128]{4,3,2,1,0:T(8,128)(2,1)}, bf16[2,2,4,256,128]{4,3,2,1,0:T(8,128)(2,1)S(1)}, u32[]{:S(2)}, u32[]{:S(2)}) collective-permute-start(bf16[2,2,4,256,128]{4,3,2,1,0:T(8,128)(2,1)} %get-tuple-element.104), channel_id=1, source_target_pairs={{0,8},{8,16},{16,24},{24,32},{32,40},{40,48},{48,56},{56,64},{64,7... | collective-permute-start | bytes 3145736 | tf_op jit(solution)/shard_map/ppermute | solution.py:408
  94.2 2.1 %collective-permute-start.5 = (bf16[272,512]{1,0:T(8,128)(2,1)S(1)}, bf16[272,512]{1,0:T(8,128)(2,1)S(1)}, u32[]{:S(2)}, u32[]{:S(2)}) collective-permute-start(bf16[272,512]{1,0:T(8,128)(2,1)S(1)} %get-tuple-element.90), channel_id=1, source_target_pairs={{0,2},{1,3},{2,4},{3,5},{4,6},{5,7},{6,0},{7,1},{8,10},{9,11},{10,... | collective-permute-start | bytes 835592 | tf_op jit(solution)/shard_map/ppermute | solution.py:508
  96.3 2.8 %collective-permute-start.6 = (bf16[272,512]{1,0:T(8,128)(2,1)S(1)}, bf16[272,512]{1,0:T(8,128)(2,1)S(1)}, u32[]{:S(2)}, u32[]{:S(2)}) collective-permute-start(bf16[272,512]{1,0:T(8,128)(2,1)S(1)} %get-tuple-element.91), channel_id=1, source_target_pairs={{0,4},{1,5},{2,6},{3,7},{4,0},{5,1},{6,2},{7,3},{8,12},{9,13},{10,... | collective-permute-start | bytes 835592 | tf_op jit(solution)/shard_map/ppermute | solution.py:508
  99.2 4.9 %branch_rows.1 = (bf16[1024,512]{1,0:T(8,128)(2,1)}, f32[1024,512]{1,0:T(8,128)S(1)}) custom-call(s32[1,1024]{1,0:T(1,128)S(1)} %bitcast.23, bf16[512,1024]{1,0:T(8,128)(2,1)S(1)} %copy-done.2, bf16[512,512]{1,0:T(8,128)(2,1)S(1)} %copy-done.12, bf16[512,1024]{1,0:T(8,128)(2,1)S(1)} %copy-done.14, bf16[512,1024]{1,0:T(8,128)(2,1)S(1)} %copy-done.15), custom_call_target="tpu_custom_call" | custom-call | flops 3221225472 | bytes 7340032 | tf_op jit(solution)/shard_map/branch_rows/pallas_call | solution.py:426
  104.1 1.3 copy-done
  105.5 6.1 %collective-permute-done.6 = bf16[272,512]{1,0:T(8,128)(2,1)S(1)} collective-permute-done((bf16[272,512]{1,0:T(8,128)(2,1)S(1)}, bf16[272,512]{1,0:T(8,128)(2,1)S(1)}, u32[]{:S(2)}, u32[]{:S(2)}) %collective-permute-start.6) | collective-permute-done | bytes 278560 | tf_op jit(solution)/shard_map/ppermute | solution.py:508
  111.6 3.0 %collective-permute-start.13 = (bf16[2,2,4,256,128]{4,3,2,1,0:T(8,128)(2,1)S(1)}, bf16[2,2,4,256,128]{4,3,2,1,0:T(8,128)(2,1)S(1)}, u32[]{:S(2)}, u32[]{:S(2)}) collective-permute-start(bf16[2,2,4,256,128]{4,3,2,1,0:T(8,128)(2,1)S(1)} %copy-done.21), channel_id=1, source_target_pairs={{1,0},{2,1},{3,2},{4,3},{5,4},{6,5},{7,6},{9,8},{10,9},{11,10},{12... | collective-permute-start | bytes 3145736 | tf_op jit(solution)/shard_map/ppermute | solution.py:408
  114.7 2.5 %collective-permute-start.14 = (bf16[2,2,4,256,128]{4,3,2,1,0:T(8,128)(2,1)S(1)}, bf16[2,2,4,256,128]{4,3,2,1,0:T(8,128)(2,1)S(1)}, u32[]{:S(2)}, u32[]{:S(2)}) collective-permute-start(bf16[2,2,4,256,128]{4,3,2,1,0:T(8,128)(2,1)S(1)} %copy-done.20), channel_id=1, source_target_pairs={{0,1},{1,2},{2,3},{3,4},{4,5},{5,6},{6,7},{8,9},{9,10},{10,11},{11... | collective-permute-start | bytes 3145736 | tf_op jit(solution)/shard_map/ppermute | solution.py:408
  117.5 15.8 %all_to_all.10 = bf16[16,16,640]{2,1,0:T(8,128)(2,1)S(1)} all-to-all(bf16[16,16,640]{2,1,0:T(8,128)(2,1)S(1)} %pad_maximum_fusion), channel_id=1, replica_groups=mesh['bx'=16,'by'=8] {'bx'}, dimensions={0} | all-to-all | bytes 655360 | tf_op jit(solution)/shard_map/all_to_all | solution.py:417
  133.4 10.7 %all_to_all.11 = bf16[16,16,512]{2,1,0:T(8,128)(2,1)S(1)} all-to-all(bf16[16,16,512]{2,1,0:T(8,128)(2,1)S(1)} %broadcast_in_dim.28), channel_id=1, replica_groups=mesh['bx'=16,'by'=8] {'bx'}, dimensions={0} | all-to-all | bytes 524288 | tf_op jit(solution)/shard_map/all_to_all | solution.py:421
  144.1 2.7 %collective-permute-start.12 = (bf16[256,512]{1,0:T(8,128)(2,1)S(1)}, bf16[256,512]{1,0:T(8,128)(2,1)S(1)}, u32[]{:S(2)}, u32[]{:S(2)}) collective-permute-start(bf16[256,512]{1,0:T(8,128)(2,1)S(1)} %bitcast.13), channel_id=1, source_target_pairs={{0,6},{1,7},{2,0},{3,1},{4,2},{5,3},{6,4},{7,5},{8,14},{9,15},{10,... | collective-permute-start | bytes 786440 | tf_op jit(solution)/shard_map/ppermute | solution.py:508
  146.9 1.3 collective-permute-start.11
  150.4 12.2 %token_rows.1 = f32[1024,512]{1,0:T(8,128)} custom-call(s32[2]{0:T(128)} %copy-done.7, s32[2048]{0:T(1024)} %copy-done.4, s32[512]{0:T(512)} %copy-done.6, s32[1,1024]{1,0:T(1,128)} %bitcast.21, bf16[1024,512]{1,0:T(8,128)(2,1)} %bitcast.18, f32[1,512]{1,0:T(1,128)} %bitcast.29, bf16[512,1024]{1,0:T(8,128)(2,1)} %w_qk.5, bf16[512,512]{1,0:T(8,128)(2,1)} %w_v.3, ...), custom_call_target="tpu_custom_call" | custom-call | flops 3221225472 | bytes 16777216 | tf_op jit(solution)/shard_map/token_rows/pallas_call | solution.py:426
  162.6 2.9 %collective-permute-start.15 = (bf16[256,512]{1,0:T(8,128)(2,1)S(1)}, bf16[256,512]{1,0:T(8,128)(2,1)S(1)}, u32[]{:S(2)}, u32[]{:S(2)}) collective-permute-start(bf16[256,512]{1,0:T(8,128)(2,1)S(1)} %bitcast.16), channel_id=1, source_target_pairs={{0,1},{1,0},{2,3},{3,2},{4,5},{5,4},{6,7},{7,6},{8,9},{9,8},{10,11... | collective-permute-start | bytes 786440 | tf_op jit(solution)/shard_map/ppermute | solution.py:511
  167.8 2.8 %weight_grads.1 = (f32[512,1024]{1,0:T(8,128)}, f32[512,512]{1,0:T(8,128)}, f32[512,512]{1,0:T(8,128)}) custom-call(s32[2]{0:T(128)S(1)} %copy-done.9, bf16[256,512]{1,0:T(8,128)(2,1)S(1)} %bitcast.17, bf16[256,512]{1,0:T(8,128)(2,1)S(1)} %collective-permute-done.10.refs_1_, bf16[256,512]{1,0:T(8,128)(2,1)S(1)} %collective-permute-done.11.refs_2_, ...), custom_call_target="tpu_custom_call" | custom-call | bytes 6291456 | tf_op jit(solution)/shard_map/weight_grads/pallas_call | solution.py:426
  (89 shorter events, 13.5 us)
Async XLA Ops:
  9.1 19.4 %collective-permute-start = (bf16[512,512]{1,0:T(8,128)(2,1)S(1)}, bf16[512,512]{1,0:T(8,128)(2,1)S(1)}, u32[]{:S(2)}, u32[]{:S(2)}) collective-permute-start(bf16[512,512]{1,0:T(8,128)(2,1)S(1)} %get-tuple-element.71), channel_id=1, source_target_pairs={{0,8},{8,16},{16,24},{24,32},{32,40},{40,48},{48,56},{56,64},{64,7... | collective-permute-start | bytes 1572872 | tf_op jit(solution)/shard_map/ppermute | solution.py:408
  13.5 15.0 %collective-permute-start.1 = (bf16[512,512]{1,0:T(8,128)(2,1)S(1)}, bf16[512,512]{1,0:T(8,128)(2,1)S(1)}, u32[]{:S(2)}, u32[]{:S(2)}) collective-permute-start(bf16[512,512]{1,0:T(8,128)(2,1)S(1)} %get-tuple-element.72), channel_id=1, source_target_pairs={{8,0},{16,8},{24,16},{32,24},{40,32},{48,40},{56,48},{64,56},{72,6... | collective-permute-start | bytes 1572872 | tf_op jit(solution)/shard_map/ppermute | solution.py:408
  14.8 13.7 %collective-permute-start.2 = (bf16[512,512]{1,0:T(8,128)(2,1)S(1)}, bf16[512,512]{1,0:T(8,128)(2,1)S(1)}, u32[]{:S(2)}, u32[]{:S(2)}) collective-permute-start(bf16[512,512]{1,0:T(8,128)(2,1)S(1)} %get-tuple-element.73), channel_id=1, source_target_pairs={{0,1},{1,2},{2,3},{3,4},{4,5},{5,6},{6,7},{8,9},{9,10},{10,11},{11... | collective-permute-start | bytes 1572872 | tf_op jit(solution)/shard_map/ppermute | solution.py:408
  18.8 10.6 %collective-permute-start.3 = (bf16[512,512]{1,0:T(8,128)(2,1)S(1)}, bf16[512,512]{1,0:T(8,128)(2,1)S(1)}, u32[]{:S(2)}, u32[]{:S(2)}) collective-permute-start(bf16[512,512]{1,0:T(8,128)(2,1)S(1)} %get-tuple-element.74), channel_id=1, source_target_pairs={{1,0},{2,1},{3,2},{4,3},{5,4},{6,5},{7,6},{9,8},{10,9},{11,10},{12... | collective-permute-start | bytes 1572872 | tf_op jit(solution)/shard_map/ppermute | solution.py:408
  30.2 61.2 %copy-start.8 = (s32[2]{0:T(128)S(1)}, s32[2]{0:T(128)}, u32[]{:S(2)}) copy-start(s32[2]{0:T(128)} %copy-done.7) | copy-start | bytes 28
  30.2 68.9 %copy-start.2 = (bf16[512,1024]{1,0:T(8,128)(2,1)S(1)}, bf16[512,1024]{1,0:T(8,128)(2,1)}, u32[]{:S(2)}) copy-start(bf16[512,1024]{1,0:T(8,128)(2,1)} %w_qk.5) | copy-start | bytes 3145732
  30.2 68.9 %copy-start.12 = (bf16[512,512]{1,0:T(8,128)(2,1)S(1)}, bf16[512,512]{1,0:T(8,128)(2,1)}, u32[]{:S(2)}) copy-start(bf16[512,512]{1,0:T(8,128)(2,1)} %w_out.3) | copy-start | bytes 1572868
  86.0 5.5 %collective-permute-start.4 = (bf16[1040,512]{1,0:T(8,128)(2,1)}, bf16[1040,512]{1,0:T(8,128)(2,1)S(1)}, u32[]{:S(2)}, u32[]{:S(2)}) collective-permute-start(bf16[1040,512]{1,0:T(8,128)(2,1)} %get-tuple-element.87), channel_id=1, source_target_pairs={{0,1},{1,0},{2,3},{3,2},{4,5},{5,4},{6,7},{7,6},{8,9},{9,8},{10,11... | collective-permute-start | bytes 3194888 | tf_op jit(solution)/shard_map/ppermute | solution.py:498
  86.1 31.3 %collective-permute-start.8 = (bf16[2,2,4,256,128]{4,3,2,1,0:T(8,128)(2,1)}, bf16[2,2,4,256,128]{4,3,2,1,0:T(8,128)(2,1)S(1)}, u32[]{:S(2)}, u32[]{:S(2)}) collective-permute-start(bf16[2,2,4,256,128]{4,3,2,1,0:T(8,128)(2,1)} %get-tuple-element.103), channel_id=1, source_target_pairs={{8,0},{16,8},{24,16},{32,24},{40,32},{48,40},{56,48},{64,56},{72,6... | collective-permute-start | bytes 3145736 | tf_op jit(solution)/shard_map/ppermute | solution.py:408
  87.4 30.0 %collective-permute-start.9 = (bf16[2,2,4,256,128]{4,3,2,1,0:T(8,128)(2,1)}, bf16[2,2,4,256,128]{4,3,2,1,0:T(8,128)(2,1)S(1)}, u32[]{:S(2)}, u32[]{:S(2)}) collective-permute-start(bf16[2,2,4,256,128]{4,3,2,1,0:T(8,128)(2,1)} %get-tuple-element.104), channel_id=1, source_target_pairs={{0,8},{8,16},{16,24},{24,32},{32,40},{40,48},{48,56},{56,64},{64,7... | collective-permute-start | bytes 3145736 | tf_op jit(solution)/shard_map/ppermute | solution.py:408
  94.2 11.2 %collective-permute-start.5 = (bf16[272,512]{1,0:T(8,128)(2,1)S(1)}, bf16[272,512]{1,0:T(8,128)(2,1)S(1)}, u32[]{:S(2)}, u32[]{:S(2)}) collective-permute-start(bf16[272,512]{1,0:T(8,128)(2,1)S(1)} %get-tuple-element.90), channel_id=1, source_target_pairs={{0,2},{1,3},{2,4},{3,5},{4,6},{5,7},{6,0},{7,1},{8,10},{9,11},{10,... | collective-permute-start | bytes 835592 | tf_op jit(solution)/shard_map/ppermute | solution.py:508
  96.3 15.3 %collective-permute-start.6 = (bf16[272,512]{1,0:T(8,128)(2,1)S(1)}, bf16[272,512]{1,0:T(8,128)(2,1)S(1)}, u32[]{:S(2)}, u32[]{:S(2)}) collective-permute-start(bf16[272,512]{1,0:T(8,128)(2,1)S(1)} %get-tuple-element.91), channel_id=1, source_target_pairs={{0,4},{1,5},{2,6},{3,7},{4,0},{5,1},{6,2},{7,3},{8,12},{9,13},{10,... | collective-permute-start | bytes 835592 | tf_op jit(solution)/shard_map/ppermute | solution.py:508
  99.2 12.4 %collective-permute-start.7 = (bf16[272,512]{1,0:T(8,128)(2,1)S(1)}, bf16[272,512]{1,0:T(8,128)(2,1)S(1)}, u32[]{:S(2)}, u32[]{:S(2)}) collective-permute-start(bf16[272,512]{1,0:T(8,128)(2,1)S(1)} %get-tuple-element.92), channel_id=1, source_target_pairs={{0,6},{1,7},{2,0},{3,1},{4,2},{5,3},{6,4},{7,5},{8,14},{9,15},{10,... | collective-permute-start | bytes 835592 | tf_op jit(solution)/shard_map/ppermute | solution.py:508
  111.6 37.4 %collective-permute-start.13 = (bf16[2,2,4,256,128]{4,3,2,1,0:T(8,128)(2,1)S(1)}, bf16[2,2,4,256,128]{4,3,2,1,0:T(8,128)(2,1)S(1)}, u32[]{:S(2)}, u32[]{:S(2)}) collective-permute-start(bf16[2,2,4,256,128]{4,3,2,1,0:T(8,128)(2,1)S(1)} %copy-done.21), channel_id=1, source_target_pairs={{1,0},{2,1},{3,2},{4,3},{5,4},{6,5},{7,6},{9,8},{10,9},{11,10},{12... | collective-permute-start | bytes 3145736 | tf_op jit(solution)/shard_map/ppermute | solution.py:408
  114.7 34.3 %collective-permute-start.14 = (bf16[2,2,4,256,128]{4,3,2,1,0:T(8,128)(2,1)S(1)}, bf16[2,2,4,256,128]{4,3,2,1,0:T(8,128)(2,1)S(1)}, u32[]{:S(2)}, u32[]{:S(2)}) collective-permute-start(bf16[2,2,4,256,128]{4,3,2,1,0:T(8,128)(2,1)S(1)} %copy-done.20), channel_id=1, source_target_pairs={{0,1},{1,2},{2,3},{3,4},{4,5},{5,6},{6,7},{8,9},{9,10},{10,11},{11... | collective-permute-start | bytes 3145736 | tf_op jit(solution)/shard_map/ppermute | solution.py:408
  117.4 31.6 %copy-start.16 = (bf16[2,2,4,256,128]{4,3,2,1,0:T(8,128)(2,1)}, bf16[2,2,4,256,128]{4,3,2,1,0:T(8,128)(2,1)S(1)}, u32[]{:S(2)}) copy-start(bf16[2,2,4,256,128]{4,3,2,1,0:T(8,128)(2,1)S(1)} %collective-permute-done.8.b0) | copy-start | bytes 3145732
  117.4 31.6 %copy-start.17 = (bf16[2,2,4,256,128]{4,3,2,1,0:T(8,128)(2,1)}, bf16[2,2,4,256,128]{4,3,2,1,0:T(8,128)(2,1)S(1)}, u32[]{:S(2)}) copy-start(bf16[2,2,4,256,128]{4,3,2,1,0:T(8,128)(2,1)S(1)} %collective-permute-done.9.b1) | copy-start | bytes 3145732
  144.1 18.5 %collective-permute-start.12 = (bf16[256,512]{1,0:T(8,128)(2,1)S(1)}, bf16[256,512]{1,0:T(8,128)(2,1)S(1)}, u32[]{:S(2)}, u32[]{:S(2)}) collective-permute-start(bf16[256,512]{1,0:T(8,128)(2,1)S(1)} %bitcast.13), channel_id=1, source_target_pairs={{0,6},{1,7},{2,0},{3,1},{4,2},{5,3},{6,4},{7,5},{8,14},{9,15},{10,... | collective-permute-start | bytes 786440 | tf_op jit(solution)/shard_map/ppermute | solution.py:508
  146.9 15.7 %collective-permute-start.11 = (bf16[256,512]{1,0:T(8,128)(2,1)S(1)}, bf16[256,512]{1,0:T(8,128)(2,1)S(1)}, u32[]{:S(2)}, u32[]{:S(2)}) collective-permute-start(bf16[256,512]{1,0:T(8,128)(2,1)S(1)} %bitcast.14), channel_id=1, source_target_pairs={{0,4},{1,5},{2,6},{3,7},{4,0},{5,1},{6,2},{7,3},{8,12},{9,13},{10,... | collective-permute-start | bytes 786440 | tf_op jit(solution)/shard_map/ppermute | solution.py:508
  148.1 14.5 %collective-permute-start.10 = (bf16[256,512]{1,0:T(8,128)(2,1)S(1)}, bf16[256,512]{1,0:T(8,128)(2,1)S(1)}, u32[]{:S(2)}, u32[]{:S(2)}) collective-permute-start(bf16[256,512]{1,0:T(8,128)(2,1)S(1)} %bitcast.15), channel_id=1, source_target_pairs={{0,2},{1,3},{2,4},{3,5},{4,6},{5,7},{6,0},{7,1},{8,10},{9,11},{10,... | collective-permute-start | bytes 786440 | tf_op jit(solution)/shard_map/ppermute | solution.py:508
  162.6 4.1 %collective-permute-start.15 = (bf16[256,512]{1,0:T(8,128)(2,1)S(1)}, bf16[256,512]{1,0:T(8,128)(2,1)S(1)}, u32[]{:S(2)}, u32[]{:S(2)}) collective-permute-start(bf16[256,512]{1,0:T(8,128)(2,1)S(1)} %bitcast.16), channel_id=1, source_target_pairs={{0,1},{1,0},{2,3},{3,2},{4,5},{5,4},{6,7},{7,6},{8,9},{9,8},{10,11... | collective-permute-start | bytes 786440 | tf_op jit(solution)/shard_map/ppermute | solution.py:511
  165.5 1.5 collective-permute-start.16
  165.6 1.8 %collective-permute-start.17 = (bf16[256,512]{1,0:T(8,128)(2,1)S(1)}, bf16[256,512]{1,0:T(8,128)(2,1)S(1)}, u32[]{:S(2)}, u32[]{:S(2)}) collective-permute-start(bf16[256,512]{1,0:T(8,128)(2,1)S(1)} %collective-permute-done.11.refs_2_), channel_id=1, source_target_pairs={{0,1},{1,0},{2,3},{3,2},{4,5},{5,4},{6,7},{7,6},{8,9},{9,8},{10,11... | collective-permute-start | bytes 786440 | tf_op jit(solution)/shard_map/ppermute | solution.py:511
  166.0 1.8 %collective-permute-start.18 = (bf16[256,512]{1,0:T(8,128)(2,1)S(1)}, bf16[256,512]{1,0:T(8,128)(2,1)S(1)}, u32[]{:S(2)}, u32[]{:S(2)}) collective-permute-start(bf16[256,512]{1,0:T(8,128)(2,1)S(1)} %collective-permute-done.12.refs_3_), channel_id=1, source_target_pairs={{0,1},{1,0},{2,3},{3,2},{4,5},{5,4},{6,7},{7,6},{8,9},{9,8},{10,11... | collective-permute-start | bytes 786440 | tf_op jit(solution)/shard_map/ppermute | solution.py:511
  (21 other events, 139.6 us)

commit v4 on v3

--- a/solution.py
+++ b/solution.py
@@ -14,6 +14,7 @@
 F32 = jnp.float32
 MIB = 1 << 20
 LIMIT = 58
+WIDE = 512
 VM = pl.BlockSpec(memory_space=pltpu.VMEM)
 SM = pl.BlockSpec(memory_space=pltpu.SMEM)
 AN = pl.BlockSpec(memory_space=pl.ANY)
@@ -156,10 +157,11 @@
                   qn_in, qt_in, kn_in, kt_in, vn_in, vt_in, gn_in, gt_in, sc_in, nt_in,
                   ctx_out, dq_out, own, h0, h1, h2, h3, keep, send, gain_out,
                   far, w_qk, w_v, qn, qt, gn, gt, pkn, pkt, pvn, pvt, sc, n_t, ctx_t, dq_t, acc,
-                  s_scr, dp_scr, p_scr, ds_scr, terms, where_ref, sem_in, sem_out):
+                  s_scr, dp_scr, p_a, ds_a, p_b, ds_b, terms, where_ref, sem_in, sem_out):
     extent_x, extent_y, blocks, slots = dims
     d = w_v.shape[0]
     mine = pl.ds(0, blocks)
+    scratch = ((p_a, ds_a), (p_b, ds_b))
     first, later = [], []
 
     def fetch(src, dst, into):
@@ -199,7 +201,7 @@
                 tra[blocks + i, p] = mat_t[p * PAIR : (p + 1) * PAIR, :]
         return 0
 
-    lax.fori_loop(0, 8, remote, 0)
+    lax.fori_loop(0, 8, remote, 0, unroll=2)
     for copy in later:
         copy.wait()
     lane = lax.broadcasted_iota(jnp.int32, (1, PAIR), 1)
@@ -214,7 +216,7 @@
             axis=0,
         )
 
-    def pair(b, p, at):
+    def weigh(b, p, at, p_scr, ds_scr):
         q_diag, g_diag = diagonal(qt[b, p]), diagonal(gt[b, p])
         top = None
         for j, k in enumerate(at):
@@ -237,6 +239,8 @@
             prob = s_scr[j] * scale
             p_scr[j] = prob.astype(BF)
             ds_scr[j] = (prob * (dp_scr[j] - centre)).astype(BF)
+
+    def spread(b, p, at, p_scr, ds_scr):
         q_rows = qn[b, p]
         g_rows = gn[b, p]
         q_mask = jnp.concatenate([q_rows * low_lanes, q_rows * high_lanes], axis=0)
@@ -266,7 +270,15 @@
             @pl.when(count == live)
             def _():
                 at = [b] + [where_ref[b * slots + j] for j in range(live)]
-                lax.fori_loop(0, np_, lambda p, c: (pair(b, p, at), c)[1], 0)
+
+                def two(i, c):
+                    for k, scr in enumerate(scratch):
+                        weigh(b, 2 * i + k, at, *scr)
+                    for k, scr in enumerate(scratch):
+                        spread(b, 2 * i + k, at, *scr)
+                    return c
+
+                lax.fori_loop(0, np_ // 2, two, 0)
 
         return 0
 
@@ -345,15 +357,15 @@
     d = w_out.shape[0]
 
     def body(a, _):
-        rows = pl.ds(pl.multiple_of(a * BLK, BLK), BLK)
-        back = one_hot_back(order, a * BLK, BLK)
+        rows = pl.ds(pl.multiple_of(a * WIDE, WIDE), WIDE)
+        back = one_hot_back(order, a * WIDE, WIDE)
         ctx = mm_nt(back, ctx_t[...]).astype(BF)
         dq = mm_nt(back, dq_t[...]).astype(BF)
         out[rows, :] = mm(ctx, w_out[...]).astype(BF)
         part[rows, :] = mm_nt(dq, w_qk[:, :d])
         return 0
 
-    lax.fori_loop(0, out.shape[0] // BLK, body, 0)
+    lax.fori_loop(0, out.shape[0] // WIDE, body, 0)
 
 
 def rows_kernel(dims, np_, pos, ids, cnt, order, tok, gain, w_qk, w_v, part, own, b0, b1, b2, b3,
@@ -373,8 +385,8 @@
                 rows_scr[b * BLK : (b + 1) * BLK, lo : lo + PAIR] = acc[b, half, p].astype(BF)
 
     def body(a, _):
-        rows = pl.ds(pl.multiple_of(a * BLK, BLK), BLK)
-        back = one_hot_back(order, a * BLK, BLK)
+        rows = pl.ds(pl.multiple_of(a * WIDE, WIDE), WIDE)
+        back = one_hot_back(order, a * WIDE, WIDE)
         mine = mm(back, rows_scr[...]).astype(BF)
         grad = part[rows, :] + mm_nt(mine[:, :d], w_qk[:, d:]) + mm_nt(mine[:, d:], w_v[...])
         values, inv = rms(tok[rows, :])
@@ -383,7 +395,7 @@
         out[rows, :] = inv * u - values * (inv * inv * inv * mean)
         return 0
 
-    lax.fori_loop(0, out.shape[0] // BLK, body, 0)
+    lax.fori_loop(0, out.shape[0] // WIDE, body, 0)
 
 
 def place_kernel(pos, *refs):
@@ -488,8 +500,8 @@
         + [vmem(nat, BF), vmem(tra, BF)] * 2
         + [vmem((pool,) + nat[1:], BF), vmem((pool,) + tra[1:], BF)] * 2
         + [vmem((n, d), BF), vmem((d, pool * BLK), BF)] + [vmem((d, n), BF)] * 2
-        + [vmem((pool, 2) + nat[1:], F32), vmem(tile, F32), vmem(tile, F32), vmem(tile, BF), vmem(tile, BF),
-           vmem((2, n + 16, d), BF), pltpu.SMEM((blocks * slots,), jnp.int32),
+        + [vmem((pool, 2) + nat[1:], F32)] + [vmem(tile, F32)] * 2 + [vmem(tile, BF)] * 4
+        + [vmem((2, n + 16, d), BF), pltpu.SMEM((blocks * slots,), jnp.int32),
            pltpu.SemaphoreType.DMA((20,)), pltpu.SemaphoreType.DMA((13,))],
         LIMIT, 12 * blocks * 5 * BLK * BLK * d, 24 << 20, blocks * 5 * BLK * BLK * 8,
         out_specs=[AN] * 9 + [VM],

time: 172 us -> 168 us (0.977)
  Pallas kernels: 87.1 us -> 82.4 us
  blocking collectives: 26.6 us -> 28.7 us
    pallas_call x7, Pallas kernels: 87.1 us -> 82.4 us  [call(): pl.pallas_call(kernel, out_shape=outs, grid=grid, in_specs=specs, out_spe...]
  transfers between devices with their start and end apart: 19 -> 19, of which waited for: 5 -> 5; matrix products, arithmetic and copies ran while one was open for 0% -> 1% of each run, Pallas kernels for 15% -> 15%
where the time goes in v4:
time: 168 us; the launch traced here: 167 us
  Pallas kernels  82.4 us (49%)
  starting transfers between devices  35 us (21%)
  blocking collectives  28.7 us (17%)
  local copies, waits for them, and re-layouts  11.3 us (7%)
  waiting for transfers between devices  8.37 us (5%)
    pallas_call x7, Pallas kernels, call(): pl.pallas_call(kernel, out_shape=outs, grid=grid, in_specs=specs, out_spe...  82.4 us
    ppermute x8, starting transfers between devices, step_to(): return lax.ppermute(block, axis, route)  22.8 us
    all_to_all x1, blocking collectives, across_x(): got = lax.all_to_all(parts, 'bx', 0, 0, tiled=True)  17.5 us
    all_to_all x1, blocking collectives, across_x(): lax.all_to_all(jnp.broadcast_to(mine[None], (count,) + mine.shape), 'bx',...  11.2 us
    unnamed x54, local copies, waits for them, and re-layouts  10.4 us
    ppermute x6, starting transfers between devices, along_y(): lax.ppermute(rows, 'by', [(i, (i + 2 * s) % extent_y) for i in range(exte...  8.77 us
    ppermute x6, waiting for transfers between devices, along_y(): lax.ppermute(rows, 'by', [(i, (i + 2 * s) % extent_y) for i in range(exte...  6.31 us
  transfers between devices with their start and end apart: 19, of which 5 were waited for; matrix products, arithmetic and copies ran while one was open for 1% of the time, Pallas kernels for 15%

profile of v4, /device:TPU:1, one launch (start us, length us, event | category | flops | bytes accessed | tf_op | source)
XLA Modules:
  0.0 167.2 jit_solution(4381680274646884776)
XLA Ops:
  3.1 1.2 copy-done.3
  5.1 3.0 %sort_rows.1 = (bf16[1024,512]{1,0:T(8,128)(2,1)S(1)}, bf16[512,512]{1,0:T(8,128)(2,1)S(1)}, bf16[512,512]{1,0:T(8,128)(2,1)S(1)}, bf16[512,512]{1,0:T(8,128)(2,1)S(1)}, bf16[512,512]{1,0:T(8,128)(2,1)S(1)}) custom-call(s32[2]{0:T(128)S(1)} %pad_add_fusion.pos, s32[2048]{0:T(1024)S(1)} %reshape.59.ids, s32[512]{0:T(512)S(1)} %reshape.60.cnt, ...), custom_call_target="tpu_custom_call" | custom-call | flops 1073741824 | bytes 4194304 | tf_op jit(solution)/shard_map/sort_rows/pallas_call | solution.py:438
  9.1 4.4 %collective-permute-start = (bf16[512,512]{1,0:T(8,128)(2,1)S(1)}, bf16[512,512]{1,0:T(8,128)(2,1)S(1)}, u32[]{:S(2)}, u32[]{:S(2)}) collective-permute-start(bf16[512,512]{1,0:T(8,128)(2,1)S(1)} %get-tuple-element.71), channel_id=1, source_target_pairs={{0,8},{8,16},{16,24},{24,32},{32,40},{40,48},{48,56},{56,64},{64,7... | collective-permute-start | bytes 1572872 | tf_op jit(solution)/shard_map/ppermute | solution.py:420
  13.5 1.3 collective-permute-start.1
  14.8 4.0 %collective-permute-start.2 = (bf16[512,512]{1,0:T(8,128)(2,1)S(1)}, bf16[512,512]{1,0:T(8,128)(2,1)S(1)}, u32[]{:S(2)}, u32[]{:S(2)}) collective-permute-start(bf16[512,512]{1,0:T(8,128)(2,1)S(1)} %get-tuple-element.73), channel_id=1, source_target_pairs={{0,1},{1,2},{2,3},{3,4},{4,5},{5,6},{6,7},{8,9},{9,10},{10,11},{11... | collective-permute-start | bytes 1572872 | tf_op jit(solution)/shard_map/ppermute | solution.py:420
  18.8 1.9 %collective-permute-start.3 = (bf16[512,512]{1,0:T(8,128)(2,1)S(1)}, bf16[512,512]{1,0:T(8,128)(2,1)S(1)}, u32[]{:S(2)}, u32[]{:S(2)}) collective-permute-start(bf16[512,512]{1,0:T(8,128)(2,1)S(1)} %get-tuple-element.74), channel_id=1, source_target_pairs={{1,0},{2,1},{3,2},{4,3},{5,4},{6,5},{7,6},{9,8},{10,9},{11,10},{12... | collective-permute-start | bytes 1572872 | tf_op jit(solution)/shard_map/ppermute | solution.py:420
  20.7 7.7 %project.1 = (bf16[1024,512]{1,0:T(8,128)(2,1)}, bf16[4,512,256]{2,1,0:T(8,128)(2,1)}, bf16[4,4,256,128]{3,2,1,0:T(8,128)(2,1)}, bf16[4,4,128,256]{3,2,1,0:T(8,1...) custom-call(s32[1,1024]{1,0:T(1,128)} %bitcast.20, ...), custom_call_target="tpu_custom_call" | custom-call | flops 3221225472 | bytes 14680064 | tf_op jit(solution)/shard_map/project/pallas_call | solution.py:438
  30.3 51.7 %attend.1 = (bf16[512,1024]{1,0:T(8,128)(2,1)}, bf16[512,1024]{1,0:T(8,128)(2,1)}, f32[4,2,4,256,128]{4,3,2,1,0:T(8,128)}, bf16[2,2,4,256,128]{4,3,2,1,0:T(8,128...) custom-call(s32[2]{0:T(128)} %copy-done.7, ...), custom_call_target="tpu_custom_call" | custom-call | flops 8053063680 | bytes 25165824 | tf_op jit(solution)/shard_map/attend/pallas_call | solution.py:438
  82.0 1.3 collective-permute-start.8
  83.3 4.1 %collective-permute-start.9 = (bf16[2,2,4,256,128]{4,3,2,1,0:T(8,128)(2,1)}, bf16[2,2,4,256,128]{4,3,2,1,0:T(8,128)(2,1)S(1)}, u32[]{:S(2)}, u32[]{:S(2)}) collective-permute-start(bf16[2,2,4,256,128]{4,3,2,1,0:T(8,128)(2,1)} %get-tuple-element.104), channel_id=1, source_target_pairs={{0,8},{8,16},{16,24},{24,32},{32,40},{40,48},{48,56},{56,64},{64,7... | collective-permute-start | bytes 3145736 | tf_op jit(solution)/shard_map/ppermute | solution.py:420
  87.4 1.2 copy-done.1
  90.1 2.3 %collective-permute-start.5 = (bf16[272,512]{1,0:T(8,128)(2,1)S(1)}, bf16[272,512]{1,0:T(8,128)(2,1)S(1)}, u32[]{:S(2)}, u32[]{:S(2)}) collective-permute-start(bf16[272,512]{1,0:T(8,128)(2,1)S(1)} %get-tuple-element.90), channel_id=1, source_target_pairs={{0,2},{1,3},{2,4},{3,5},{4,6},{5,7},{6,0},{7,1},{8,10},{9,11},{10,... | collective-permute-start | bytes 835592 | tf_op jit(solution)/shard_map/ppermute | solution.py:520
  92.5 2.4 %collective-permute-start.6 = (bf16[272,512]{1,0:T(8,128)(2,1)S(1)}, bf16[272,512]{1,0:T(8,128)(2,1)S(1)}, u32[]{:S(2)}, u32[]{:S(2)}) collective-permute-start(bf16[272,512]{1,0:T(8,128)(2,1)S(1)} %get-tuple-element.91), channel_id=1, source_target_pairs={{0,4},{1,5},{2,6},{3,7},{4,0},{5,1},{6,2},{7,3},{8,12},{9,13},{10,... | collective-permute-start | bytes 835592 | tf_op jit(solution)/shard_map/ppermute | solution.py:520
  95.0 4.4 %branch_rows.1 = (bf16[1024,512]{1,0:T(8,128)(2,1)}, f32[1024,512]{1,0:T(8,128)S(1)}) custom-call(s32[1,1024]{1,0:T(1,128)S(1)} %bitcast.23, bf16[512,1024]{1,0:T(8,128)(2,1)S(1)} %copy-done.2, bf16[512,512]{1,0:T(8,128)(2,1)S(1)} %copy-done.12, bf16[512,1024]{1,0:T(8,128)(2,1)S(1)} %copy-done.14, bf16[512,1024]{1,0:T(8,128)(2,1)S(1)} %copy-done.15), custom_call_target="tpu_custom_call" | custom-call | flops 3221225472 | bytes 7340032 | tf_op jit(solution)/shard_map/branch_rows/pallas_call | solution.py:438
  99.4 1.3 copy-done
  100.7 6.3 %collective-permute-done.6 = bf16[272,512]{1,0:T(8,128)(2,1)S(1)} collective-permute-done((bf16[272,512]{1,0:T(8,128)(2,1)S(1)}, bf16[272,512]{1,0:T(8,128)(2,1)S(1)}, u32[]{:S(2)}, u32[]{:S(2)}) %collective-permute-start.6) | collective-permute-done | bytes 278560 | tf_op jit(solution)/shard_map/ppermute | solution.py:520
  107.0 3.3 %collective-permute-start.13 = (bf16[2,2,4,256,128]{4,3,2,1,0:T(8,128)(2,1)S(1)}, bf16[2,2,4,256,128]{4,3,2,1,0:T(8,128)(2,1)S(1)}, u32[]{:S(2)}, u32[]{:S(2)}) collective-permute-start(bf16[2,2,4,256,128]{4,3,2,1,0:T(8,128)(2,1)S(1)} %copy-done.21), channel_id=1, source_target_pairs={{1,0},{2,1},{3,2},{4,3},{5,4},{6,5},{7,6},{9,8},{10,9},{11,10},{12... | collective-permute-start | bytes 3145736 | tf_op jit(solution)/shard_map/ppermute | solution.py:420
  110.3 2.5 %collective-permute-start.14 = (bf16[2,2,4,256,128]{4,3,2,1,0:T(8,128)(2,1)S(1)}, bf16[2,2,4,256,128]{4,3,2,1,0:T(8,128)(2,1)S(1)}, u32[]{:S(2)}, u32[]{:S(2)}) collective-permute-start(bf16[2,2,4,256,128]{4,3,2,1,0:T(8,128)(2,1)S(1)} %copy-done.20), channel_id=1, source_target_pairs={{0,1},{1,2},{2,3},{3,4},{4,5},{5,6},{6,7},{8,9},{9,10},{10,11},{11... | collective-permute-start | bytes 3145736 | tf_op jit(solution)/shard_map/ppermute | solution.py:420
  113.1 17.5 %all_to_all.10 = bf16[16,16,640]{2,1,0:T(8,128)(2,1)S(1)} all-to-all(bf16[16,16,640]{2,1,0:T(8,128)(2,1)S(1)} %pad_maximum_fusion), channel_id=1, replica_groups=mesh['bx'=16,'by'=8] {'bx'}, dimensions={0} | all-to-all | bytes 655360 | tf_op jit(solution)/shard_map/all_to_all | solution.py:429
  130.7 11.2 %all_to_all.11 = bf16[16,16,512]{2,1,0:T(8,128)(2,1)S(1)} all-to-all(bf16[16,16,512]{2,1,0:T(8,128)(2,1)S(1)} %broadcast_in_dim.28), channel_id=1, replica_groups=mesh['bx'=16,'by'=8] {'bx'}, dimensions={0} | all-to-all | bytes 524288 | tf_op jit(solution)/shard_map/all_to_all | solution.py:433
  142.8 2.2 %collective-permute-start.11 = (bf16[256,512]{1,0:T(8,128)(2,1)S(1)}, bf16[256,512]{1,0:T(8,128)(2,1)S(1)}, u32[]{:S(2)}, u32[]{:S(2)}) collective-permute-start(bf16[256,512]{1,0:T(8,128)(2,1)S(1)} %bitcast.14), channel_id=1, source_target_pairs={{0,4},{1,5},{2,6},{3,7},{4,0},{5,1},{6,2},{7,3},{8,12},{9,13},{10,... | collective-permute-start | bytes 786440 | tf_op jit(solution)/shard_map/ppermute | solution.py:520
  147.2 12.1 %token_rows.1 = f32[1024,512]{1,0:T(8,128)} custom-call(s32[2]{0:T(128)} %copy-done.7, s32[2048]{0:T(1024)} %copy-done.4, s32[512]{0:T(512)} %copy-done.6, s32[1,1024]{1,0:T(1,128)} %bitcast.21, bf16[1024,512]{1,0:T(8,128)(2,1)} %bitcast.18, f32[1,512]{1,0:T(1,128)} %bitcast.29, bf16[512,1024]{1,0:T(8,128)(2,1)} %w_qk.5, bf16[512,512]{1,0:T(8,128)(2,1)} %w_v.3, ...), custom_call_target="tpu_custom_call" | custom-call | flops 3221225472 | bytes 16777216 | tf_op jit(solution)/shard_map/token_rows/pallas_call | solution.py:438
  159.4 2.8 %collective-permute-start.15 = (bf16[256,512]{1,0:T(8,128)(2,1)S(1)}, bf16[256,512]{1,0:T(8,128)(2,1)S(1)}, u32[]{:S(2)}, u32[]{:S(2)}) collective-permute-start(bf16[256,512]{1,0:T(8,128)(2,1)S(1)} %bitcast.16), channel_id=1, source_target_pairs={{0,1},{1,0},{2,3},{3,2},{4,5},{5,4},{6,7},{7,6},{8,9},{9,8},{10,11... | collective-permute-start | bytes 786440 | tf_op jit(solution)/shard_map/ppermute | solution.py:523
  164.4 2.8 %weight_grads.1 = (f32[512,1024]{1,0:T(8,128)}, f32[512,512]{1,0:T(8,128)}, f32[512,512]{1,0:T(8,128)}) custom-call(s32[2]{0:T(128)S(1)} %copy-done.9, bf16[256,512]{1,0:T(8,128)(2,1)S(1)} %bitcast.17, bf16[256,512]{1,0:T(8,128)(2,1)S(1)} %collective-permute-done.10.refs_1_, bf16[256,512]{1,0:T(8,128)(2,1)S(1)} %collective-permute-done.11.refs_2_, ...), custom_call_target="tpu_custom_call" | custom-call | bytes 6291456 | tf_op jit(solution)/shard_map/weight_grads/pallas_call | solution.py:438
  (89 shorter events, 13.3 us)
Async XLA Ops:
  9.1 19.4 %collective-permute-start = (bf16[512,512]{1,0:T(8,128)(2,1)S(1)}, bf16[512,512]{1,0:T(8,128)(2,1)S(1)}, u32[]{:S(2)}, u32[]{:S(2)}) collective-permute-start(bf16[512,512]{1,0:T(8,128)(2,1)S(1)} %get-tuple-element.71), channel_id=1, source_target_pairs={{0,8},{8,16},{16,24},{24,32},{32,40},{40,48},{48,56},{56,64},{64,7... | collective-permute-start | bytes 1572872 | tf_op jit(solution)/shard_map/ppermute | solution.py:420
  13.5 15.0 %collective-permute-start.1 = (bf16[512,512]{1,0:T(8,128)(2,1)S(1)}, bf16[512,512]{1,0:T(8,128)(2,1)S(1)}, u32[]{:S(2)}, u32[]{:S(2)}) collective-permute-start(bf16[512,512]{1,0:T(8,128)(2,1)S(1)} %get-tuple-element.72), channel_id=1, source_target_pairs={{8,0},{16,8},{24,16},{32,24},{40,32},{48,40},{56,48},{64,56},{72,6... | collective-permute-start | bytes 1572872 | tf_op jit(solution)/shard_map/ppermute | solution.py:420
  14.8 13.7 %collective-permute-start.2 = (bf16[512,512]{1,0:T(8,128)(2,1)S(1)}, bf16[512,512]{1,0:T(8,128)(2,1)S(1)}, u32[]{:S(2)}, u32[]{:S(2)}) collective-permute-start(bf16[512,512]{1,0:T(8,128)(2,1)S(1)} %get-tuple-element.73), channel_id=1, source_target_pairs={{0,1},{1,2},{2,3},{3,4},{4,5},{5,6},{6,7},{8,9},{9,10},{10,11},{11... | collective-permute-start | bytes 1572872 | tf_op jit(solution)/shard_map/ppermute | solution.py:420
  18.8 10.6 %collective-permute-start.3 = (bf16[512,512]{1,0:T(8,128)(2,1)S(1)}, bf16[512,512]{1,0:T(8,128)(2,1)S(1)}, u32[]{:S(2)}, u32[]{:S(2)}) collective-permute-start(bf16[512,512]{1,0:T(8,128)(2,1)S(1)} %get-tuple-element.74), channel_id=1, source_target_pairs={{1,0},{2,1},{3,2},{4,3},{5,4},{6,5},{7,6},{9,8},{10,9},{11,10},{12... | collective-permute-start | bytes 1572872 | tf_op jit(solution)/shard_map/ppermute | solution.py:420
  30.2 57.2 %copy-start.8 = (s32[2]{0:T(128)S(1)}, s32[2]{0:T(128)}, u32[]{:S(2)}) copy-start(s32[2]{0:T(128)} %copy-done.7) | copy-start | bytes 28
  30.2 64.7 %copy-start.2 = (bf16[512,1024]{1,0:T(8,128)(2,1)S(1)}, bf16[512,1024]{1,0:T(8,128)(2,1)}, u32[]{:S(2)}) copy-start(bf16[512,1024]{1,0:T(8,128)(2,1)} %w_qk.5) | copy-start | bytes 3145732
  30.2 64.7 %copy-start.12 = (bf16[512,512]{1,0:T(8,128)(2,1)S(1)}, bf16[512,512]{1,0:T(8,128)(2,1)}, u32[]{:S(2)}) copy-start(bf16[512,512]{1,0:T(8,128)(2,1)} %w_out.3) | copy-start | bytes 1572868
  81.9 5.5 %collective-permute-start.4 = (bf16[1040,512]{1,0:T(8,128)(2,1)}, bf16[1040,512]{1,0:T(8,128)(2,1)S(1)}, u32[]{:S(2)}, u32[]{:S(2)}) collective-permute-start(bf16[1040,512]{1,0:T(8,128)(2,1)} %get-tuple-element.87), channel_id=1, source_target_pairs={{0,1},{1,0},{2,3},{3,2},{4,5},{5,4},{6,7},{7,6},{8,9},{9,8},{10,11... | collective-permute-start | bytes 3194888 | tf_op jit(solution)/shard_map/ppermute | solution.py:510
  82.0 31.0 %collective-permute-start.8 = (bf16[2,2,4,256,128]{4,3,2,1,0:T(8,128)(2,1)}, bf16[2,2,4,256,128]{4,3,2,1,0:T(8,128)(2,1)S(1)}, u32[]{:S(2)}, u32[]{:S(2)}) collective-permute-start(bf16[2,2,4,256,128]{4,3,2,1,0:T(8,128)(2,1)} %get-tuple-element.103), channel_id=1, source_target_pairs={{8,0},{16,8},{24,16},{32,24},{40,32},{48,40},{56,48},{64,56},{72,6... | collective-permute-start | bytes 3145736 | tf_op jit(solution)/shard_map/ppermute | solution.py:420
  83.3 29.7 %collective-permute-start.9 = (bf16[2,2,4,256,128]{4,3,2,1,0:T(8,128)(2,1)}, bf16[2,2,4,256,128]{4,3,2,1,0:T(8,128)(2,1)S(1)}, u32[]{:S(2)}, u32[]{:S(2)}) collective-permute-start(bf16[2,2,4,256,128]{4,3,2,1,0:T(8,128)(2,1)} %get-tuple-element.104), channel_id=1, source_target_pairs={{0,8},{8,16},{16,24},{24,32},{32,40},{40,48},{48,56},{56,64},{64,7... | collective-permute-start | bytes 3145736 | tf_op jit(solution)/shard_map/ppermute | solution.py:420
  90.1 10.5 %collective-permute-start.5 = (bf16[272,512]{1,0:T(8,128)(2,1)S(1)}, bf16[272,512]{1,0:T(8,128)(2,1)S(1)}, u32[]{:S(2)}, u32[]{:S(2)}) collective-permute-start(bf16[272,512]{1,0:T(8,128)(2,1)S(1)} %get-tuple-element.90), channel_id=1, source_target_pairs={{0,2},{1,3},{2,4},{3,5},{4,6},{5,7},{6,0},{7,1},{8,10},{9,11},{10,... | collective-permute-start | bytes 835592 | tf_op jit(solution)/shard_map/ppermute | solution.py:520
  92.5 14.5 %collective-permute-start.6 = (bf16[272,512]{1,0:T(8,128)(2,1)S(1)}, bf16[272,512]{1,0:T(8,128)(2,1)S(1)}, u32[]{:S(2)}, u32[]{:S(2)}) collective-permute-start(bf16[272,512]{1,0:T(8,128)(2,1)S(1)} %get-tuple-element.91), channel_id=1, source_target_pairs={{0,4},{1,5},{2,6},{3,7},{4,0},{5,1},{6,2},{7,3},{8,12},{9,13},{10,... | collective-permute-start | bytes 835592 | tf_op jit(solution)/shard_map/ppermute | solution.py:520
  94.9 12.1 %collective-permute-start.7 = (bf16[272,512]{1,0:T(8,128)(2,1)S(1)}, bf16[272,512]{1,0:T(8,128)(2,1)S(1)}, u32[]{:S(2)}, u32[]{:S(2)}) collective-permute-start(bf16[272,512]{1,0:T(8,128)(2,1)S(1)} %get-tuple-element.92), channel_id=1, source_target_pairs={{0,6},{1,7},{2,0},{3,1},{4,2},{5,3},{6,4},{7,5},{8,14},{9,15},{10,... | collective-permute-start | bytes 835592 | tf_op jit(solution)/shard_map/ppermute | solution.py:520
  107.0 38.9 %collective-permute-start.13 = (bf16[2,2,4,256,128]{4,3,2,1,0:T(8,128)(2,1)S(1)}, bf16[2,2,4,256,128]{4,3,2,1,0:T(8,128)(2,1)S(1)}, u32[]{:S(2)}, u32[]{:S(2)}) collective-permute-start(bf16[2,2,4,256,128]{4,3,2,1,0:T(8,128)(2,1)S(1)} %copy-done.21), channel_id=1, source_target_pairs={{1,0},{2,1},{3,2},{4,3},{5,4},{6,5},{7,6},{9,8},{10,9},{11,10},{12... | collective-permute-start | bytes 3145736 | tf_op jit(solution)/shard_map/ppermute | solution.py:420
  110.3 35.5 %collective-permute-start.14 = (bf16[2,2,4,256,128]{4,3,2,1,0:T(8,128)(2,1)S(1)}, bf16[2,2,4,256,128]{4,3,2,1,0:T(8,128)(2,1)S(1)}, u32[]{:S(2)}, u32[]{:S(2)}) collective-permute-start(bf16[2,2,4,256,128]{4,3,2,1,0:T(8,128)(2,1)S(1)} %copy-done.20), channel_id=1, source_target_pairs={{0,1},{1,2},{2,3},{3,4},{4,5},{5,6},{6,7},{8,9},{9,10},{10,11},{11... | collective-permute-start | bytes 3145736 | tf_op jit(solution)/shard_map/ppermute | solution.py:420
  113.0 32.9 %copy-start.16 = (bf16[2,2,4,256,128]{4,3,2,1,0:T(8,128)(2,1)}, bf16[2,2,4,256,128]{4,3,2,1,0:T(8,128)(2,1)S(1)}, u32[]{:S(2)}) copy-start(bf16[2,2,4,256,128]{4,3,2,1,0:T(8,128)(2,1)S(1)} %collective-permute-done.8.b0) | copy-start | bytes 3145732
  113.0 32.9 %copy-start.17 = (bf16[2,2,4,256,128]{4,3,2,1,0:T(8,128)(2,1)}, bf16[2,2,4,256,128]{4,3,2,1,0:T(8,128)(2,1)S(1)}, u32[]{:S(2)}) copy-start(bf16[2,2,4,256,128]{4,3,2,1,0:T(8,128)(2,1)S(1)} %collective-permute-done.9.b1) | copy-start | bytes 3145732
  141.9 17.5 %collective-permute-start.12 = (bf16[256,512]{1,0:T(8,128)(2,1)S(1)}, bf16[256,512]{1,0:T(8,128)(2,1)S(1)}, u32[]{:S(2)}, u32[]{:S(2)}) collective-permute-start(bf16[256,512]{1,0:T(8,128)(2,1)S(1)} %bitcast.13), channel_id=1, source_target_pairs={{0,6},{1,7},{2,0},{3,1},{4,2},{5,3},{6,4},{7,5},{8,14},{9,15},{10,... | collective-permute-start | bytes 786440 | tf_op jit(solution)/shard_map/ppermute | solution.py:520
  142.8 16.6 %collective-permute-start.11 = (bf16[256,512]{1,0:T(8,128)(2,1)S(1)}, bf16[256,512]{1,0:T(8,128)(2,1)S(1)}, u32[]{:S(2)}, u32[]{:S(2)}) collective-permute-start(bf16[256,512]{1,0:T(8,128)(2,1)S(1)} %bitcast.14), channel_id=1, source_target_pairs={{0,4},{1,5},{2,6},{3,7},{4,0},{5,1},{6,2},{7,3},{8,12},{9,13},{10,... | collective-permute-start | bytes 786440 | tf_op jit(solution)/shard_map/ppermute | solution.py:520
  145.0 14.4 %collective-permute-start.10 = (bf16[256,512]{1,0:T(8,128)(2,1)S(1)}, bf16[256,512]{1,0:T(8,128)(2,1)S(1)}, u32[]{:S(2)}, u32[]{:S(2)}) collective-permute-start(bf16[256,512]{1,0:T(8,128)(2,1)S(1)} %bitcast.15), channel_id=1, source_target_pairs={{0,2},{1,3},{2,4},{3,5},{4,6},{5,7},{6,0},{7,1},{8,10},{9,11},{10,... | collective-permute-start | bytes 786440 | tf_op jit(solution)/shard_map/ppermute | solution.py:520
  159.4 3.9 %collective-permute-start.15 = (bf16[256,512]{1,0:T(8,128)(2,1)S(1)}, bf16[256,512]{1,0:T(8,128)(2,1)S(1)}, u32[]{:S(2)}, u32[]{:S(2)}) collective-permute-start(bf16[256,512]{1,0:T(8,128)(2,1)S(1)} %bitcast.16), channel_id=1, source_target_pairs={{0,1},{1,0},{2,3},{3,2},{4,5},{5,4},{6,7},{7,6},{8,9},{9,8},{10,11... | collective-permute-start | bytes 786440 | tf_op jit(solution)/shard_map/ppermute | solution.py:523
  162.1 1.5 collective-permute-start.16
  162.2 1.8 %collective-permute-start.17 = (bf16[256,512]{1,0:T(8,128)(2,1)S(1)}, bf16[256,512]{1,0:T(8,128)(2,1)S(1)}, u32[]{:S(2)}, u32[]{:S(2)}) collective-permute-start(bf16[256,512]{1,0:T(8,128)(2,1)S(1)} %collective-permute-done.11.refs_2_), channel_id=1, source_target_pairs={{0,1},{1,0},{2,3},{3,2},{4,5},{5,4},{6,7},{7,6},{8,9},{9,8},{10,11... | collective-permute-start | bytes 786440 | tf_op jit(solution)/shard_map/ppermute | solution.py:523
  162.7 1.8 %collective-permute-start.18 = (bf16[256,512]{1,0:T(8,128)(2,1)S(1)}, bf16[256,512]{1,0:T(8,128)(2,1)S(1)}, u32[]{:S(2)}, u32[]{:S(2)}) collective-permute-start(bf16[256,512]{1,0:T(8,128)(2,1)S(1)} %collective-permute-done.12.refs_3_), channel_id=1, source_target_pairs={{0,1},{1,0},{2,3},{3,2},{4,5},{5,4},{6,7},{7,6},{8,9},{9,8},{10,11... | collective-permute-start | bytes 786440 | tf_op jit(solution)/shard_map/ppermute | solution.py:523
  (21 other events, 138.3 us)

commit v5 on v4

--- a/solution.py
+++ b/solution.py
@@ -525,7 +525,7 @@
     got = [along_y(cut[s - 1], s) for s in range(1, count)]
     branch_out, part = call(
         output_kernel, "branch_rows", [shape((n, d), BF), shape((n, d), F32)],
-        (order, w_query_key, w_out, ctx_t, dq_t), [VM] * 5, [], 40,
+        (order, w_query_key, w_out, ctx_t, dq_t), [VM] * 5, [], 24,
         4 * n * n * d + 4 * n * d * d, 7 << 20,
     )
     got, h2, h3 = lax.optimization_barrier((got, h2, h3))
@@ -544,7 +544,7 @@
         (pos, ids, cnt, order, tok, gain, w_query_key, w_value, part, own, *b_x, *b_y),
         [SM] * 3 + [VM] * 11,
         [pltpu.VMEM((blocks, 2, np_, BLK, PAIR), F32), pltpu.VMEM((n, 2 * d), BF)],
-        56, 4 * n * n * d + 4 * n * d * d, 16 << 20,
+        30, 4 * n * n * d + 4 * n * d * d, 16 << 20,
     )
     chunks, grad_rows = lax.optimization_barrier((chunks, grad_rows))
     chunks = chunks + [other_core(c) for c in chunks]

time: 168 us -> 164 us (0.976)
  Pallas kernels: 82.4 us -> 72 us
  starting transfers between devices: 35 us -> 41.9 us
  local copies, waits for them, and re-layouts: 11.3 us -> 8.7 us
  waiting for transfers between devices: 8.37 us -> 10.1 us
    pallas_call x7, Pallas kernels: 82.4 us -> 72 us  [call(): pl.pallas_call(kernel, out_shape=outs, grid=grid, in_specs=specs, out_spe...]
    ppermute x1, starting transfers between devices: 0.08 us -> 5.01 us  [shards(): cores = lax.ppermute(send, 'by', [(i, i ^ 1) for i in range(extent_y)])]
    unnamed x54, local copies, waits for them, and re-layouts: 10.4 us -> 7.72 us
    ppermute x6, starting transfers between devices: 8.77 us -> 10.9 us  [along_y(): lax.ppermute(rows, 'by', [(i, (i + 2 * s) % extent_y) for i in range(exte...]
    ppermute x6, waiting for transfers between devices: 6.31 us -> 8 us  [along_y(): lax.ppermute(rows, 'by', [(i, (i + 2 * s) % extent_y) for i in range(exte...]
  transfers between devices with their start and end apart: 19 -> 19, of which waited for: 5 -> 7; matrix products, arithmetic and copies ran while one was open for 1% -> 1% of each run, Pallas kernels for 15% -> 13%
where the time goes in v5:
time: 164 us
  Pallas kernels  72 us (44%)
  starting transfers between devices  41.9 us (26%)
  blocking collectives  29.6 us (18%)
  waiting for transfers between devices  10.1 us (6%)
  local copies, waits for them, and re-layouts  8.7 us (5%)
    pallas_call x7, Pallas kernels, call(): pl.pallas_call(kernel, out_shape=outs, grid=grid, in_specs=specs, out_spe...  72 us
    ppermute x8, starting transfers between devices, step_to(): return lax.ppermute(block, axis, route)  23 us
    all_to_all x1, blocking collectives, across_x(): got = lax.all_to_all(parts, 'bx', 0, 0, tiled=True)  18.4 us
    all_to_all x1, blocking collectives, across_x(): lax.all_to_all(jnp.broadcast_to(mine[None], (count,) + mine.shape), 'bx',...  11.1 us
    ppermute x6, starting transfers between devices, along_y(): lax.ppermute(rows, 'by', [(i, (i + 2 * s) % extent_y) for i in range(exte...  10.9 us
    ppermute x6, waiting for transfers between devices, along_y(): lax.ppermute(rows, 'by', [(i, (i + 2 * s) % extent_y) for i in range(exte...  8 us
    unnamed x54, local copies, waits for them, and re-layouts  7.72 us
    ppermute x1, starting transfers between devices, shards(): cores = lax.ppermute(send, 'by', [(i, i ^ 1) for i in range(extent_y)])  5.01 us
  transfers between devices with their start and end apart: 19, of which 7 were waited for; matrix products, arithmetic and copies ran while one was open for 1% of the time, Pallas kernels for 13%

profile of v5, /device:TPU:1, one launch (start us, length us, event | category | flops | bytes accessed | tf_op | source)
XLA Modules:
  0.0 163.7 jit_solution(13513415136347261412)
XLA Ops:
  3.1 1.2 copy-done.3
  5.1 3.0 %sort_rows.1 = (bf16[1024,512]{1,0:T(8,128)(2,1)S(1)}, bf16[512,512]{1,0:T(8,128)(2,1)S(1)}, bf16[512,512]{1,0:T(8,128)(2,1)S(1)}, bf16[512,512]{1,0:T(8,128)(2,1)S(1)}, bf16[512,512]{1,0:T(8,128)(2,1)S(1)}) custom-call(s32[2]{0:T(128)S(1)} %pad_add_fusion.pos, s32[2048]{0:T(1024)S(1)} %reshape.59.ids, s32[512]{0:T(512)S(1)} %reshape.60.cnt, ...), custom_call_target="tpu_custom_call" | custom-call | flops 1073741824 | bytes 4194304 | tf_op jit(solution)/shard_map/sort_rows/pallas_call | solution.py:438
  9.1 4.4 %collective-permute-start = (bf16[512,512]{1,0:T(8,128)(2,1)S(1)}, bf16[512,512]{1,0:T(8,128)(2,1)S(1)}, u32[]{:S(2)}, u32[]{:S(2)}) collective-permute-start(bf16[512,512]{1,0:T(8,128)(2,1)S(1)} %get-tuple-element.71), channel_id=1, source_target_pairs={{0,8},{8,16},{16,24},{24,32},{32,40},{40,48},{48,56},{56,64},{64,7... | collective-permute-start | bytes 1572872 | tf_op jit(solution)/shard_map/ppermute | solution.py:420
  13.5 1.3 collective-permute-start.1
  14.8 4.0 %collective-permute-start.2 = (bf16[512,512]{1,0:T(8,128)(2,1)S(1)}, bf16[512,512]{1,0:T(8,128)(2,1)S(1)}, u32[]{:S(2)}, u32[]{:S(2)}) collective-permute-start(bf16[512,512]{1,0:T(8,128)(2,1)S(1)} %get-tuple-element.73), channel_id=1, source_target_pairs={{0,1},{1,2},{2,3},{3,4},{4,5},{5,6},{6,7},{8,9},{9,10},{10,11},{11... | collective-permute-start | bytes 1572872 | tf_op jit(solution)/shard_map/ppermute | solution.py:420
  18.8 1.9 %collective-permute-start.3 = (bf16[512,512]{1,0:T(8,128)(2,1)S(1)}, bf16[512,512]{1,0:T(8,128)(2,1)S(1)}, u32[]{:S(2)}, u32[]{:S(2)}) collective-permute-start(bf16[512,512]{1,0:T(8,128)(2,1)S(1)} %get-tuple-element.74), channel_id=1, source_target_pairs={{1,0},{2,1},{3,2},{4,3},{5,4},{6,5},{7,6},{9,8},{10,9},{11,10},{12... | collective-permute-start | bytes 1572872 | tf_op jit(solution)/shard_map/ppermute | solution.py:420
  20.7 7.7 %project.1 = (bf16[1024,512]{1,0:T(8,128)(2,1)}, bf16[4,512,256]{2,1,0:T(8,128)(2,1)}, bf16[4,4,256,128]{3,2,1,0:T(8,128)(2,1)}, bf16[4,4,128,256]{3,2,1,0:T(8,1...) custom-call(s32[1,1024]{1,0:T(1,128)} %bitcast.20, ...), custom_call_target="tpu_custom_call" | custom-call | flops 3221225472 | bytes 14680064 | tf_op jit(solution)/shard_map/project/pallas_call | solution.py:438
  30.3 45.2 %attend.1 = (bf16[512,1024]{1,0:T(8,128)(2,1)}, bf16[512,1024]{1,0:T(8,128)(2,1)}, f32[4,2,4,256,128]{4,3,2,1,0:T(8,128)}, bf16[2,2,4,256,128]{4,3,2,1,0:T(8,128...) custom-call(s32[2]{0:T(128)} %copy-done.11, ...), custom_call_target="tpu_custom_call" | custom-call | flops 8053063680 | bytes 25165824 | tf_op jit(solution)/shard_map/attend/pallas_call | solution.py:438
  75.5 5.0 %collective-permute-start.4 = (bf16[1040,512]{1,0:T(8,128)(2,1)}, bf16[1040,512]{1,0:T(8,128)(2,1)S(1)}, u32[]{:S(2)}, u32[]{:S(2)}) collective-permute-start(bf16[1040,512]{1,0:T(8,128)(2,1)} %get-tuple-element.87), channel_id=1, source_target_pairs={{0,1},{1,0},{2,3},{3,2},{4,5},{5,4},{6,7},{7,6},{8,9},{9,8},{10,11... | collective-permute-start | bytes 3194888 | tf_op jit(solution)/shard_map/ppermute | solution.py:510
  80.5 1.3 collective-permute-start.8
  81.8 4.1 %collective-permute-start.9 = (bf16[2,2,4,256,128]{4,3,2,1,0:T(8,128)(2,1)}, bf16[2,2,4,256,128]{4,3,2,1,0:T(8,128)(2,1)S(1)}, u32[]{:S(2)}, u32[]{:S(2)}) collective-permute-start(bf16[2,2,4,256,128]{4,3,2,1,0:T(8,128)(2,1)} %get-tuple-element.104), channel_id=1, source_target_pairs={{0,8},{8,16},{16,24},{24,32},{32,40},{40,48},{48,56},{56,64},{64,7... | collective-permute-start | bytes 3145736 | tf_op jit(solution)/shard_map/ppermute | solution.py:420
  89.3 4.7 %collective-permute-start.6 = (bf16[272,512]{1,0:T(8,128)(2,1)S(1)}, bf16[272,512]{1,0:T(8,128)(2,1)S(1)}, u32[]{:S(2)}, u32[]{:S(2)}) collective-permute-start(bf16[272,512]{1,0:T(8,128)(2,1)S(1)} %get-tuple-element.91), channel_id=1, source_target_pairs={{0,4},{1,5},{2,6},{3,7},{4,0},{5,1},{6,2},{7,3},{8,12},{9,13},{10,... | collective-permute-start | bytes 835592 | tf_op jit(solution)/shard_map/ppermute | solution.py:520
  93.9 2.0 %collective-permute-start.7 = (bf16[272,512]{1,0:T(8,128)(2,1)S(1)}, bf16[272,512]{1,0:T(8,128)(2,1)S(1)}, u32[]{:S(2)}, u32[]{:S(2)}) collective-permute-start(bf16[272,512]{1,0:T(8,128)(2,1)S(1)} %get-tuple-element.92), channel_id=1, source_target_pairs={{0,6},{1,7},{2,0},{3,1},{4,2},{5,3},{6,4},{7,5},{8,14},{9,15},{10,... | collective-permute-start | bytes 835592 | tf_op jit(solution)/shard_map/ppermute | solution.py:520
  96.0 4.4 %branch_rows.1 = (bf16[1024,512]{1,0:T(8,128)(2,1)}, f32[1024,512]{1,0:T(8,128)S(1)}) custom-call(s32[1,1024]{1,0:T(1,128)S(1)} %bitcast.22, bf16[512,1024]{1,0:T(8,128)(2,1)S(1)} %copy-done.2, bf16[512,512]{1,0:T(8,128)(2,1)S(1)} %copy-done.16, bf16[512,1024]{1,0:T(8,128)(2,1)S(1)} %copy-done.18, bf16[512,1024]{1,0:T(8,128)(2,1)S(1)} %copy-done.19), custom_call_target="tpu_custom_call" | custom-call | flops 3221225472 | bytes 7340032 | tf_op jit(solution)/shard_map/branch_rows/pallas_call | solution.py:438
  100.4 5.9 %collective-permute-done.6 = bf16[272,512]{1,0:T(8,128)(2,1)S(1)} collective-permute-done((bf16[272,512]{1,0:T(8,128)(2,1)S(1)}, bf16[272,512]{1,0:T(8,128)(2,1)S(1)}, u32[]{:S(2)}, u32[]{:S(2)}) %collective-permute-start.6) | collective-permute-done | bytes 278560 | tf_op jit(solution)/shard_map/ppermute | solution.py:520
  106.3 3.0 %collective-permute-start.13 = (bf16[2,2,4,256,128]{4,3,2,1,0:T(8,128)(2,1)S(1)}, bf16[2,2,4,256,128]{4,3,2,1,0:T(8,128)(2,1)S(1)}, u32[]{:S(2)}, u32[]{:S(2)}) collective-permute-start(bf16[2,2,4,256,128]{4,3,2,1,0:T(8,128)(2,1)S(1)} %copy-done.21), channel_id=1, source_target_pairs={{1,0},{2,1},{3,2},{4,3},{5,4},{6,5},{7,6},{9,8},{10,9},{11,10},{12... | collective-permute-start | bytes 3145736 | tf_op jit(solution)/shard_map/ppermute | solution.py:420
  109.4 2.9 %collective-permute-start.14 = (bf16[2,2,4,256,128]{4,3,2,1,0:T(8,128)(2,1)S(1)}, bf16[2,2,4,256,128]{4,3,2,1,0:T(8,128)(2,1)S(1)}, u32[]{:S(2)}, u32[]{:S(2)}) collective-permute-start(bf16[2,2,4,256,128]{4,3,2,1,0:T(8,128)(2,1)S(1)} %copy-done.20), channel_id=1, source_target_pairs={{0,1},{1,2},{2,3},{3,4},{4,5},{5,6},{6,7},{8,9},{9,10},{10,11},{11... | collective-permute-start | bytes 3145736 | tf_op jit(solution)/shard_map/ppermute | solution.py:420
  112.6 18.4 %all_to_all.10 = bf16[16,16,640]{2,1,0:T(8,128)(2,1)S(1)} all-to-all(bf16[16,16,640]{2,1,0:T(8,128)(2,1)S(1)} %pad_maximum_fusion), channel_id=1, replica_groups=mesh['bx'=16,'by'=8] {'bx'}, dimensions={0} | all-to-all | bytes 655360 | tf_op jit(solution)/shard_map/all_to_all | solution.py:429
  131.1 11.1 %all_to_all.11 = bf16[16,16,512]{2,1,0:T(8,128)(2,1)S(1)} all-to-all(bf16[16,16,512]{2,1,0:T(8,128)(2,1)S(1)} %broadcast_in_dim.28), channel_id=1, replica_groups=mesh['bx'=16,'by'=8] {'bx'}, dimensions={0} | all-to-all | bytes 524288 | tf_op jit(solution)/shard_map/all_to_all | solution.py:433
  142.8 3.0 %collective-permute-start.11 = (bf16[256,512]{1,0:T(8,128)(2,1)S(1)}, bf16[256,512]{1,0:T(8,128)(2,1)S(1)}, u32[]{:S(2)}, u32[]{:S(2)}) collective-permute-start(bf16[256,512]{1,0:T(8,128)(2,1)S(1)} %bitcast.14), channel_id=1, source_target_pairs={{0,4},{1,5},{2,6},{3,7},{4,0},{5,1},{6,2},{7,3},{8,12},{9,13},{10,... | collective-permute-start | bytes 786440 | tf_op jit(solution)/shard_map/ppermute | solution.py:520
  145.9 8.1 %token_rows.1 = f32[1024,512]{1,0:T(8,128)} custom-call(s32[2]{0:T(128)S(1)} %copy-done.12, s32[2048]{0:T(1024)S(1)} %copy-done.7, s32[512]{0:T(512)S(1)} %copy-done.10, s32[1,1024]{1,0:T(1,128)S(1)} %bitcast.23, bf16[1024,512]{1,0:T(8,128)(2,1)S(1)} %bitcast.19, f32[1,512]{1,0:T(1,128)S(1)} %bitcast.26, bf16[512,1024]{1,0:T(8,128)(2,1)S(1)} %copy-done.2, ...), custom_call_target="tpu_custom_call" | custom-call | flops 3221225472 | bytes 16777216 | tf_op jit(solution)/shard_map/token_rows/pallas_call | solution.py:438
  154.0 2.1 %collective-permute-done.10.refs_1_ = bf16[256,512]{1,0:T(8,128)(2,1)S(1)} collective-permute-done((bf16[256,512]{1,0:T(8,128)(2,1)S(1)}, bf16[256,512]{1,0:T(8,128)(2,1)S(1)}, u32[]{:S(2)}, u32[]{:S(2)}) %collective-permute-start.10) | collective-permute-done | bytes 262176 | tf_op jit(solution)/shard_map/ppermute | solution.py:520
  156.1 2.6 %collective-permute-start.15 = (bf16[256,512]{1,0:T(8,128)(2,1)S(1)}, bf16[256,512]{1,0:T(8,128)(2,1)S(1)}, u32[]{:S(2)}, u32[]{:S(2)}) collective-permute-start(bf16[256,512]{1,0:T(8,128)(2,1)S(1)} %bitcast.16), channel_id=1, source_target_pairs={{0,1},{1,0},{2,3},{3,2},{4,5},{5,4},{6,7},{7,6},{8,9},{9,8},{10,11... | collective-permute-start | bytes 786440 | tf_op jit(solution)/shard_map/ppermute | solution.py:523
  160.9 2.8 %weight_grads.1 = (f32[512,1024]{1,0:T(8,128)}, f32[512,512]{1,0:T(8,128)}, f32[512,512]{1,0:T(8,128)}) custom-call(s32[2]{0:T(128)S(1)} %copy-done.12, bf16[256,512]{1,0:T(8,128)(2,1)S(1)} %bitcast.17, bf16[256,512]{1,0:T(8,128)(2,1)S(1)} %collective-permute-done.10.refs_1_, bf16[256,512]{1,0:T(8,128)(2,1)S(1)} %collective-permute-done.11.refs_2_, ...), custom_call_target="tpu_custom_call" | custom-call | bytes 6291456 | tf_op jit(solution)/shard_map/weight_grads/pallas_call | solution.py:438
  (89 shorter events, 12.5 us)
Async XLA Ops:
  9.1 19.4 %collective-permute-start = (bf16[512,512]{1,0:T(8,128)(2,1)S(1)}, bf16[512,512]{1,0:T(8,128)(2,1)S(1)}, u32[]{:S(2)}, u32[]{:S(2)}) collective-permute-start(bf16[512,512]{1,0:T(8,128)(2,1)S(1)} %get-tuple-element.71), channel_id=1, source_target_pairs={{0,8},{8,16},{16,24},{24,32},{32,40},{40,48},{48,56},{56,64},{64,7... | collective-permute-start | bytes 1572872 | tf_op jit(solution)/shard_map/ppermute | solution.py:420
  13.5 15.0 %collective-permute-start.1 = (bf16[512,512]{1,0:T(8,128)(2,1)S(1)}, bf16[512,512]{1,0:T(8,128)(2,1)S(1)}, u32[]{:S(2)}, u32[]{:S(2)}) collective-permute-start(bf16[512,512]{1,0:T(8,128)(2,1)S(1)} %get-tuple-element.72), channel_id=1, source_target_pairs={{8,0},{16,8},{24,16},{32,24},{40,32},{48,40},{56,48},{64,56},{72,6... | collective-permute-start | bytes 1572872 | tf_op jit(solution)/shard_map/ppermute | solution.py:420
  14.8 13.7 %collective-permute-start.2 = (bf16[512,512]{1,0:T(8,128)(2,1)S(1)}, bf16[512,512]{1,0:T(8,128)(2,1)S(1)}, u32[]{:S(2)}, u32[]{:S(2)}) collective-permute-start(bf16[512,512]{1,0:T(8,128)(2,1)S(1)} %get-tuple-element.73), channel_id=1, source_target_pairs={{0,1},{1,2},{2,3},{3,4},{4,5},{5,6},{6,7},{8,9},{9,10},{10,11},{11... | collective-permute-start | bytes 1572872 | tf_op jit(solution)/shard_map/ppermute | solution.py:420
  18.8 10.6 %collective-permute-start.3 = (bf16[512,512]{1,0:T(8,128)(2,1)S(1)}, bf16[512,512]{1,0:T(8,128)(2,1)S(1)}, u32[]{:S(2)}, u32[]{:S(2)}) collective-permute-start(bf16[512,512]{1,0:T(8,128)(2,1)S(1)} %get-tuple-element.74), channel_id=1, source_target_pairs={{1,0},{2,1},{3,2},{4,3},{5,4},{6,5},{7,6},{9,8},{10,9},{11,10},{12... | collective-permute-start | bytes 1572872 | tf_op jit(solution)/shard_map/ppermute | solution.py:420
  30.2 55.6 %copy-start.12 = (s32[2]{0:T(128)S(1)}, s32[2]{0:T(128)}, u32[]{:S(2)}) copy-start(s32[2]{0:T(128)} %copy-done.11) | copy-start | bytes 28
  30.2 65.7 %copy-start.2 = (bf16[512,1024]{1,0:T(8,128)(2,1)S(1)}, bf16[512,1024]{1,0:T(8,128)(2,1)}, u32[]{:S(2)}) copy-start(bf16[512,1024]{1,0:T(8,128)(2,1)} %w_qk.5) | copy-start | bytes 3145732
  30.2 65.7 %copy-start.16 = (bf16[512,512]{1,0:T(8,128)(2,1)S(1)}, bf16[512,512]{1,0:T(8,128)(2,1)}, u32[]{:S(2)}) copy-start(bf16[512,512]{1,0:T(8,128)(2,1)} %w_out.3) | copy-start | bytes 1572868
  75.5 10.4 %collective-permute-start.4 = (bf16[1040,512]{1,0:T(8,128)(2,1)}, bf16[1040,512]{1,0:T(8,128)(2,1)S(1)}, u32[]{:S(2)}, u32[]{:S(2)}) collective-permute-start(bf16[1040,512]{1,0:T(8,128)(2,1)} %get-tuple-element.87), channel_id=1, source_target_pairs={{0,1},{1,0},{2,3},{3,2},{4,5},{5,4},{6,7},{7,6},{8,9},{9,8},{10,11... | collective-permute-start | bytes 3194888 | tf_op jit(solution)/shard_map/ppermute | solution.py:510
  80.5 32.0 %collective-permute-start.8 = (bf16[2,2,4,256,128]{4,3,2,1,0:T(8,128)(2,1)}, bf16[2,2,4,256,128]{4,3,2,1,0:T(8,128)(2,1)S(1)}, u32[]{:S(2)}, u32[]{:S(2)}) collective-permute-start(bf16[2,2,4,256,128]{4,3,2,1,0:T(8,128)(2,1)} %get-tuple-element.103), channel_id=1, source_target_pairs={{8,0},{16,8},{24,16},{32,24},{40,32},{48,40},{56,48},{64,56},{72,6... | collective-permute-start | bytes 3145736 | tf_op jit(solution)/shard_map/ppermute | solution.py:420
  81.8 30.7 %collective-permute-start.9 = (bf16[2,2,4,256,128]{4,3,2,1,0:T(8,128)(2,1)}, bf16[2,2,4,256,128]{4,3,2,1,0:T(8,128)(2,1)S(1)}, u32[]{:S(2)}, u32[]{:S(2)}) collective-permute-start(bf16[2,2,4,256,128]{4,3,2,1,0:T(8,128)(2,1)} %get-tuple-element.104), channel_id=1, source_target_pairs={{0,8},{8,16},{16,24},{24,32},{32,40},{40,48},{48,56},{56,64},{64,7... | collective-permute-start | bytes 3145736 | tf_op jit(solution)/shard_map/ppermute | solution.py:420
  88.6 11.8 %collective-permute-start.5 = (bf16[272,512]{1,0:T(8,128)(2,1)S(1)}, bf16[272,512]{1,0:T(8,128)(2,1)S(1)}, u32[]{:S(2)}, u32[]{:S(2)}) collective-permute-start(bf16[272,512]{1,0:T(8,128)(2,1)S(1)} %get-tuple-element.90), channel_id=1, source_target_pairs={{0,2},{1,3},{2,4},{3,5},{4,6},{5,7},{6,0},{7,1},{8,10},{9,11},{10,... | collective-permute-start | bytes 835592 | tf_op jit(solution)/shard_map/ppermute | solution.py:520
  89.3 17.0 %collective-permute-start.6 = (bf16[272,512]{1,0:T(8,128)(2,1)S(1)}, bf16[272,512]{1,0:T(8,128)(2,1)S(1)}, u32[]{:S(2)}, u32[]{:S(2)}) collective-permute-start(bf16[272,512]{1,0:T(8,128)(2,1)S(1)} %get-tuple-element.91), channel_id=1, source_target_pairs={{0,4},{1,5},{2,6},{3,7},{4,0},{5,1},{6,2},{7,3},{8,12},{9,13},{10,... | collective-permute-start | bytes 835592 | tf_op jit(solution)/shard_map/ppermute | solution.py:520
  93.9 12.4 %collective-permute-start.7 = (bf16[272,512]{1,0:T(8,128)(2,1)S(1)}, bf16[272,512]{1,0:T(8,128)(2,1)S(1)}, u32[]{:S(2)}, u32[]{:S(2)}) collective-permute-start(bf16[272,512]{1,0:T(8,128)(2,1)S(1)} %get-tuple-element.92), channel_id=1, source_target_pairs={{0,6},{1,7},{2,0},{3,1},{4,2},{5,3},{6,4},{7,5},{8,14},{9,15},{10,... | collective-permute-start | bytes 835592 | tf_op jit(solution)/shard_map/ppermute | solution.py:520
  96.0 49.8 %copy-start = (f32[4,2,4,256,128]{4,3,2,1,0:T(8,128)S(1)}, f32[4,2,4,256,128]{4,3,2,1,0:T(8,128)}, u32[]{:S(2)}) copy-start(f32[4,2,4,256,128]{4,3,2,1,0:T(8,128)} %get-tuple-element.111.own) | copy-start | bytes 12582916
  100.4 45.5 %copy-start.15 = (f32[512]{0:T(512)S(1)}, f32[512]{0:T(512)}, u32[]{:S(2)}) copy-start(f32[512]{0:T(512)} %param.12) | copy-start | bytes 6148
  106.3 39.5 %collective-permute-start.13 = (bf16[2,2,4,256,128]{4,3,2,1,0:T(8,128)(2,1)S(1)}, bf16[2,2,4,256,128]{4,3,2,1,0:T(8,128)(2,1)S(1)}, u32[]{:S(2)}, u32[]{:S(2)}) collective-permute-start(bf16[2,2,4,256,128]{4,3,2,1,0:T(8,128)(2,1)S(1)} %copy-done.21), channel_id=1, source_target_pairs={{1,0},{2,1},{3,2},{4,3},{5,4},{6,5},{7,6},{9,8},{10,9},{11,10},{12... | collective-permute-start | bytes 3145736 | tf_op jit(solution)/shard_map/ppermute | solution.py:420
  109.4 36.4 %collective-permute-start.14 = (bf16[2,2,4,256,128]{4,3,2,1,0:T(8,128)(2,1)S(1)}, bf16[2,2,4,256,128]{4,3,2,1,0:T(8,128)(2,1)S(1)}, u32[]{:S(2)}, u32[]{:S(2)}) collective-permute-start(bf16[2,2,4,256,128]{4,3,2,1,0:T(8,128)(2,1)S(1)} %copy-done.20), channel_id=1, source_target_pairs={{0,1},{1,2},{2,3},{3,4},{4,5},{5,6},{6,7},{8,9},{9,10},{10,11},{11... | collective-permute-start | bytes 3145736 | tf_op jit(solution)/shard_map/ppermute | solution.py:420
  142.2 11.8 %collective-permute-start.12 = (bf16[256,512]{1,0:T(8,128)(2,1)S(1)}, bf16[256,512]{1,0:T(8,128)(2,1)S(1)}, u32[]{:S(2)}, u32[]{:S(2)}) collective-permute-start(bf16[256,512]{1,0:T(8,128)(2,1)S(1)} %bitcast.13), channel_id=1, source_target_pairs={{0,6},{1,7},{2,0},{3,1},{4,2},{5,3},{6,4},{7,5},{8,14},{9,15},{10,... | collective-permute-start | bytes 786440 | tf_op jit(solution)/shard_map/ppermute | solution.py:520
  142.8 11.2 %collective-permute-start.11 = (bf16[256,512]{1,0:T(8,128)(2,1)S(1)}, bf16[256,512]{1,0:T(8,128)(2,1)S(1)}, u32[]{:S(2)}, u32[]{:S(2)}) collective-permute-start(bf16[256,512]{1,0:T(8,128)(2,1)S(1)} %bitcast.14), channel_id=1, source_target_pairs={{0,4},{1,5},{2,6},{3,7},{4,0},{5,1},{6,2},{7,3},{8,12},{9,13},{10,... | collective-permute-start | bytes 786440 | tf_op jit(solution)/shard_map/ppermute | solution.py:520
  145.8 10.3 %collective-permute-start.10 = (bf16[256,512]{1,0:T(8,128)(2,1)S(1)}, bf16[256,512]{1,0:T(8,128)(2,1)S(1)}, u32[]{:S(2)}, u32[]{:S(2)}) collective-permute-start(bf16[256,512]{1,0:T(8,128)(2,1)S(1)} %bitcast.15), channel_id=1, source_target_pairs={{0,2},{1,3},{2,4},{3,5},{4,6},{5,7},{6,0},{7,1},{8,10},{9,11},{10,... | collective-permute-start | bytes 786440 | tf_op jit(solution)/shard_map/ppermute | solution.py:520
  156.1 3.7 %collective-permute-start.15 = (bf16[256,512]{1,0:T(8,128)(2,1)S(1)}, bf16[256,512]{1,0:T(8,128)(2,1)S(1)}, u32[]{:S(2)}, u32[]{:S(2)}) collective-permute-start(bf16[256,512]{1,0:T(8,128)(2,1)S(1)} %bitcast.16), channel_id=1, source_target_pairs={{0,1},{1,0},{2,3},{3,2},{4,5},{5,4},{6,7},{7,6},{8,9},{9,8},{10,11... | collective-permute-start | bytes 786440 | tf_op jit(solution)/shard_map/ppermute | solution.py:523
  158.7 1.5 collective-permute-start.16
  158.7 1.9 %collective-permute-start.17 = (bf16[256,512]{1,0:T(8,128)(2,1)S(1)}, bf16[256,512]{1,0:T(8,128)(2,1)S(1)}, u32[]{:S(2)}, u32[]{:S(2)}) collective-permute-start(bf16[256,512]{1,0:T(8,128)(2,1)S(1)} %collective-permute-done.11.refs_2_), channel_id=1, source_target_pairs={{0,1},{1,0},{2,3},{3,2},{4,5},{5,4},{6,7},{7,6},{8,9},{9,8},{10,11... | collective-permute-start | bytes 786440 | tf_op jit(solution)/shard_map/ppermute | solution.py:523
  159.2 1.8 %collective-permute-start.18 = (bf16[256,512]{1,0:T(8,128)(2,1)S(1)}, bf16[256,512]{1,0:T(8,128)(2,1)S(1)}, u32[]{:S(2)}, u32[]{:S(2)}) collective-permute-start(bf16[256,512]{1,0:T(8,128)(2,1)S(1)} %collective-permute-done.12.refs_3_), channel_id=1, source_target_pairs={{0,1},{1,0},{2,3},{3,2},{4,5},{5,4},{6,7},{7,6},{8,9},{9,8},{10,11... | collective-permute-start | bytes 786440 | tf_op jit(solution)/shard_map/ppermute | solution.py:523
  (21 other events, 308.2 us)
